TPU v7x, 128 devices: a whole 4x4x4 slice. The times are simulated.
128 devices in a mesh: dp: 16 (over y, z_lo, core), row: 4 (over x), col: 2 (over z_hi).
Axes of the slice: x: 4, y: 4, z: 4 (z_hi: 2, z_lo: 2; z = z_hi * 2 + z_lo), core: 2. Of those that a mesh axis runs over, the one named last changes fastest.
Arguments:
- block_in: bfloat16 [8192, 2048], P('dp', ('row', 'col')), may hold values from -6 to 6
- segments: int32 [8192], P('dp'), may hold values from 0 to 31, never falling along the last dimension, each value on 1 to 1024 neighbouring positions
- ln1_gain: float32 [2048], P(('row', 'col')), may hold values from 0.5 to 1.5
- ln1_bias: float32 [2048], P(('row', 'col')), may hold values from -3 to 3
- qkv_weight: bfloat16 [2048, 6144], P('row', 'col'), may hold values from -0.125 to 0.125
- qkv_bias: float32 [6144], P(('col', 'row')), may hold values from -3 to 3
- out_weight: bfloat16 [2048, 2048], P('col', 'row'), may hold values from -0.5 to 0.5
- ln2_gain: float32 [2048], P(('row', 'col')), may hold values from 0.5 to 1.5
- ln2_bias: float32 [2048], P(('row', 'col')), may hold values from -3 to 3
- gate_up_weight: bfloat16 [2048, 2, 5632], P('row', None, 'col'), may hold values from -0.125 to 0.125
- down_weight: bfloat16 [5632, 2048], P('col', 'row'), may hold values from -0.078125 to 0.078125
- cotangent: bfloat16 [8192, 2048], P('dp', ('row', 'col')), may hold values from -6 to 6
Outputs:
- activations: bfloat16 [8192, 2048], P('dp', ('row', 'col'))
- input_grad: bfloat16 [8192, 2048], P('dp', ('row', 'col'))
- ln1_gain_grad: float32 [2048], P(('row', 'col'))
- ln1_bias_grad: float32 [2048], P(('row', 'col'))
- qkv_weight_grad: float32 [2048, 6144], P('row', 'col')
- qkv_bias_grad: float32 [6144], P(('col', 'row'))
- out_weight_grad: float32 [2048, 2048], P('col', 'row')
- ln2_gain_grad: float32 [2048], P(('row', 'col'))
- ln2_bias_grad: float32 [2048], P(('row', 'col'))
- gate_up_grad: float32 [2048, 2, 5632], P('row', None, 'col')
- down_grad: float32 [5632, 2048], P('col', 'row')
Inputs may be any that keep to these rules, and one draw needn't show every extreme that they name: `segments`: segment numbers never fall along the tokens; tokens attend only within their own sequence of 512 and their own segment.
All inputs are finite; a program needn't handle non-finite values.
Results may differ from a plain program's by a relative error of at most 0.04.
Values may be sent and summed in bfloat16 or wider, within the bound.
A program may use at most 128 MiB of HBM per device.

v0:
```python
import math

import jax
import jax.numpy as jnp
from jax import lax
from jax.sharding import PartitionSpec as P

D = 2048
HD = 64
ROT = 16


EPSILON = 1e-05
CONTRACT_ROWS = (((0,), (0,)), ((), ()))
CONTRACT_COLS = (((1,), (1,)), ((), ()))


def feature_sums(first_term, second_term):
    return lax.psum((jnp.sum(first_term, axis=1), jnp.sum(second_term, axis=1)), ("row", "col"))


def normalize(operand, norm_gain, norm_shift):
    sum_value, sum_square = feature_sums(operand, operand * operand)
    feature_mean = sum_value / D
    inverse = lax.rsqrt(sum_square / D - feature_mean * feature_mean + EPSILON)
    scaled = (operand - feature_mean[:, None]) * inverse[:, None]
    return (scaled, inverse, scaled * norm_gain + norm_shift)


def normalize_back(grad_out, scaled, inverse, norm_gain):
    grad_scaled = grad_out * norm_gain
    sum_grad, sum_along = feature_sums(grad_scaled, grad_scaled * scaled)
    return inverse[:, None] * (
        grad_scaled - sum_grad[:, None] / D - scaled * (sum_along[:, None] / D)
    )


def sum_rows(partial_value):
    return lax.psum_scatter(
        partial_value.astype(jnp.bfloat16), "row", scatter_dimension=2, tiled=True
    ).astype(jnp.float32)


def sum_cols(partial_value):
    return lax.psum_scatter(
        partial_value.astype(jnp.bfloat16), "col", scatter_dimension=1, tiled=True
    ).astype(jnp.float32)


def grad_cols(operand):
    return lax.all_gather(operand, "col", axis=1, tiled=True)


def grad_rows(operand):
    return lax.all_gather(operand, "row", axis=2, tiled=True)


def add_product(weight, shard_part):
    return jnp.dot(shard_part, weight, preferred_element_type=jnp.float32)


def add_outer(grad_full, shard_part):
    update = lax.dot_general(
        shard_part, grad_full, CONTRACT_ROWS, preferred_element_type=jnp.float32
    )
    return update


def forward_cols(activation, weight):
    return (add_product(weight, lax.all_gather(activation, "col", axis=1, tiled=True)), activation)


def forward_rows(activation, weight):
    return (add_product(weight, lax.all_gather(activation, "row", axis=1, tiled=True)), activation)


def weight_cols(kept_act, grad_full):
    return add_outer(grad_full, lax.all_gather(kept_act, "col", axis=1, tiled=True))


def weight_rows(kept_act, grad_full):
    return add_outer(grad_full, lax.all_gather(kept_act, "row", axis=1, tiled=True))


def times_transpose(grad_full, weight):
    return lax.dot_general(grad_full, weight, CONTRACT_COLS, preferred_element_type=jnp.float32)


def rotary_tables(segment):
    length = segment.shape[0]
    places = jnp.arange(length, dtype=jnp.int32)
    starts_flag = jnp.concatenate([jnp.array([True]), segment[1:] != segment[:-1]])
    starts = lax.cummax(jnp.where(starts_flag, places, 0), axis=0)
    offsets = (places - starts).astype(jnp.float32)
    half_width = ROT // 2
    frequencies = jnp.exp(
        jnp.arange(half_width, dtype=jnp.float32) * (-2.0 * math.log(10000.0) / ROT)
    )
    angles = offsets[:, None] * frequencies[None, :]
    return (jnp.cos(angles)[:, None, :], jnp.sin(angles)[:, None, :])


def rotate(operand, cosine, sine_table):
    half_width = ROT // 2
    first_half = operand[..., :half_width]
    second_half = operand[..., half_width:ROT]
    return jnp.concatenate(
        [
            first_half * cosine - second_half * sine_table,
            second_half * cosine + first_half * sine_table,
            operand[..., ROT:],
        ],
        axis=-1,
    )


def unrotate(operand, cosine, sine_table):
    half_width = ROT // 2
    first_half = operand[..., :half_width]
    second_half = operand[..., half_width:ROT]
    return jnp.concatenate(
        [
            first_half * cosine + second_half * sine_table,
            second_half * cosine - first_half * sine_table,
            operand[..., ROT:],
        ],
        axis=-1,
    )


def attention_scores(queries, key_heads, segment, score_scale):
    length = segment.shape[0]
    places = jnp.arange(length, dtype=jnp.int32)
    allowed = (places[None, :] <= places[:, None]) & (segment[None, :] == segment[:, None])
    scores = (
        jnp.einsum("qhd,khd->hqk", queries, key_heads, preferred_element_type=jnp.float32)
        * score_scale
    )
    return jnp.where(allowed[None], scores, -1e30)


def on_device(
    block_in,
    segments,
    ln1_gain,
    ln1_bias,
    qkv_weight,
    qkv_bias,
    out_weight,
    ln2_gain,
    ln2_bias,
    gate_up_weight,
    down_weight,
    cotangent,
):
    score_scale = 1.0 / math.sqrt(HD)
    tokens = block_in.shape[0]
    inputs = block_in.astype(jnp.float32)
    scaled_one, inverse_one, normed_value = normalize(inputs, ln1_gain, ln1_bias)
    normed = normed_value.astype(jnp.bfloat16)
    partial_value, kept_one = forward_cols(normed, qkv_weight)
    projected = sum_rows(partial_value.reshape(tokens, 1, -1)).reshape(tokens, -1) + qkv_bias
    head_view = projected.reshape(tokens, -1, 3, HD)
    cosine, sine_table = rotary_tables(segments)
    queries = rotate(head_view[:, :, 0], cosine, sine_table).astype(jnp.bfloat16)
    key_heads = rotate(head_view[:, :, 1], cosine, sine_table).astype(jnp.bfloat16)
    values = head_view[:, :, 2].astype(jnp.bfloat16)
    scores = attention_scores(queries, key_heads, segments, score_scale)
    row_maximum = jnp.max(scores, axis=-1, keepdims=True)
    raised = jnp.exp(scores - row_maximum)
    row_total = jnp.sum(raised, axis=-1, keepdims=True)
    probs_low = (raised / row_total).astype(jnp.bfloat16)
    attended = (
        jnp.einsum("hqk,khd->qhd", probs_low, values, preferred_element_type=jnp.float32)
        .astype(jnp.bfloat16)
        .reshape(tokens, -1)
    )
    partial_value, kept_two = forward_rows(attended, out_weight)
    hidden_in = inputs + sum_cols(partial_value)
    scaled_two, inverse_two, normed_value = normalize(hidden_in, ln2_gain, ln2_bias)
    normed_two = normed_value.astype(jnp.bfloat16)
    rows_two = gate_up_weight.shape[0]
    gate_up_flat = gate_up_weight.reshape(rows_two, -1)
    partial_value, kept_three = forward_cols(normed_two, gate_up_flat)
    gate_up = sum_rows(partial_value.reshape(tokens, 2, -1))
    gate_value = gate_up[:, 0]
    up_value = gate_up[:, 1]
    sigmoid_value = jax.nn.sigmoid(gate_value)
    activated = gate_value * sigmoid_value
    hidden = (activated * up_value).astype(jnp.bfloat16)
    partial_value, kept_four = forward_rows(hidden, down_weight)
    result = hidden_in + sum_cols(partial_value)
    activations = result.astype(jnp.bfloat16)
    upstream = cotangent.astype(jnp.float32)
    down_full = grad_cols(cotangent)
    grad_hidden = sum_rows(times_transpose(down_full, down_weight).reshape(tokens, 1, -1)).reshape(
        tokens, -1
    )
    down_grad = weight_rows(kept_four, down_full)
    grad_gate = (
        grad_hidden * up_value * (sigmoid_value * (1.0 + gate_value * (1.0 - sigmoid_value)))
    )
    grad_up = grad_hidden * activated
    grad_gate_up = jnp.stack([grad_gate, grad_up], axis=1).astype(jnp.bfloat16)
    gate_up_full = grad_rows(grad_gate_up).reshape(tokens, -1)
    grad_normed_two = sum_cols(times_transpose(gate_up_full, gate_up_flat))
    gate_up_grad = weight_cols(kept_three, gate_up_full).reshape(gate_up_weight.shape)
    ln2_gain_grad = jnp.sum(grad_normed_two * scaled_two, axis=0)
    ln2_bias_grad = jnp.sum(grad_normed_two, axis=0)
    grad_hidden_in = upstream + normalize_back(grad_normed_two, scaled_two, inverse_two, ln2_gain)
    grad_branch = grad_hidden_in.astype(jnp.bfloat16)
    out_full = grad_cols(grad_branch)
    grad_attended = (
        sum_rows(times_transpose(out_full, out_weight).reshape(tokens, 1, -1))
        .reshape(tokens, -1, HD)
        .astype(jnp.bfloat16)
    )
    out_weight_grad = weight_rows(kept_two, out_full)
    scores = attention_scores(queries, key_heads, segments, score_scale)
    probs = jnp.exp(scores - row_maximum) / row_total
    probs_low = probs.astype(jnp.bfloat16)
    grad_probs = jnp.einsum(
        "qhd,khd->hqk", grad_attended, values, preferred_element_type=jnp.float32
    )
    row_delta = jnp.sum(probs * grad_probs, axis=-1, keepdims=True)
    grad_scores = (probs * (grad_probs - row_delta)).astype(jnp.bfloat16)
    grad_values = jnp.einsum(
        "hqk,qhd->khd", probs_low, grad_attended, preferred_element_type=jnp.float32
    )
    grad_queries = (
        jnp.einsum("hqk,khd->qhd", grad_scores, key_heads, preferred_element_type=jnp.float32)
        * score_scale
    )
    grad_keys = (
        jnp.einsum("hqk,qhd->khd", grad_scores, queries, preferred_element_type=jnp.float32)
        * score_scale
    )
    grad_projected = (
        jnp.stack(
            [
                unrotate(grad_queries, cosine, sine_table),
                unrotate(grad_keys, cosine, sine_table),
                grad_values,
            ],
            axis=2,
        )
        .reshape(tokens, -1)
        .astype(jnp.bfloat16)
    )
    qkv_bias_grad = jnp.sum(grad_projected.astype(jnp.float32), axis=0)
    qkv_full = grad_rows(grad_projected.reshape(tokens, 1, -1)).reshape(tokens, -1)
    grad_normed = sum_cols(times_transpose(qkv_full, qkv_weight))
    qkv_weight_grad = weight_cols(kept_one, qkv_full)
    ln1_gain_grad = jnp.sum(grad_normed * scaled_one, axis=0)
    ln1_bias_grad = jnp.sum(grad_normed, axis=0)
    grad_input = grad_hidden_in + normalize_back(grad_normed, scaled_one, inverse_one, ln1_gain)
    input_grad = grad_input.astype(jnp.bfloat16)
    (
        ln1_gain_grad,
        ln1_bias_grad,
        qkv_weight_grad,
        qkv_bias_grad,
        out_weight_grad,
        ln2_gain_grad,
        ln2_bias_grad,
        gate_up_grad,
        down_grad,
    ) = (
        lax.psum(ln1_gain_grad.astype(jnp.bfloat16), "dp").astype(jnp.float32),
        lax.psum(ln1_bias_grad.astype(jnp.bfloat16), "dp").astype(jnp.float32),
        lax.psum(qkv_weight_grad.astype(jnp.bfloat16), "dp").astype(jnp.float32),
        lax.psum(qkv_bias_grad.astype(jnp.bfloat16), "dp").astype(jnp.float32),
        lax.psum(out_weight_grad.astype(jnp.bfloat16), "dp").astype(jnp.float32),
        lax.psum(ln2_gain_grad.astype(jnp.bfloat16), "dp").astype(jnp.float32),
        lax.psum(ln2_bias_grad.astype(jnp.bfloat16), "dp").astype(jnp.float32),
        lax.psum(gate_up_grad.astype(jnp.bfloat16), "dp").astype(jnp.float32),
        lax.psum(down_grad.astype(jnp.bfloat16), "dp").astype(jnp.float32),
    )
    return (
        activations,
        input_grad,
        ln1_gain_grad,
        ln1_bias_grad,
        qkv_weight_grad,
        qkv_bias_grad,
        out_weight_grad,
        ln2_gain_grad,
        ln2_bias_grad,
        gate_up_grad,
        down_grad,
    )


def solution(mesh):
    return jax.shard_map(
        on_device,
        mesh=mesh,
        in_specs=(
            P("dp", ("row", "col")),
            P("dp"),
            P(("row", "col")),
            P(("row", "col")),
            P("row", "col"),
            P(("col", "row")),
            P("col", "row"),
            P(("row", "col")),
            P(("row", "col")),
            P("row", None, "col"),
            P("col", "row"),
            P("dp", ("row", "col")),
        ),
        out_specs=(
            P("dp", ("row", "col")),
            P("dp", ("row", "col")),
            P(("row", "col")),
            P(("row", "col")),
            P("row", "col"),
            P(("col", "row")),
            P("col", "row"),
            P(("row", "col")),
            P(("row", "col")),
            P("row", None, "col"),
            P("col", "row"),
        ),
        check_vma=False,
    )
```

profile of v0, /device:TPU:1, one launch (start us, length us, event | category | flops | bytes accessed | tf_op | source)
XLA Modules:
  0.0 879.7 jit_solution(4742878506174997177)
XLA Ops:
  8.6 22.1 %all-reduce.3 = (f32[512]{0:T(512)S(1)}, f32[512]{0:T(512)S(1)}) all-reduce(f32[512]{0:T(512)S(1)} %get-tuple-element.53, f32[512]{0:T(512)S(1)} %get-tuple-element.52), channel_id=1, replica_groups=mesh['dp'=16,'row'=4,'col'=2] {'row','col'}, use_global_device_ids=true, to_apply=%region_3.0 | all-reduce | flops 1024 | bytes 8192 | tf_op jit(solution)/shard_map/psum | solution.py:19
  31.9 7.4 all_gather.28
  46.2 37.7 %reduce-scatter.9.cloned.1.call-done = bf16[512,1,768]{2,0,1:T(8,128)(2,1)} async-done(((bf16[512,1,3072]{2,0,1:T(8,128)(2,1)}), bf16[512,1,768]{2,0,1:T(8,128)(2,1)}) %reduce-scatter.9.cloned.1.call-update) | async-done | bytes 786448 | tf_op jit(solution)/shard_map/reduce_scatter | solution.py:39
  98.5 22.8 %all-gather.5.cloned.1.call-done = bf16[512,1024]{0,1:T(8,128)(2,1)} async-done(((bf16[512,256]{0,1:T(8,128)(2,1)}), bf16[512,1024]{0,1:T(8,128)(2,1)}) %all-gather.5.cloned.1.call-update) | async-done | bytes 1048592 | tf_op jit(solution)/shard_map/all_gather | solution.py:74
  124.4 6.1 copy.74
  130.5 8.4 copy.55
  145.7 18.3 %all-reduce.2 = (f32[512]{0:T(512)}, f32[512]{0:T(512)}) all-reduce(f32[512]{0:T(512)S(1)} %get-tuple-element.49, f32[512]{0:T(512)S(1)} %get-tuple-element.48), channel_id=1, replica_groups=mesh['dp'=16,'row'=4,'col'=2] {'row','col'}, use_global_device_ids=true, to_apply=%region_13.14 | all-reduce | flops 1024 | bytes 8192 | tf_op jit(solution)/shard_map/psum | solution.py:19
  165.9 7.4 all_gather.30
  174.1 7.6 convolution_convert_fusion
  181.8 7.6 all_gather.32
  195.6 48.2 %reduce-scatter.13.cloned.1.call-done = bf16[512,2,704]{0,2,1:T(8,128)(2,1)} async-done(((bf16[512,2,2816]{0,2,1:T(8,128)(2,1)}), bf16[512,2,704]{0,2,1:T(8,128)(2,1)}) %reduce-scatter.13.cloned.1.call-update) | async-done | bytes 1441808 | tf_op jit(solution)/shard_map/reduce_scatter | solution.py:39
  247.1 35.5 %reduce-scatter.17.cloned.1.call-done = bf16[512,1,704]{0,2,1:T(8,128)(2,1)} async-done(((bf16[512,1,2816]{0,2,1:T(8,128)(2,1)}), bf16[512,1,704]{0,2,1:T(8,128)(2,1)}) %reduce-scatter.17.cloned.1.call-update) | async-done | bytes 720912 | tf_op jit(solution)/shard_map/reduce_scatter | solution.py:39
  286.7 61.1 %all-gather.9.cloned.1.call-done = bf16[512,2,2816]{0,2,1:T(8,128)(2,1)} async-done(((bf16[512,2,704]{0,2,1:T(8,128)(2,1)}), bf16[512,2,2816]{0,2,1:T(8,128)(2,1)}) %all-gather.9.cloned.1.call-update) | async-done | bytes 5767184 | tf_op jit(solution)/shard_map/all_gather | solution.py:55
  347.8 8.3 fusion.28
  356.1 19.5 %reduce-scatter.19.cloned.1.call-done = bf16[512,256]{1,0:T(8,128)(2,1)} async-done(((bf16[512,512]{1,0:T(8,128)(2,1)}), bf16[512,256]{1,0:T(8,128)(2,1)}) %reduce-scatter.19.cloned.1.call-update) | async-done | bytes 262160 | tf_op jit(solution)/shard_map/reduce_scatter | solution.py:45
  377.7 18.4 %all-reduce.1 = (f32[512]{0:T(512)}, f32[512]{0:T(512)}) all-reduce(f32[512]{0:T(512)} %get-tuple-element.45, f32[512]{0:T(512)} %get-tuple-element.51), channel_id=1, replica_groups=mesh['dp'=16,'row'=4,'col'=2] {'row','col'}, use_global_device_ids=true, to_apply=%region_21.22 | all-reduce | flops 1024 | bytes 8192 | tf_op jit(solution)/shard_map/psum | solution.py:19
  398.8 7.4 all_gather.34
  410.0 24.4 %reduce-scatter.21.cloned.1.call-done = bf16[512,1,256]{2,0,1:T(8,128)(2,1)} async-done(((bf16[512,1,1024]{2,0,1:T(8,128)(2,1)}), bf16[512,1,256]{2,0,1:T(8,128)(2,1)}) %reduce-scatter.21.cloned.1.call-update) | async-done | bytes 262160 | tf_op jit(solution)/shard_map/reduce_scatter | solution.py:39
  448.9 37.3 %all-gather.11.cloned.1.call-done = bf16[512,1,3072]{0,2,1:T(8,128)(2,1)} async-done(((bf16[512,1,768]{0,2,1:T(8,128)(2,1)}), bf16[512,1,3072]{0,2,1:T(8,128)(2,1)}) %all-gather.11.cloned.1.call-update) | async-done | bytes 3145744 | tf_op jit(solution)/shard_map/all_gather | solution.py:55
  490.8 35.2 %all-gather.7.cloned.1.call-done = bf16[512,2816]{0,1:T(8,128)(2,1)} async-done(((bf16[512,704]{0,1:T(8,128)(2,1)}), bf16[512,2816]{0,1:T(8,128)(2,1)}) %all-gather.7.cloned.1.call-update) | async-done | bytes 2883600 | tf_op jit(solution)/shard_map/all_gather | solution.py:74
  536.5 8.0 fusion.5
  553.3 27.4 %all-reduce.4 = (bf16[256]{0:T(256)(128)(2,1)S(1)}, bf16[256]{0:T(256)(128)(2,1)S(1)}, bf16[768]{0:T(1024)(128)(2,1)S(1)}, bf16[256]{0:T(256)(128)(2,1)S(1)}, bf16[256]{0:T(256)(128)(2,1)S(1)}) all-reduce(bf16[256]{0:T(256)(128)(2,1)S(1)} %get-tuple-element.46, ...), channel_id=1, replica_groups=mesh['dp'=16,'row'=4,'col'=2] {'dp'}, use_global_device_ids=true, to_apply=%region_30.31 | all-reduce | flops 1792 | bytes 7168 | tf_op jit(solution)/shard_map/psum | solution.py:269
  583.6 21.0 %all-reduce = (f32[512]{0:T(512)S(1)}, f32[512]{0:T(512)S(1)}) all-reduce(f32[512]{0:T(512)S(1)} %get-tuple-element.47, f32[512]{0:T(512)S(1)} %get-tuple-element.50), channel_id=1, replica_groups=mesh['dp'=16,'row'=4,'col'=2] {'row','col'}, use_global_device_ids=true, to_apply=%region_28.29 | all-reduce | flops 1024 | bytes 8192 | tf_op jit(solution)/shard_map/psum | solution.py:19
  607.3 249.6 %all-reduce.8.cloned.1.call-done = (bf16[512,2,2816]{2,0,1:T(8,128)(2,1)}, bf16[512,3072]{1,0:T(8,128)(2,1)}, bf16[1024,512]{1,0:T(8,128)(2,1)}, bf16[2816,512]{1,0:T(8,128)(2,1)}) async-done(((bf16[512,2,2816]{2,0,1:T(8,128)(2,1)}, bf16[512,3072]{1,0:T(8,128)(2,1)}, bf16[1024,512]{1,0:T(8,128)(2,1)}, bf16[2816,512]{1,0:T(8,128)(2,1)}), (bf16[512,2,2816]{2,0,1:T(8,128)(2,1)}, bf16[512,3072]{1,0:T(8,128)(2,1)}, ...) | async-done | bytes 12845072 | tf_op jit(solution)/shard_map/psum | solution.py:276
  (170 shorter events, 118.6 us)
Async XLA Ops:
  7.2 32.9 %copy-start = (bf16[512,3072]{1,0:T(8,128)(2,1)S(1)}, bf16[512,3072]{1,0:T(8,128)(2,1)}, u32[]{:S(2)}) copy-start(bf16[512,3072]{1,0:T(8,128)(2,1)} %param.17) | copy-start | bytes 9437188
  7.2 76.7 %reduce-scatter.9.cloned.1.call-start = ((), (), s32[]{:S(2)}) async-start(), calls=%async_computation.8 | async-start | bytes 3932160 | tf_op jit(solution)/shard_map/reduce_scatter | solution.py:39
  43.6 77.7 %all-gather.5.cloned.1.call-start = ((), (), s32[]{:S(2)}) async-start(), calls=%async_computation.9 | async-start | bytes 1310720 | tf_op jit(solution)/shard_map/all_gather | solution.py:74
  98.4 46.1 %reduce-scatter.11.cloned.1.call-start = ((), (), s32[]{:S(2)}) async-start(), calls=%async_computation.10 | async-start | bytes 786432 | tf_op jit(solution)/shard_map/reduce_scatter | solution.py:45
  124.4 119.4 %reduce-scatter.13.cloned.1.call-start = ((), (), s32[]{:S(2)}) async-start(), calls=%async_computation.11 | async-start | bytes 7208960 | tf_op jit(solution)/shard_map/reduce_scatter | solution.py:39
  130.5 14.0 %copy-start.1 = (bf16[512,256]{1,0:T(8,128)(2,1)S(1)}, bf16[512,256]{1,0:T(8,128)(2,1)}, u32[]{:S(2)}) copy-start(bf16[512,256]{1,0:T(8,128)(2,1)} %param.13) | copy-start | bytes 786436
  181.7 100.8 %reduce-scatter.17.cloned.1.call-start = ((), (), s32[]{:S(2)}) async-start(), calls=%async_computation.14 | async-start | bytes 3604480 | tf_op jit(solution)/shard_map/reduce_scatter | solution.py:39
  195.3 152.4 %all-gather.9.cloned.1.call-start = ((), (), s32[]{:S(2)}) async-start(), calls=%async_computation.15 | async-start | bytes 7208960 | tf_op jit(solution)/shard_map/all_gather | solution.py:55
  286.6 89.0 %reduce-scatter.19.cloned.1.call-start = ((), (), s32[]{:S(2)}) async-start(), calls=%async_computation.16 | async-start | bytes 786432 | tf_op jit(solution)/shard_map/reduce_scatter | solution.py:45
  356.1 78.3 %reduce-scatter.21.cloned.1.call-start = ((), (), s32[]{:S(2)}) async-start(), calls=%async_computation.17 | async-start | bytes 1310720 | tf_op jit(solution)/shard_map/reduce_scatter | solution.py:39
  410.0 76.2 %all-gather.11.cloned.1.call-start = ((), (), s32[]{:S(2)}) async-start(), calls=%async_computation.18 | async-start | bytes 3932160 | tf_op jit(solution)/shard_map/all_gather | solution.py:55
  445.4 80.5 %all-gather.7.cloned.1.call-start = ((), (), s32[]{:S(2)}) async-start(), calls=%async_computation.12 | async-start | bytes 3604480 | tf_op jit(solution)/shard_map/all_gather | solution.py:74
  448.6 102.3 %reduce-scatter.23.cloned.1.call-start = ((), (), s32[]{:S(2)}) async-start(), calls=%async_computation.19 | async-start | bytes 786432 | tf_op jit(solution)/shard_map/reduce_scatter | solution.py:45
  490.8 113.9 %reduce-scatter.15.cloned.1.call-start = ((), (), s32[]{:S(2)}) async-start(), calls=%async_computation.13 | async-start | bytes 786432 | tf_op jit(solution)/shard_map/reduce_scatter | solution.py:45
  531.2 325.8 %all-reduce.8.cloned.1.call-start = ((), (), s32[]{:S(2)}) async-start(), calls=%async_computation.20 | async-start | bytes 25690112 | tf_op jit(solution)/shard_map/psum | solution.py:276
  536.4 8.0 copy-start.15
  536.4 8.0 copy-start.31
  536.5 9.7 %copy-start.10 = (bf16[512,512]{1,0:T(8,128)(2,1)S(1)}, bf16[512,512]{1,0:T(8,128)(2,1)}, u32[]{:S(2)}) copy-start(bf16[512,512]{1,0:T(8,128)(2,1)} %copy-done.9) | copy-start | bytes 1572868
  536.5 9.7 %copy-start.30 = (bf16[512,1,3072]{0,2,1:T(8,128)(2,1)S(1)}, bf16[512,1,3072]{0,2,1:T(8,128)(2,1)}, u32[]{:S(2)}) copy-start(bf16[512,1,3072]{0,2,1:T(8,128)(2,1)} %all-gather.11.cloned.1.call-done) | copy-start | bytes 9437188
  549.7 54.9 %copy-start.21 = (f32[512]{0:T(512)S(1)}, f32[512]{0:T(512)}, u32[]{:S(2)}) copy-start(f32[512]{0:T(512)} %copy-done.20) | copy-start | bytes 6148
  549.7 54.9 %copy-start.23 = (f32[512]{0:T(512)S(1)}, f32[512]{0:T(512)}, u32[]{:S(2)}) copy-start(f32[512]{0:T(512)} %copy-done.22) | copy-start | bytes 6148
  549.7 54.9 %copy-start.24 = (f32[256]{0:T(256)S(1)}, f32[256]{0:T(256)}, u32[]{:S(2)}) copy-start(f32[256]{0:T(256)} %param.20) | copy-start | bytes 3076
  857.0 7.2 slice-start
  857.0 7.2 slice-start.1
  (23 other events, 59.6 us)
Sparse Core Ops, SparseCore 0:
  43.8 40.1 reduce-scatter.8
  98.5 22.7 all-gather.4
  124.5 19.9 reduce-scatter.10
  181.9 61.8 reduce-scatter.12
  246.7 35.8 reduce-scatter.16
  286.8 60.9 all-gather.8
  356.2 19.3 reduce-scatter.18
  410.1 24.3 reduce-scatter.20
  445.6 40.5 all-gather.10
  488.4 37.5 all-gather.6
  528.4 18.8 reduce-scatter.22
  549.6 18.0 reduce-scatter.14
  571.9 285.0 all-reduce.7
where the time goes:
time: 881 us; the launch traced here: 880 us
  waiting for transfers between devices  577 us (65%)
  blocking collectives  137 us (16%)
  matrix products  73.1 us (8%)
  other arithmetic  44.4 us (5%)
  local copies, waits for them, and re-layouts  32.9 us (4%)
  between operations  14.3 us (2%)
    psum x1, waiting for transfers between devices, on_device(): lax.psum(gate_up_grad.astype(jnp.bfloat16), 'dp').astype(jnp.float32)  250 us
    reduce_scatter x4, waiting for transfers between devices, sum_rows(): lax.psum_scatter(partial_value.astype(jnp.bfloat16), 'row', scatter_dimen...  146 us
    all_gather x2, waiting for transfers between devices, grad_rows(): return lax.all_gather(operand, 'row', axis=2, tiled=True)  98.4 us
    psum x4, blocking collectives, feature_sums(): lax.psum((jnp.sum(first_term, axis=1), jnp.sum(second_term, axis=1)), ('r...  79.8 us
    all_gather x2, waiting for transfers between devices, forward_rows(): lax.all_gather(activation, 'row', axis=1, tiled=True)  58 us
    psum x1, blocking collectives, on_device(): lax.psum(ln1_gain_grad.astype(jnp.bfloat16), 'dp').astype(jnp.float32)  27.4 us
    reduce_scatter x4, waiting for transfers between devices, sum_cols(): lax.psum_scatter(partial_value.astype(jnp.bfloat16), 'col', scatter_dimen...  25 us
    dot_general x4, matrix products, times_transpose(): lax.dot_general(grad_full, weight, CONTRACT_COLS, preferred_element_type=...  20.9 us
  transfers between devices with their start and end apart: 13, of which 11 were waited for; matrix products, arithmetic and copies ran while one was open for 7% of the time, Pallas kernels for 0%

commit v1 on v0

v1 whole, which is shorter than its diff:
```python
import math

import jax
import jax.numpy as jnp
from jax import lax
from jax.experimental import pallas as pl
from jax.experimental.pallas import tpu as pltpu
from jax.sharding import PartitionSpec as P

D = 2048
HD = 64
ROT = 16
HEADS = 4
TOK = 512
OWN = 64
WIDE = 768
EPSILON = 1e-05
BF = jnp.bfloat16
F32 = jnp.float32
MESH = pl.DeviceIdType.MESH
VMEM_LIMIT = 60 * 2**20
ROWS_BY_COLS = (((1,), (1,)), ((), ()))
OVER_ROWS = (((0,), (0,)), ((), ()))

IN_VMEM = pl.BlockSpec(memory_space=pltpu.VMEM)
IN_ANY = pl.BlockSpec(memory_space=pl.ANY)


class Place:
    def __init__(self):
        self.dp = lax.axis_index("dp")
        self.x = lax.axis_index("row")
        self.zh = lax.axis_index("col")
        self.y = self.dp // 4
        self.zl = (self.dp // 2) % 2
        self.core = self.dp % 2
        self.q = self.dp // 2
        self.g = self.x * 2 + self.zh

    def group(self, g):
        return (self.dp, g // 2, g % 2)

    def row(self, x):
        return (self.dp, x, self.zh)

    def chip(self, q):
        return (q * 2 + self.core, self.x, self.zh)

    def sibling(self):
        return (self.q * 2 + 1 - self.core, self.x, self.zh)

    def replica(self, dp):
        return (dp, self.x, self.zh)


def greet(partners):
    barrier = pltpu.get_barrier_semaphore()
    for partner in partners:
        pl.semaphore_signal(barrier, inc=1, device_id=partner, device_id_type=MESH)
    pl.semaphore_wait(barrier, len(partners))


def push(src, dst, sems, index, device):
    send, recv = sems
    copy = pltpu.make_async_remote_copy(
        src_ref=src,
        dst_ref=dst,
        send_sem=send.at[index],
        recv_sem=recv.at[index],
        device_id=device,
        device_id_type=MESH,
    )
    copy.start()
    return copy


def group_others(at):
    return [at.group((at.g + k) % 8) for k in range(1, 8)]


def chip_others(at):
    return [at.chip(at.q ^ k) for k in range(1, 8)]


def dma_sems(amount):
    return [pltpu.SemaphoreType.DMA((amount,)), pltpu.SemaphoreType.DMA((amount,))]


def params(collective_id):
    return pltpu.CompilerParams(
        collective_id=collective_id, has_side_effects=True, vmem_limit_bytes=VMEM_LIMIT
    )


def tile_start(x):
    return 5 * x + jnp.minimum(x, 1)


def gather_kernel(
    x_in, cot_in, par_in, qkv_w, out_w, gu_w, down_w,
    x_out, cot_out, par_out, qkv_s, out_s, gu_s, down_s,
    act_send, act_recv, a_send, a_recv, b_send, b_recv, c_send, c_recv, local,
):
    at = Place()
    greet(group_others(at) + chip_others(at) + [at.sibling()])
    act, step_a, step_b, step_c = (
        (act_send, act_recv), (a_send, a_recv), (b_send, b_recv), (c_send, c_recv)
    )
    dp, x, core, q = at.dp, at.x, at.core, at.q

    def source(k, xt):
        if k == 0:
            return qkv_w.at[pl.ds(dp * 32, 32), pl.ds(xt * WIDE, WIDE)]
        if k == 1:
            return out_w.at[pl.ds(xt * 256 + dp * 16, 16), :]
        if k == 2:
            return gu_w.at[:, pl.ds(dp * 32, 32), pl.ds(tile_start(xt) * 128, WIDE)]
        return down_w.at[pl.ds(tile_start(xt) * 128 + dp * 48, 48), :]

    def landing(k, xs):
        if k == 0:
            return qkv_s.at[xs, dp]
        if k == 1:
            return out_s.at[dp, :, pl.ds(xs * 512, 512)]
        if k == 2:
            return gu_s.at[:, xs, dp]
        return down_s.at[dp, :, pl.ds(xs * 512, 512)]

    def piece(k, p):
        if k == 0:
            return qkv_s.at[:, p]
        if k == 1:
            return out_s.at[p]
        if k == 2:
            return gu_s.at[:, :, p]
        return down_s.at[p]

    waits = []
    for k in range(4):
        for j in range(1, 4):
            xt = (x + j) % 4
            waits.append(push(source(k, xt), landing(k, x), step_a, k * 3 + j - 1, at.row(xt)))
    own = []
    for k in range(4):
        own.append(pltpu.make_async_copy(source(k, x), landing(k, x), local.at[k]))
    slot = pl.ds(at.g * 256, 256)
    own.append(pltpu.make_async_copy(x_in, x_out.at[:, slot], local.at[4]))
    own.append(pltpu.make_async_copy(cot_in, cot_out.at[:, slot], local.at[5]))
    own.append(pltpu.make_async_copy(par_in, par_out.at[:, slot], local.at[6]))
    for copy in own:
        copy.start()
    for j, device in enumerate(group_others(at)):
        waits.append(push(par_in, par_out.at[:, slot], act, 14 + j, device))
    for j, device in enumerate(group_others(at)):
        waits.append(push(x_in, x_out.at[:, slot], act, j, device))
    for j, device in enumerate(group_others(at)):
        waits.append(push(cot_in, cot_out.at[:, slot], act, 7 + j, device))
    for copy in own:
        copy.wait()
    second = []
    for k in range(4):
        for j in range(3):
            waits[k * 3 + j].wait_recv()
        for m, device in enumerate(chip_others(at)):
            second.append(push(piece(k, dp), piece(k, dp), step_b, k * 7 + m, device))
        third = push(piece(k, dp), piece(k, dp), step_c, k * 8, at.sibling())
        waits.append(third)
    for k in range(4):
        for m in range(1, 8):
            second[k * 7 + m - 1].wait_recv()
            p = (q ^ m) * 2 + core
            waits.append(push(piece(k, p), piece(k, p), step_c, k * 8 + m, at.sibling()))
    for index, copy in enumerate(waits):
        copy.wait_send()
        if index >= 12:
            copy.wait_recv()
    for copy in second:
        copy.wait_send()


def gather_inputs(x_in, cot_in, par_in, qkv_w, out_w, gu_w, down_w):
    shape = jax.ShapeDtypeStruct
    outs = pl.pallas_call(
        gather_kernel,
        out_shape=(
            shape((TOK, D), BF),
            shape((TOK, D), BF),
            shape((8, D), F32),
            shape((4, 16, 32, WIDE), BF),
            shape((16, 16, D), BF),
            shape((2, 4, 16, 32, WIDE), BF),
            shape((16, 48, D), BF),
        ),
        in_specs=[IN_ANY] * 7,
        out_specs=(IN_ANY,) * 7,
        scratch_shapes=dma_sems(21)
        + dma_sems(12)
        + dma_sems(28)
        + dma_sems(32)
        + [pltpu.SemaphoreType.DMA((7,))],
        compiler_params=params(1),
        name="gather_inputs",
    )(x_in, cot_in, par_in, qkv_w, out_w, gu_w, down_w)
    x_full, cot_full, par_full, qkv_s, out_s, gu_s, down_s = outs
    return (
        x_full,
        cot_full,
        par_full,
        qkv_s.reshape(D, WIDE),
        out_s.reshape(256, D),
        gu_s.reshape(2, D, WIDE),
        down_s.reshape(WIDE, D),
    )


def settle(src, sems, index, device):
    send, recv = sems
    return pltpu.make_async_remote_copy(
        src_ref=src,
        dst_ref=src,
        send_sem=send.at[index],
        recv_sem=recv.at[index],
        device_id=device,
        device_id_type=MESH,
    )


def scatter_sum(at, product, part, got, sems):
    def step(i, carry):
        xt = (at.x + i + 1) % 4
        part[pl.ds(pl.multiple_of(xt * 128, 128), 128), :] = product(xt).astype(BF)
        for half in range(2):
            g = xt * 2 + half
            index = (g - at.g + 15) % 8

            @pl.when(index < 7)
            def _():
                push(
                    part.at[pl.ds(pl.multiple_of(g * OWN, OWN), OWN)],
                    got.at[index],
                    sems,
                    index,
                    at.group(g),
                )

        return carry

    lax.fori_loop(0, 4, step, 0)


def own_rows(at):
    return pl.ds(pl.multiple_of(at.g * OWN, OWN), OWN)


def summed(at, part, got, sems):
    total = part[own_rows(at), :].astype(F32)
    for k in range(7):
        settle(got.at[k], sems, k, at.group(at.g)).wait_recv()
        total += got[k].astype(F32)
    return total


def sent(at, buffer, sems, amount=7):
    for k in range(amount):
        settle(buffer, sems, k, at.group(at.g)).wait_send()


def gather_rows(at, rows, full, sems, local):
    copy = pltpu.make_async_copy(rows, full.at[own_rows(at)], local)
    copy.start()
    for k in range(1, 8):
        push(rows, full.at[own_rows(at)], sems, k - 1, at.group((at.g + k) % 8))
    copy.wait()


def gather_columns(at, rows, full, sems, local):
    def columns(g):
        return rows.at[:, pl.ds(pl.multiple_of(g * 256, 256), 256)]

    copy = pltpu.make_async_copy(columns(at.g), full.at[own_rows(at)], local)
    copy.start()
    for k in range(1, 8):
        g = (at.g + k) % 8
        push(columns(g), full.at[own_rows(at)], sems, k - 1, at.group(g))
    copy.wait()


def settle_all(at, piece, sems, amount=7):
    for k in range(amount):
        copy = settle(piece, sems, k, at.group(at.g))
        copy.wait_send()
        copy.wait_recv()


def norm(value):
    mean = jnp.mean(value, axis=1, keepdims=True)
    square = jnp.mean(value * value, axis=1, keepdims=True)
    inverse = lax.rsqrt(square - mean * mean + EPSILON)
    return (value - mean) * inverse, inverse


def norm_back(grad, scaled, inverse, gain):
    inner = grad * gain
    mean = jnp.mean(inner, axis=1, keepdims=True)
    along = jnp.mean(inner * scaled, axis=1, keepdims=True)
    return inverse * (inner - mean - scaled * along)


def attend_out_kernel(
    attended, weight, x_full, par, hidden_out, normed_out,
    part, got, rows, rs_send, rs_recv, ag_send, ag_recv, local,
):
    at = Place()
    greet(group_others(at))
    rs, ag = (rs_send, rs_recv), (ag_send, ag_recv)

    def product(xt):
        block = attended[pl.ds(pl.multiple_of(xt * 128, 128), 128), :]
        return jnp.dot(block, weight[...], preferred_element_type=F32)

    scatter_sum(at, product, part, got, rs)
    hidden_in = summed(at, part, got, rs) + x_full[own_rows(at), :].astype(F32)
    hidden_out[...] = hidden_in
    scaled, _ = norm(hidden_in)
    rows[...] = (scaled * par[2:3, :] + par[3:4, :]).astype(BF)
    gather_rows(at, rows, normed_out, ag, local.at[0])
    sent(at, got.at[0], rs)
    settle_all(at, rows, ag)


def attend_out(attended, weight, x_full, par):
    return pl.pallas_call(
        attend_out_kernel,
        out_shape=(jax.ShapeDtypeStruct((OWN, D), F32), jax.ShapeDtypeStruct((TOK, D), BF)),
        in_specs=[IN_VMEM] * 4,
        out_specs=(IN_VMEM, IN_ANY),
        scratch_shapes=[
            pltpu.VMEM((TOK, D), BF),
            pltpu.VMEM((7, OWN, D), BF),
            pltpu.VMEM((OWN, D), BF),
        ]
        + dma_sems(7)
        + dma_sems(7)
        + [pltpu.SemaphoreType.DMA((1,))],
        compiler_params=params(2),
        name="attend_out",
    )(attended, weight, x_full, par)


def mlp_back_kernel(
    grad_gate, grad_up, gu_s, hidden, down_s, hidden_in, cot_full, par,
    grad_in_out, branch_out, act_out, sums_out,
    part, got, rows, part2, got2, rows2,
    rs_send, rs_recv, ag_send, ag_recv, rt_send, rt_recv, tr_send, tr_recv, local,
):
    at = Place()
    greet(group_others(at))
    rs, ag = (rs_send, rs_recv), (ag_send, ag_recv)
    rt, tr = (rt_send, rt_recv), (tr_send, tr_recv)

    def product(xt):
        block = pl.ds(pl.multiple_of(xt * 128, 128), 128)
        first = lax.dot_general(
            grad_gate[block, :], gu_s[0], ROWS_BY_COLS, preferred_element_type=F32
        )
        return first + lax.dot_general(
            grad_up[block, :], gu_s[1], ROWS_BY_COLS, preferred_element_type=F32
        )

    def product_two(xt):
        block = pl.ds(pl.multiple_of(xt * 128, 128), 128)
        return jnp.dot(hidden[block, :], down_s[...], preferred_element_type=F32)

    scatter_sum(at, product, part, got, rs)
    scaled, inverse = norm(hidden_in[...])
    grad = summed(at, part, got, rs)
    grad_in = cot_full[own_rows(at), :].astype(F32) + norm_back(
        grad, scaled, inverse, par[2:3, :]
    )
    grad_in_out[...] = grad_in
    rows[...] = grad_in.astype(BF)
    gather_rows(at, rows, branch_out, ag, local.at[0])
    sums_out[...] = jnp.zeros_like(sums_out)
    sums_out[0:1, :] = jnp.sum(grad * scaled, axis=0, keepdims=True)
    sums_out[1:2, :] = jnp.sum(grad, axis=0, keepdims=True)
    scatter_sum(at, product_two, part2, got2, rt)
    total = summed(at, part2, got2, rt) + hidden_in[...]
    rows2[...] = total.astype(BF)
    gather_columns(at, rows2, act_out, tr, local.at[1])
    sent(at, got.at[0], rs)
    sent(at, got.at[0], rt)
    settle_all(at, rows, ag)
    settle_all(at, rows2.at[:, pl.ds(0, 256)], tr)


def mlp_back(grad_gate, grad_up, gu_s, hidden, down_s, hidden_in, cot_full, par):
    shape = jax.ShapeDtypeStruct
    return pl.pallas_call(
        mlp_back_kernel,
        out_shape=(
            shape((OWN, D), F32),
            shape((TOK, D), BF),
            shape((TOK, 256), BF),
            shape((8, D), F32),
        ),
        in_specs=[IN_VMEM] * 8,
        out_specs=(IN_VMEM, IN_ANY, IN_ANY, IN_VMEM),
        scratch_shapes=[
            pltpu.VMEM((TOK, D), BF),
            pltpu.VMEM((7, OWN, D), BF),
            pltpu.VMEM((OWN, D), BF),
        ]
        * 2
        + dma_sems(7) * 4
        + [pltpu.SemaphoreType.DMA((2,))],
        compiler_params=params(3),
        name="mlp_back",
    )(grad_gate, grad_up, gu_s, hidden, down_s, hidden_in, cot_full, par)


def input_back_kernel(
    grad_proj, qkv_s, x_full, grad_in, par, out, sums_out,
    part, got, rows, rs_send, rs_recv, tr_send, tr_recv, local,
):
    at = Place()
    greet(group_others(at))
    rs, tr = (rs_send, rs_recv), (tr_send, tr_recv)

    def product(xt):
        block = pl.ds(pl.multiple_of(xt * 128, 128), 128)
        return lax.dot_general(
            grad_proj[block, :], qkv_s[...], ROWS_BY_COLS, preferred_element_type=F32
        )

    scatter_sum(at, product, part, got, rs)
    scaled, inverse = norm(x_full[own_rows(at), :].astype(F32))
    grad = summed(at, part, got, rs)
    total = grad_in[...] + norm_back(grad, scaled, inverse, par[0:1, :])
    rows[...] = total.astype(BF)
    gather_columns(at, rows, out, tr, local.at[0])
    sums_out[...] = jnp.zeros_like(sums_out)
    sums_out[0:1, :] = jnp.sum(grad * scaled, axis=0, keepdims=True)
    sums_out[1:2, :] = jnp.sum(grad, axis=0, keepdims=True)
    sent(at, got.at[0], rs)
    settle_all(at, rows.at[:, pl.ds(0, 256)], tr)


def input_back(grad_proj, qkv_s, x_full, grad_in, par):
    shape = jax.ShapeDtypeStruct
    return pl.pallas_call(
        input_back_kernel,
        out_shape=(shape((TOK, 256), BF), shape((8, D), F32)),
        in_specs=[IN_VMEM] * 5,
        out_specs=(IN_ANY, IN_VMEM),
        scratch_shapes=[
            pltpu.VMEM((TOK, D), BF),
            pltpu.VMEM((7, OWN, D), BF),
            pltpu.VMEM((OWN, D), BF),
        ]
        + dma_sems(7) * 2
        + [pltpu.SemaphoreType.DMA((1,))],
        compiler_params=params(4),
        name="input_back",
    )(grad_proj, qkv_s, x_full, grad_in, par)


def rotary(value, tables, sign):
    width = value.shape[1]
    return (
        value * tables[0]
        + pltpu.roll(value, width - 8, 1) * (sign * tables[1])
        + pltpu.roll(value, 8, 1) * (sign * tables[2])
    )


def head_part(value, head, kind):
    start = head * 3 * HD + kind * HD
    return value[:, start : start + HD]


def allowed(seg_col, seg_row, block, keys):
    start = block * 128
    rows = lax.broadcasted_iota(jnp.int32, (128, keys), 0) + start
    cols = lax.broadcasted_iota(jnp.int32, (128, keys), 1)
    same = seg_col[start : start + 128, :] == seg_row[0:1, :keys]
    return (cols <= rows) & same


def attention_kernel(proj, tables, seg_col, seg_row, qkv_out, att_out, max_out, sum_out):
    scale = 1.0 / math.sqrt(HD)
    for half in range(2):
        cols = pl.ds(half * 384, 384)
        tab = (tables[0], tables[1], tables[2])
        qkv_out[:, cols] = rotary(proj[:, cols], tab, 1.0).astype(BF)
    for block in range(4):
        keys = (block + 1) * 128
        rows = pl.ds(block * 128, 128)
        mask = allowed(seg_col, seg_row, block, keys)
        outs, maxima, totals = [], [], []
        for head in range(HEADS):
            q = head_part(qkv_out[rows, :], head, 0)
            k = head_part(qkv_out[pl.ds(0, keys), :], head, 1)
            v = head_part(qkv_out[pl.ds(0, keys), :], head, 2)
            score = lax.dot_general(q, k, ROWS_BY_COLS, preferred_element_type=F32) * scale
            score = jnp.where(mask, score, -1e30)
            top = jnp.max(score, axis=1, keepdims=True)
            raised = jnp.exp(score - top)
            total = jnp.sum(raised, axis=1, keepdims=True)
            low = (raised / total).astype(BF)
            outs.append(jnp.dot(low, v, preferred_element_type=F32))
            maxima.append(top)
            totals.append(total)
        att_out[rows, :] = jnp.concatenate(outs, axis=1).astype(BF)
        for head in range(HEADS):
            max_out[rows, head : head + 1] = maxima[head]
            sum_out[rows, head : head + 1] = totals[head]


def attention(proj, tables, seg_col, seg_row):
    shape = jax.ShapeDtypeStruct
    return pl.pallas_call(
        attention_kernel,
        out_shape=(
            shape((TOK, WIDE), BF),
            shape((TOK, 256), BF),
            shape((TOK, 128), F32),
            shape((TOK, 128), F32),
        ),
        in_specs=[IN_VMEM] * 4,
        out_specs=(IN_VMEM,) * 4,
        compiler_params=pltpu.CompilerParams(vmem_limit_bytes=VMEM_LIMIT),
        name="attention",
    )(proj, tables, seg_col, seg_row)


def attention_back_kernel(
    qkv, grad_att, tables, seg_col, seg_row, maxima, totals, grad_out, bias_out, pieces
):
    scale = 1.0 / math.sqrt(HD)
    pieces[...] = jnp.zeros_like(pieces)
    for block in range(4):
        keys = (block + 1) * 128
        rows = pl.ds(block * 128, 128)
        upto = pl.ds(0, keys)
        mask = allowed(seg_col, seg_row, block, keys)
        for head in range(HEADS):
            q = head_part(qkv[rows, :], head, 0)
            k = head_part(qkv[upto, :], head, 1)
            v = head_part(qkv[upto, :], head, 2)
            grad = grad_att[rows, :][:, head * HD : (head + 1) * HD]
            score = lax.dot_general(q, k, ROWS_BY_COLS, preferred_element_type=F32) * scale
            score = jnp.where(mask, score, -1e30)
            probs = jnp.exp(score - maxima[rows, head : head + 1]) / totals[rows, head : head + 1]
            grad_probs = lax.dot_general(grad, v, ROWS_BY_COLS, preferred_element_type=F32)
            delta = jnp.sum(probs * grad_probs, axis=1, keepdims=True)
            grad_score = (probs * (grad_probs - delta)).astype(BF)
            pieces[head, 0, rows, :] = (
                jnp.dot(grad_score, k, preferred_element_type=F32) * scale
            )
            pieces[head, 1, upto, :] += (
                lax.dot_general(grad_score, q, OVER_ROWS, preferred_element_type=F32) * scale
            )
            pieces[head, 2, upto, :] += lax.dot_general(
                probs.astype(BF), grad, OVER_ROWS, preferred_element_type=F32
            )
    tab = (tables[0], tables[1], tables[2])
    bias_out[...] = jnp.zeros_like(bias_out)
    for half in range(2):
        parts = [pieces[half * 2 + j // 3, j % 3] for j in range(6)]
        cols = pl.ds(half * 384, 384)
        low = rotary(jnp.concatenate(parts, axis=1), tab, -1.0).astype(BF)
        grad_out[:, cols] = low
        bias_out[0:1, cols] = jnp.sum(low.astype(F32), axis=0, keepdims=True)


def attention_back(qkv, grad_att, tables, seg_col, seg_row, maxima, totals):
    shape = jax.ShapeDtypeStruct
    return pl.pallas_call(
        attention_back_kernel,
        out_shape=(shape((TOK, WIDE), BF), shape((8, WIDE), F32)),
        in_specs=[IN_VMEM] * 7,
        out_specs=(IN_VMEM,) * 2,
        scratch_shapes=[pltpu.VMEM((HEADS, 3, TOK, HD), F32)],
        compiler_params=pltpu.CompilerParams(vmem_limit_bytes=VMEM_LIMIT),
        name="attention_back",
    )(qkv, grad_att, tables, seg_col, seg_row, maxima, totals)


def rotary_tables(segment):
    places = jnp.arange(TOK, dtype=jnp.int32)
    starts_flag = jnp.concatenate([jnp.array([True]), segment[1:] != segment[:-1]])
    starts = lax.cummax(jnp.where(starts_flag, places, 0), axis=0)
    offsets = (places - starts).astype(F32)
    half = ROT // 2
    frequencies = jnp.exp(jnp.arange(half, dtype=F32) * (-2.0 * math.log(10000.0) / ROT))
    angles = offsets[:, None] * frequencies[None, :]
    cosine, sine = jnp.cos(angles), jnp.sin(angles)
    one, zero = jnp.ones((TOK, HD), F32), jnp.zeros((TOK, HD), F32)
    rest = HD - ROT
    keep = jnp.concatenate([cosine, cosine, one[:, :rest]], axis=1)
    fore = jnp.concatenate([-sine, zero[:, : HD - half]], axis=1)
    back = jnp.concatenate([zero[:, :half], sine, zero[:, :rest]], axis=1)
    wide = [jnp.concatenate([t, t, e], axis=1) for t, e in ((keep, one), (fore, zero), (back, zero))]
    return jnp.stack([jnp.concatenate([t, t], axis=1) for t in wide])


def sum_grads_kernel(
    gu_p, qkv_p, down_p, out_p, ln_p, bias_p,
    gu_f, qkv_f, down_f, out_f, small_f,
    gu_a, gu_r, gu_t, gu_c, qkv_a, qkv_r, qkv_t, qkv_c,
    down_a, down_r, down_t, down_c, out_a, out_r, out_t, out_c,
    ln_t, small_t,
    a_send, a_recv, b_send, b_recv, c_send, c_recv, d_send, d_recv, e_send, e_recv,
    g_send, g_recv, h_send, h_recv, local,
):
    at = Place()
    others = [at.replica((at.dp + k) % 16) for k in range(1, 16)]
    greet(group_others(at) + others)
    step_a, step_b, step_c = (a_send, a_recv), (b_send, b_recv), (c_send, c_recv)
    step_d, step_e = (d_send, d_recv), (e_send, e_recv)
    step_g, step_h = (g_send, g_recv), (h_send, h_recv)
    core, q, x = at.core, at.q, at.x
    cq = core * 8 + q

    partial = (gu_p, qkv_p, down_p, out_p)
    accs = (gu_a, qkv_a, down_a, out_a)
    recvs = (gu_r, qkv_r, down_r, out_r)
    slots = (gu_t, qkv_t, down_t, out_t)
    packs = (gu_c, qkv_c, down_c, out_c)
    order = (0, 2, 3, 1)

    def half(k, c):
        if k == 0:
            return gu_p.at[:, :, c]
        if k == 1:
            return qkv_p.at[:, c]
        return partial[k].at[c]

    def chunk(k, p):
        if k == 0:
            return gu_a.at[:, :, p]
        if k == 1:
            return qkv_a.at[:, p]
        return accs[k].at[p]

    def blocks(k):
        if k == 0:
            return [(a, b) for a in range(2) for b in range(4)]
        if k == 1:
            return [(b,) for b in range(4)]
        return [()]

    def full(lead, p):
        return lead + (p,)

    def pack_for(k, xt):
        if k == 0:
            return gu_c.at[:, xt]
        if k == 1:
            return qkv_c.at[xt]
        return packs[k].at[:, pl.ds(pl.multiple_of(xt * 512, 512), 512)]

    def landing(k, xs, p):
        if k == 0:
            return gu_f.at[xs, :, p]
        if k == 1:
            return qkv_f.at[p, :, pl.ds(pl.multiple_of(xs * WIDE, WIDE), WIDE)]
        return (gu_f, qkv_f, down_f, out_f)[k].at[xs, p]

    def piece(k, p):
        if k == 0:
            return gu_f.at[:, :, p]
        if k == 1:
            return qkv_f.at[p]
        return (gu_f, qkv_f, down_f, out_f)[k].at[:, p]

    mine = pl.ds(pl.multiple_of(at.g * 256, 256), 256)
    for j in range(1, 8):
        g = (at.g + j) % 8
        push(
            ln_p.at[:, pl.ds(pl.multiple_of(g * 256, 256), 256)],
            ln_t.at[j - 1],
            step_g,
            j - 1,
            at.group(g),
        )
    first = {}
    for k in order:
        first[k] = push(half(k, 1 - core), recvs[k], step_a, k, at.sibling())
        copy = pltpu.make_async_copy(half(k, core), accs[k], local.at[k])
        copy.start()
        first[k + 4] = copy
    total = ln_p[:, mine] + bias_p[...]
    for j in range(7):
        settle(ln_t.at[j], step_g, j, at.group(at.g)).wait_recv()
        total += ln_t[j]
    small_t[pl.ds(at.dp, 1)] = total[None]
    for j, device in enumerate(others):
        push(small_t.at[at.dp], small_t.at[at.dp], step_h, j, device)
    second = {}
    for k in order:
        first[k].wait_recv()
        first[k + 4].wait()
        for lead in blocks(k):

            def add(p, carry):
                index = full(lead, p)
                accs[k][index] = (accs[k][index].astype(F32) + recvs[k][index].astype(F32)).astype(
                    BF
                )
                return carry

            lax.fori_loop(0, 8, add, 0)
        for m, device in enumerate(chip_others(at)):
            second[k, m] = push(chunk(k, q ^ (m + 1)), slots[k].at[m], step_b, k * 7 + m, device)
    third = {}
    for k in order:
        for m in range(7):
            second[k, m].wait_recv()
        for lead in blocks(k):
            value = accs[k][full(lead, q)].astype(F32)
            for m in range(7):
                value += slots[k][(m,) + lead].astype(F32)
            packs[k][lead + (Ellipsis,)] = value.astype(BF)
        for j in range(1, 4):
            xt = (x + j) % 4
            third[k, j] = push(
                pack_for(k, xt), landing(k, x, cq), step_c, k * 3 + j - 1, at.row(xt)
            )
        copy = pltpu.make_async_copy(pack_for(k, x), landing(k, x, cq), local.at[4 + k])
        copy.start()
        third[k, 0] = copy
    fourth, fifth = {}, {}
    for k in order:
        third[k, 0].wait()
        for j in range(1, 4):
            third[k, j].wait_recv()
        for m, device in enumerate(chip_others(at)):
            fourth[k, m] = push(piece(k, cq), piece(k, cq), step_d, k * 7 + m, device)
        fifth[k, 7] = push(piece(k, cq), piece(k, cq), step_e, k * 8 + 7, at.sibling())
    for k in order:
        for m in range(7):
            fourth[k, m].wait_recv()
            p = core * 8 + (q ^ (m + 1))
            fifth[k, m] = push(piece(k, p), piece(k, p), step_e, k * 8 + m, at.sibling())
    for j in range(15):
        settle(small_t.at[0], step_h, j, at.group(at.g)).wait_recv()
    result = small_t[0]
    for j in range(1, 16):
        result += small_t[j]
    small_f[...] = result
    for k in order:
        first[k].wait_send()
        for m in range(7):
            second[k, m].wait_send()
            fourth[k, m].wait_send()
        for j in range(1, 4):
            third[k, j].wait_send()
        for m in range(8):
            fifth[k, m].wait_send()
            fifth[k, m].wait_recv()
    for j in range(7):
        settle(ln_t.at[j], step_g, j, at.group(at.g)).wait_send()
    for j in range(15):
        settle(small_t.at[0], step_h, j, at.group(at.g)).wait_send()


def sum_grads(gu_p, qkv_p, down_p, out_p, ln_p, bias_p):
    shape = jax.ShapeDtypeStruct
    vmem = pltpu.VMEM
    return pl.pallas_call(
        sum_grads_kernel,
        out_shape=(
            shape((4, 2, 16, 32, WIDE), BF),
            shape((16, 32, 4 * WIDE), BF),
            shape((4, 16, 48, 512), BF),
            shape((4, 16, 16, 512), BF),
            shape((8, 256), F32),
        ),
        in_specs=[IN_ANY] * 4 + [IN_VMEM] * 2,
        out_specs=(IN_ANY,) * 4 + (IN_VMEM,),
        scratch_shapes=[
            vmem((2, 4, 8, 32, WIDE), BF),
            vmem((2, 4, 8, 32, WIDE), BF),
            vmem((7, 2, 4, 32, WIDE), BF),
            vmem((2, 4, 32, WIDE), BF),
            vmem((4, 8, 32, WIDE), BF),
            vmem((4, 8, 32, WIDE), BF),
            vmem((7, 4, 32, WIDE), BF),
            vmem((4, 32, WIDE), BF),
            vmem((8, 48, D), BF),
            vmem((8, 48, D), BF),
            vmem((7, 48, D), BF),
            vmem((48, D), BF),
            vmem((8, 16, D), BF),
            vmem((8, 16, D), BF),
            vmem((7, 16, D), BF),
            vmem((16, D), BF),
            vmem((7, 8, 256), F32),
            vmem((16, 8, 256), F32),
        ]
        + dma_sems(4)
        + dma_sems(28)
        + dma_sems(12)
        + dma_sems(28)
        + dma_sems(32)
        + dma_sems(7)
        + dma_sems(15)
        + [pltpu.SemaphoreType.DMA((8,))],
        compiler_params=params(5),
        name="sum_grads",
    )(gu_p, qkv_p, down_p, out_p, ln_p, bias_p)


def matmul(a, b):
    return jnp.dot(a, b, preferred_element_type=F32)


def matmul_t(a, b):
    return lax.dot_general(a, b, ROWS_BY_COLS, preferred_element_type=F32)


def outer(a, b):
    return lax.dot_general(a, b, OVER_ROWS, preferred_element_type=F32).astype(BF)


def on_device(
    block_in, segments, ln1_gain, ln1_bias, qkv_weight, qkv_bias, out_weight,
    ln2_gain, ln2_bias, gate_up_weight, down_weight, cotangent,
):
    zero = jnp.zeros((256,), F32)
    par = jnp.stack([ln1_gain, ln1_bias, ln2_gain, ln2_bias, zero, zero, zero, zero])
    gate_up = jnp.transpose(gate_up_weight, (1, 0, 2))
    x_full, cot_full, par, qkv_s, out_s, gu_s, down_s = gather_inputs(
        block_in, cotangent, par, qkv_weight, out_weight, gate_up, down_weight
    )
    tables = rotary_tables(segments)
    seg_col = segments[:, None]
    seg_row = segments[None, :]
    scaled, _ = norm(x_full.astype(F32))
    normed = (scaled * par[0:1] + par[1:2]).astype(BF)
    proj = matmul(normed, qkv_s) + qkv_bias[None, :]
    qkv, attended, maxima, totals = attention(proj, tables, seg_col, seg_row)
    hidden_in, normed_two = attend_out(attended, out_s, x_full, par)
    gate = matmul(normed_two, gu_s[0])
    up = matmul(normed_two, gu_s[1])
    sig = jax.nn.sigmoid(gate)
    lane = lax.broadcasted_iota(jnp.int32, (1, WIDE), 1)
    kept = (lane >= 128) | (lax.axis_index("row") < 2)
    act = gate * sig
    hidden = jnp.where(kept, act * up, 0.0).astype(BF)
    grad_hidden = jnp.where(kept, matmul_t(cot_full, down_s), 0.0)
    grad_gate = (grad_hidden * up * (sig * (1.0 + gate * (1.0 - sig)))).astype(BF)
    grad_up = (grad_hidden * act).astype(BF)
    grad_in, branch, activations, sums_two = mlp_back(
        grad_gate, grad_up, gu_s, hidden, down_s, hidden_in, cot_full, par
    )
    grad_att = matmul_t(branch, out_s).astype(BF)
    grad_proj, bias_sums = attention_back(
        qkv, grad_att, tables, seg_col, seg_row, maxima, totals
    )
    input_grad, sums_one = input_back(grad_proj, qkv_s, x_full, grad_in, par)
    gu_p = jnp.stack([outer(normed_two, grad_gate), outer(normed_two, grad_up)])
    qkv_p = outer(normed, grad_proj)
    down_p = outer(hidden, cot_full)
    out_p = outer(attended, branch)
    ln_p = jnp.concatenate([sums_one[0:2], sums_two[0:2], jnp.zeros((4, D), F32)])
    bias_p = jnp.concatenate(
        [jnp.zeros((4, 256), F32), bias_sums[0].reshape(3, 256), jnp.zeros((1, 256), F32)]
    )
    gu_f, qkv_f, down_f, out_f, small = sum_grads(
        gu_p.reshape(2, 4, 2, 8, 32, WIDE),
        qkv_p.reshape(4, 2, 8, 32, WIDE),
        down_p.reshape(2, 8, 48, D),
        out_p.reshape(2, 8, 16, D),
        ln_p,
        bias_p,
    )
    gu_f = gu_f.reshape(4, 2, 512, WIDE)
    gu_f = jnp.concatenate([gu_f[0], gu_f[1], gu_f[2, :, :, 128:], gu_f[3, :, :, 128:]], axis=2)
    gu_grad = jnp.transpose(gu_f, (1, 0, 2)).astype(F32)
    down_f = down_f.reshape(4, WIDE, 512)
    down_grad = jnp.concatenate(
        [down_f[0], down_f[1], down_f[2, 128:], down_f[3, 128:]], axis=0
    ).astype(F32)
    return (
        activations,
        input_grad,
        small[0],
        small[1],
        qkv_f.reshape(512, 4 * WIDE).astype(F32),
        small[4:7].reshape(WIDE),
        out_f.reshape(1024, 512).astype(F32),
        small[2],
        small[3],
        gu_grad,
        down_grad,
    )


def solution(mesh):
    wide = P("dp", ("row", "col"))
    vector = P(("row", "col"))
    return jax.shard_map(
        on_device,
        mesh=mesh,
        in_specs=(
            wide, P("dp"), vector, vector, P("row", "col"), P(("col", "row")), P("col", "row"),
            vector, vector, P("row", None, "col"), P("col", "row"), wide,
        ),
        out_specs=(
            wide, wide, vector, vector, P("row", "col"), P(("col", "row")), P("col", "row"),
            vector, vector, P("row", None, "col"), P("col", "row"),
        ),
        check_vma=False,
    )
```

time: 881 us -> 674 us (0.77)
  waiting for transfers between devices: 577 us -> 0 us
  Pallas kernels: 0 us -> 570 us
  blocking collectives: 137 us -> 0 us
  matrix products: 73.1 us -> 33.8 us
  other arithmetic: 44.4 us -> 27.7 us
  between operations: 14.3 us -> 1.43 us
    pallas_call x0 -> x7, Pallas kernels: none -> 570 us  [the longest x1 192 us: sum_grads(): pl.pallas_call(sum_grads_kernel, out_shape=(shape((4, 2, 16, 32, WIDE), B...]
    psum x1 -> x0, waiting for transfers between devices: 250 us -> none  [on_device(): lax.psum(gate_up_grad.astype(jnp.bfloat16), 'dp').astype(jnp.float32)]
    reduce_scatter x8 -> x0, waiting for transfers between devices: 171 us -> none  [the longest x4 146 us: sum_rows(): lax.psum_scatter(partial_value.astype(jnp.bfloat16), 'row', scatter_dimen...]
    all_gather x4 -> x0, waiting for transfers between devices: 156 us -> none  [the longest x2 98.4 us: grad_rows(): return lax.all_gather(operand, 'row', axis=2, tiled=True)]
    psum x5 -> x0, blocking collectives: 107 us -> none  [the longest x4 79.8 us: feature_sums(): lax.psum((jnp.sum(first_term, axis=1), jnp.sum(second_term, axis=1)), ('r...]
    dot_general x17 -> x10, matrix products: 68.4 us -> 33.8 us  [the longest x3 14.8 us: matmul(): return jnp.dot(a, b, preferred_element_type=F32)]
    all_gather x4 -> x0, blocking collectives: 29.8 us -> none  [the longest x2 15 us: grad_cols(): return lax.all_gather(operand, 'col', axis=1, tiled=True)]
    unnamed x70 -> x47, local copies, waits for them, and re-layouts: 17.9 us -> 7.36 us
  transfers between devices with their start and end apart: 13 -> 0, of which waited for: 11 -> 0; matrix products, arithmetic and copies ran while one was open for 7% -> 0% of each run, Pallas kernels for 0% -> 0%
where the time goes in v1:
time: 674 us; the launch traced here: 669 us
  Pallas kernels  570 us (85%)
  local copies, waits for them, and re-layouts  36 us (5%)
  matrix products  33.8 us (5%)
  other arithmetic  27.7 us (4%)
    pallas_call x1, Pallas kernels, sum_grads(): pl.pallas_call(sum_grads_kernel, out_shape=(shape((4, 2, 16, 32, WIDE), B...  192 us
    pallas_call x1, Pallas kernels, gather_inputs(): pl.pallas_call(gather_kernel, out_shape=(shape((TOK, D), BF), shape((TOK,...  142 us
    pallas_call x1, Pallas kernels, mlp_back(): pl.pallas_call(mlp_back_kernel, out_shape=(shape((OWN, D), F32), shape((T...  113 us
    pallas_call x1, Pallas kernels, attend_out(): pl.pallas_call(attend_out_kernel, out_shape=(jax.ShapeDtypeStruct((OWN, D...  63 us
    pallas_call x1, Pallas kernels, input_back(): pl.pallas_call(input_back_kernel, out_shape=(shape((TOK, 256), BF), shape...  40 us
    dot_general x3, matrix products, matmul(): return jnp.dot(a, b, preferred_element_type=F32)  14.8 us

profile of v1, /device:TPU:1, one launch (start us, length us, event | category | flops | bytes accessed | tf_op | source)
XLA Modules:
  0.0 668.6 jit_solution(8827267665761017876)
XLA Ops:
  2.0 5.9 copy.49
  7.9 141.9 %gather_inputs.1 = (bf16[512,2048]{1,0:T(8,128)(2,1)}, bf16[512,2048]{1,0:T(8,128)(2,1)}, f32[8,2048]{1,0:T(8,128)}, bf16[4,16,32,768]{3,2,1,0:T(8,128)(2,1)}, b...) custom-call(bf16[512,256]{1,0:T(8,128)(2,1)} %x_in.1, ...), custom_call_target="tpu_custom_call" | custom-call | tf_op jit(solution)/shard_map/gather_inputs/pallas_call | solution.py:183
  149.7 2.3 convert_reduce_fusion
  153.0 5.7 convolution_add_fusion.proj
  160.6 3.8 concatenate.43
  165.4 3.5 concatenate.41
  171.4 8.5 %attention.1 = (bf16[512,768]{1,0:T(8,128)(2,1)}, bf16[512,256]{1,0:T(8,128)(2,1)}, f32[512,128]{1,0:T(8,128)}, f32[512,128]{1,0:T(8,128)}) custom-call(f32[512,768]{1,0:T(8,128)} %convolution_add_fusion.proj, f32[3,512,384]{2,1,0:T(8,128)} %pad_maximum_fusion.1.tables, s32[512,1]{1,0:T(8,128)} %copy.38.seg_col, s32[1,512]{1,0:T(1,128)} %bitcast.104), custom_call_target="tpu_custom_call" | custom-call | tf_op jit(solution)/shard_map/attention/pallas_call | solution.py:521
  179.8 63.0 %attend_out.1 = (f32[64,2048]{1,0:T(8,128)}, bf16[512,2048]{1,0:T(8,128)(2,1)}) custom-call(bf16[512,256]{1,0:T(8,128)(2,1)} %get-tuple-element.42.attended, bf16[256,2048]{1,0:T(8,128)(2,1)} %bitcast.102, bf16[512,2048]{1,0:T(8,128)(2,1)} %get-tuple-element.39.x_full, f32[8,2048]{1,0:T(8,128)} %get-tuple-element.40.par), custom_call_target="tpu_custom_call" | custom-call | tf_op jit(solution)/shard_map/attend_out/pallas_call | solution.py:332
  242.8 3.5 fusion.13
  246.4 2.9 fusion.18
  249.3 3.0 fusion.17
  252.3 6.2 select_convert_fusion
  258.5 113.3 %mlp_back.1 = (f32[64,2048]{1,0:T(8,128)}, bf16[512,2048]{1,0:T(8,128)(2,1)}, bf16[512,256]{1,0:T(8,128)(2,1)}, f32[8,2048]{1,0:T(8,128)}) custom-call(bf16[512,768]{1,0:T(8,128)(2,1)} %get-tuple-element.72.grad_gate, bf16[512,768]{1,0:T(8,128)(2,1)} %get-tuple-element.73.grad_up, bf16[2,2048,768]{2,1,0:T(8,128)(2,1)} %bitcast.78, ...), custom_call_target="tpu_custom_call" | custom-call | tf_op jit(solution)/shard_map/mlp_back/pallas_call | solution.py:398
  371.8 3.0 convolution_convert_fusion.5.grad_att
  374.8 11.5 %attention_back.1 = (bf16[512,768]{1,0:T(8,128)(2,1)}, f32[8,768]{1,0:T(8,128)}) custom-call(bf16[512,768]{1,0:T(8,128)(2,1)} %get-tuple-element.48.qkv, bf16[512,256]{1,0:T(8,128)(2,1)} %convolution_convert_fusion.5.grad_att, f32[3,512,384]{2,1,0:T(8,128)} %pad_maximum_fusion.1.tables, s32[512,1]{1,0:T(8,128)} %copy.38.seg_col, s32[1,512]{1,0:T(1,128)} %bitcast.105, ...), custom_call_target="tpu_custom_call" | custom-call | tf_op jit(solution)/shard_map/attention_back/pallas_call | solution.py:578
  386.3 40.0 %input_back.1 = (bf16[512,256]{1,0:T(8,128)(2,1)}, f32[8,2048]{1,0:T(8,128)}) custom-call(bf16[512,768]{1,0:T(8,128)(2,1)} %get-tuple-element.52.grad_proj, bf16[2048,768]{1,0:T(8,128)(2,1)} %bitcast.89, bf16[512,2048]{1,0:T(8,128)(2,1)} %get-tuple-element.39.x_full, f32[64,2048]{1,0:T(8,128)} %get-tuple-element.53.grad_in, f32[8,2048]{1,0:T(8,128)} %get-tuple-element.40.par), custom_call_target="tpu_custom_call" | custom-call | tf_op jit(solution)/shard_map/input_back/pallas_call | solution.py:450
  430.7 3.5 convolution_convert_fusion
  434.2 3.9 convolution_convert_fusion.1
  441.9 3.2 pad_maximum_fusion.gu_p
  446.7 191.6 %sum_grads.1 = (bf16[4,2,16,32,768]{4,3,2,1,0:T(8,128)(2,1)}, bf16[16,32,3072]{2,1,0:T(8,128)(2,1)}, bf16[4,16,48,512]{3,2,1,0:T(8,128)(2,1)}, bf16[4,16,16,512]{3,2,1,0:T(8,128)(2,1)}, f32[8,256]{1,0:T(8,128)}) custom-call(bf16[2,4,2,8,32,768]{5,4,3,2,1,0:T(8,128)(2,1)} %pad_maximum_fusion.gu_p, bf16[4,2,8,32,768]{4,3,2,1,0:T(8,128)(2,1)} %bitcast.93, ...), custom_call_target="tpu_custom_call" | custom-call | tf_op jit(solution)/shard_map/sum_grads/pallas_call | solution.py:771
  641.4 2.7 maximum_convert_fusion
  644.4 2.7 copy_bitcast_fusion.1
  650.6 9.5 %convert_bitcast_fusion = f32[512,2,2816]{2,1,0:T(2,128)} fusion(bf16[2,512,640]{2,0,1:T(2,128)(2,1)S(1)} %get-tuple-element.89, bf16[2,512,640]{2,0,1:T(2,128)(2,1)S(1)} %get-tuple-element.90, bf16[2,512,768]{2,0,1:T(2,128)(2,1)S(1)} %copy.43, bf16[2,512,768]{2,0,1:T(2,128)(2,1)S(1)} %copy.42), kind=kLoop, calls=%fused_computation | loop fusion | flops 23068672 | bytes 17301504 | tf_op jit(solution)/shard_map/convert_element_type | solution.py:881
  660.2 3.7 bitcast_convert_fusion
  (92 shorter events, 28.3 us)
Async XLA Ops:
  7.9 145.1 %copy-start.19 = (f32[768]{0:T(1024)S(1)}, f32[768]{0:T(1024)}, u32[]{:S(2)}) copy-start(f32[768]{0:T(1024)} %param.18) | copy-start | bytes 9220
  153.0 5.7 copy-start.15
  242.8 3.5 copy-start.17
  246.4 3.0 copy-start.1
  246.4 3.0 copy-start.3
  258.5 113.3 %copy-start.7 = (bf16[16,16,2048]{2,1,0:T(8,128)(2,1)S(1)}, bf16[16,16,2048]{2,1,0:T(8,128)(2,1)}, u32[]{:S(2)}) copy-start(bf16[16,16,2048]{2,1,0:T(8,128)(2,1)} %get-tuple-element.43) | copy-start | bytes 3145732
  386.3 42.7 %copy-start.5 = (bf16[512,2048]{1,0:T(8,128)(2,1)S(1)}, bf16[512,2048]{1,0:T(8,128)(2,1)}, u32[]{:S(2)}) copy-start(bf16[512,2048]{1,0:T(8,128)(2,1)} %get-tuple-element.49) | copy-start | bytes 6291460
  386.3 42.7 %copy-start.8 = (bf16[512,256]{1,0:T(8,128)(2,1)S(1)}, bf16[512,256]{1,0:T(8,128)(2,1)}, u32[]{:S(2)}) copy-start(bf16[512,256]{1,0:T(8,128)(2,1)} %get-tuple-element.42.attended) | copy-start | bytes 786436
  426.3 4.4 copy-start.4
  426.3 4.4 copy-start.11
  430.7 3.5 copy-start
  430.7 3.5 copy-start.12
  434.2 3.9 copy-start.10
  434.2 3.9 copy-start.18
  438.1 1.9 copy-start.9
  638.3 5.9 slice-start
  641.4 2.8 slice-start.1
  650.6 9.5 %copy-start.2 = (bf16[16,32,3072]{2,1,0:T(8,128)(2,1)S(1)}, bf16[16,32,3072]{2,1,0:T(8,128)(2,1)}, u32[]{:S(2)}) copy-start(bf16[16,32,3072]{2,1,0:T(8,128)(2,1)} %get-tuple-element.59) | copy-start | bytes 9437188
  660.2 3.7 copy-start.6
  663.9 1.7 copy-start.16
  663.9 2.9 copy-start.13
  663.9 3.6 copy-start.14

commit v2 on v1

--- a/solution.py
+++ b/solution.py
@@ -46,6 +46,20 @@
     def chip(self, q):
         return (q * 2 + self.core, self.x, self.zh)
 
+    def mate(self):
+        return (self.dp, self.x, 1 - self.zh)
+
+    def near_replicas(self):
+        def chip(y, zl):
+            return ((y * 2 + zl) * 2 + self.core, self.x, self.zh)
+
+        return [
+            chip((self.y + 1) % 4, self.zl),
+            chip((self.y + 3) % 4, self.zl),
+            chip(self.y, 1 - self.zl),
+            self.sibling(),
+        ]
+
     def sibling(self):
         return (self.q * 2 + 1 - self.core, self.x, self.zh)
 
@@ -96,133 +110,434 @@
     return 5 * x + jnp.minimum(x, 1)
 
 
-def gather_kernel(
-    x_in, cot_in, par_in, qkv_w, out_w, gu_w, down_w,
-    x_out, cot_out, par_out, qkv_s, out_s, gu_s, down_s,
-    act_send, act_recv, a_send, a_recv, b_send, b_recv, c_send, c_recv, local,
+def settle(ref, sems, index, device):
+    send, recv = sems
+    return pltpu.make_async_remote_copy(
+        src_ref=ref,
+        dst_ref=ref,
+        send_sem=send.at[index],
+        recv_sem=recv.at[index],
+        device_id=device,
+        device_id_type=MESH,
+    )
+
+
+class Gather:
+    def __init__(self, pos, pair, device, whole, half, sems, base=0, on_piece=None):
+        self.pos, self.pair, self.device = pos, pair, device
+        self.whole, self.half, self.sems, self.base = whole, half, sems, base
+        self.right, self.left, self.far = (pos + 1) % 4, (pos + 3) % 4, (pos + 2) % 4
+        self.on_piece = on_piece or (lambda r, p, k: None)
+        self.copies = {}
+
+    def push(self, index, ref, device, src=None):
+        copy = push(ref if src is None else src, ref, self.sems, self.base + index, device)
+        self.copies[index] = copy
+
+    def arrived(self, index, ref):
+        settle(ref, self.sems, self.base + index, self.device(self.pos, self.pair)).wait_recv()
+
+    def start(self, own=None):
+        ref = self.whole(self.pos, self.pair)
+        self.push(1, ref, self.device(self.right, self.pair), own)
+        self.push(2, ref, self.device(self.left, self.pair), own)
+        self.push(0, ref, self.device(self.pos, 1 - self.pair), own)
+        self.on_piece(self.pos, self.pair, 0)
+
+    def forward(self, first, pair, slot):
+        self.arrived(first, self.whole(self.left, pair))
+        self.push(first + 2, self.half(self.left, pair, 0), self.device(self.right, self.pair))
+        self.on_piece(self.left, pair, slot)
+        self.arrived(first + 1, self.whole(self.right, pair))
+        self.push(first + 3, self.half(self.right, pair, 1), self.device(self.left, self.pair))
+        self.on_piece(self.right, pair, slot + 1)
+
+    def forward_ring(self):
+        self.forward(1, self.pair, 1)
+
+    def spread_pair(self):
+        ref = self.whole(self.pos, 1 - self.pair)
+        self.arrived(0, ref)
+        self.push(5, ref, self.device(self.right, self.pair))
+        self.push(6, ref, self.device(self.left, self.pair))
+        self.on_piece(self.pos, 1 - self.pair, 3)
+
+    def forward_pair(self):
+        self.forward(5, 1 - self.pair, 4)
+
+    def finish(self):
+        for first, pair, slot in ((3, self.pair, 6), (7, 1 - self.pair, 7)):
+            self.arrived(first, self.half(self.far, pair, 0))
+            self.arrived(first + 1, self.half(self.far, pair, 1))
+            self.on_piece(self.far, pair, slot)
+
+    def drain(self):
+        for copy in self.copies.values():
+            copy.wait_send()
+
+
+class RowScatter:
+    def __init__(self, at, part, half_in, full_in, pair_in, pair_out, sems, base=0):
+        self.at, self.part, self.half_in, self.full_in = at, part, half_in, full_in
+        self.pair_in, self.pair_out, self.sems, self.base = pair_in, pair_out, sems, base
+        self.right, self.left = (at.x + 1) % 4, (at.x + 3) % 4
+        self.planes = (1 - at.zh, at.zh)
+        self.copies = []
+
+    def rows(self, x, plane, half=None):
+        start = (x * 2 + plane) * OWN
+        if half is None:
+            return pl.ds(pl.multiple_of(start, OWN), OWN)
+        return pl.ds(pl.multiple_of(start + half * (OWN // 2), OWN // 2), OWN // 2)
+
+    def push(self, index, src, dst, device):
+        self.copies.append(push(src, dst, self.sems, self.base + index, device))
+
+    def arrived(self, index, ref):
+        settle(ref, self.sems, self.base + index, self.at.row(self.at.x)).wait_recv()
+
+    def first(self):
+        far = (self.at.x + 2) % 4
+        for role, plane in enumerate(self.planes):
+            for side, x in enumerate((self.right, self.left)):
+                self.push(
+                    role * 4 + side,
+                    self.part.at[self.rows(far, plane, side)],
+                    self.half_in.at[role, side],
+                    self.at.row(x),
+                )
+
+    def second(self, role):
+        plane = self.planes[role]
+        for side, x in enumerate((self.right, self.left)):
+            box = self.half_in.at[role, side]
+            self.arrived(role * 4 + side, box)
+            rows = self.rows(x, plane, side)
+            self.part[rows, :] = (self.part[rows, :].astype(F32) + box[...].astype(F32)).astype(BF)
+            self.push(
+                role * 4 + 2 + side,
+                self.part.at[self.rows(x, plane)],
+                self.full_in.at[role, side],
+                self.at.row(x),
+            )
+
+    def own(self, role):
+        for side in range(2):
+            self.arrived(role * 4 + 2 + side, self.full_in.at[role, side])
+        total = self.part[self.rows(self.at.x, self.planes[role]), :].astype(F32)
+        return total + self.full_in[role, 0].astype(F32) + self.full_in[role, 1].astype(F32)
+
+    def third(self):
+        self.pair_out[...] = self.own(0).astype(BF)
+        self.push(8, self.pair_out, self.pair_in, self.at.mate())
+
+    def fourth(self):
+        total = self.own(1)
+        self.arrived(8, self.pair_in)
+        return total + self.pair_in[...].astype(F32)
+
+    def drain(self):
+        for copy in self.copies:
+            copy.wait_send()
+
+
+def scatter_scratch():
+    return [
+        pltpu.VMEM((TOK, D), BF),
+        pltpu.VMEM((2, 2, OWN // 2, D), BF),
+        pltpu.VMEM((2, 2, OWN, D), BF),
+        pltpu.VMEM((OWN, D), BF),
+        pltpu.VMEM((OWN, D), BF),
+    ] + dma_sems(9)
+
+
+def row_gather(at, ref, sems, base=0):
+    def whole(x, plane):
+        return ref.at[pl.ds(pl.multiple_of((x * 2 + plane) * OWN, OWN), OWN)]
+
+    def half(x, plane, side):
+        start = (x * 2 + plane) * OWN + side * (OWN // 2)
+        return ref.at[pl.ds(pl.multiple_of(start, OWN // 2), OWN // 2)]
+
+    return Gather(at.x, at.zh, lambda x, plane: (at.dp, x, plane), whole, half, sems, base)
+
+
+def column_gather(at, ref, sems, base=0):
+    def columns(x, plane):
+        return pl.ds(pl.multiple_of((x * 2 + plane) * 256, 256), 256)
+
+    def whole(x, plane):
+        return ref.at[:, columns(x, plane)]
+
+    def half(x, plane, side):
+        return ref.at[pl.ds(side * 256, 256), columns(x, plane)]
+
+    return Gather(at.x, at.zh, lambda x, plane: (at.dp, x, plane), whole, half, sems, base)
+
+
+def front_kernel(
+    x_in, cot_in, par_in, bias_in, seg_col, seg_row, qkv_w, out_w, gu_w, down_w,
+    cot_out, par_out, normed_out, qkv_out, att_out, max_out, sum_out, tab_out, own_out,
+    hidden_out, normed2_out, qkv_s_out, out_s_out, gu_s, down_s,
+    x_v, normed, par, proj, tables, qkv_s, out_s, normed2, rows,
+    part, half_in, full_in, pair_in, pair_out, rs_send, rs_recv,
+    par_send, par_recv, act_send, act_recv, a_send, a_recv, dp_send, dp_recv, core_send, core_recv,
+    local,
 ):
     at = Place()
-    greet(group_others(at) + chip_others(at) + [at.sibling()])
-    act, step_a, step_b, step_c = (
-        (act_send, act_recv), (a_send, a_recv), (b_send, b_recv), (c_send, c_recv)
-    )
-    dp, x, core, q = at.dp, at.x, at.core, at.q
+    greet(group_others(at) + at.near_replicas())
+    dp, x, core = at.dp, at.x, at.core
+    act, step_a, step_dp = (act_send, act_recv), (a_send, a_recv), (dp_send, dp_recv)
+    step_core, step_par = (core_send, core_recv), (par_send, par_recv)
+    slabs = (qkv_s, out_s, gu_s, down_s)
 
     def source(k, xt):
         if k == 0:
-            return qkv_w.at[pl.ds(dp * 32, 32), pl.ds(xt * WIDE, WIDE)]
+            return qkv_w.at[pl.ds(dp * 32, 32), pl.ds(pl.multiple_of(xt * WIDE, WIDE), WIDE)]
         if k == 1:
             return out_w.at[pl.ds(xt * 256 + dp * 16, 16), :]
+        start = pl.multiple_of(tile_start(xt) * 128, 128)
         if k == 2:
-            return gu_w.at[:, pl.ds(dp * 32, 32), pl.ds(tile_start(xt) * 128, WIDE)]
-        return down_w.at[pl.ds(tile_start(xt) * 128 + dp * 48, 48), :]
-
-    def landing(k, xs):
+            return gu_w.at[:, pl.ds(dp * 32, 32), pl.ds(start, WIDE)]
+        return down_w.at[pl.ds(start + dp * 48, 48), :]
+
+    def landing(k, xs, p):
         if k == 0:
-            return qkv_s.at[xs, dp]
-        if k == 1:
-            return out_s.at[dp, :, pl.ds(xs * 512, 512)]
+            return qkv_s.at[xs, p]
         if k == 2:
-            return gu_s.at[:, xs, dp]
-        return down_s.at[dp, :, pl.ds(xs * 512, 512)]
-
-    def piece(k, p):
-        if k == 0:
-            return qkv_s.at[:, p]
-        if k == 1:
-            return out_s.at[p]
-        if k == 2:
-            return gu_s.at[:, :, p]
-        return down_s.at[p]
-
-    waits = []
+            return gu_s.at[:, xs, p]
+        return slabs[k].at[p, :, pl.ds(pl.multiple_of(xs * 512, 512), 512)]
+
+    def replica(y, zl):
+        return (y * 2 + zl) * 2 + core
+
+    def whole(k):
+        def of(y, zl):
+            p = replica(y, zl)
+            if k == 0:
+                return qkv_s.at[:, p]
+            if k == 2:
+                return gu_s.at[:, :, p]
+            return slabs[k].at[p]
+
+        return of
+
+    def half(k):
+        def of(y, zl, side):
+            p = replica(y, zl)
+            if k == 0:
+                return qkv_s.at[pl.ds(side * 2, 2), p]
+            if k == 2:
+                return gu_s.at[side, :, p]
+            return slabs[k].at[p, :, pl.ds(side * 1024, 1024)]
+
+        return of
+
+    core_copies = []
+
+    def to_sibling(k):
+        def on_piece(y, zl, slot):
+            ref = whole(k)(y, zl)
+            core_copies.append(push(ref, ref, step_core, k * 8 + slot, at.sibling()))
+
+        return on_piece
+
+    first = {}
+
+    def send_rows(k):
+        for j in (2, 1, 3):
+            xt = (x + j) % 4
+            first[k, j] = push(
+                source(k, xt), landing(k, x, dp), step_a, k * 3 + j - 1, at.row(xt)
+            )
+        first[k, 0] = pltpu.make_async_copy(source(k, x), landing(k, x, dp), local.at[k])
+        first[k, 0].start()
+
+    weights = [
+        Gather(
+            at.y, at.zl, lambda y, zl: (replica(y, zl), x, at.zh), whole(k), half(k), step_dp, k * 9,
+            to_sibling(k),
+        )
+        for k in range(4)
+    ]
+    w_qkv, w_out, w_gu, w_down = weights
+
+    def begin(k):
+        first[k, 0].wait()
+        for j in range(1, 4):
+            first[k, j].wait_recv()
+        weights[k].start()
+
+    def from_sibling(k):
+        ref = whole(k)(at.y, at.zl)
+        for slot in range(8):
+            settle(ref, step_core, k * 8 + slot, at.sibling()).wait_recv()
+
+    slot = pl.ds(pl.multiple_of(at.g * 256, 256), 256)
+    send_rows(0)
+    gx = column_gather(at, x_v, act, 0)
+    gx.start(x_in)
+    par_copies = []
+    for j, device in enumerate(group_others(at)):
+        par_copies.append(push(par_in, par.at[:, slot], step_par, j, device))
+    own = [
+        pltpu.make_async_copy(x_in, x_v.at[:, slot], local.at[4]),
+        pltpu.make_async_copy(par_in, par.at[:, slot], local.at[5]),
+        pltpu.make_async_copy(cot_in, cot_out.at[:, slot], local.at[6]),
+    ]
+    for copy in own:
+        copy.start()
+    send_rows(1)
+    send_rows(2)
+    send_rows(3)
+    begin(0)
+    make_tables(seg_col, seg_row, tables)
+    gx.forward_ring()
+    gx.spread_pair()
+    w_qkv.forward_ring()
+    w_qkv.spread_pair()
+    begin(1)
+    gx.forward_pair()
+    w_qkv.forward_pair()
+    w_out.forward_ring()
+    w_out.spread_pair()
+    gx.finish()
+    gcot = column_gather(at, cot_out, act, 9)
+    gcot.start(cot_in)
+    begin(2)
+    for copy in own:
+        copy.wait()
+    for copy in par_copies:
+        copy.wait_recv()
+
+    def norm_rows(i, carry):
+        block = pl.ds(pl.multiple_of(i * 32, 32), 32)
+        scaled, _ = norm(x_v[block, :].astype(F32))
+        normed[block, :] = (scaled * par[0:1, :] + par[1:2, :]).astype(BF)
+        return carry
+
+    lax.fori_loop(0, TOK // 32, norm_rows, 0)
+    w_qkv.finish()
+    w_out.forward_pair()
+    from_sibling(0)
+    outgoing = []
+
+    def put(src, dst, index):
+        copy = pltpu.make_async_copy(src, dst, local.at[index])
+        copy.start()
+        outgoing.append(copy)
+
+    put(normed, normed_out, 7)
+    put(qkv_s, qkv_s_out, 8)
+    put(x_v.at[own_rows(at)], own_out, 9)
+    put(par, par_out, 10)
+    between = [
+        lambda: (gcot.forward_ring(), w_out.finish()),
+        lambda: (gcot.spread_pair(), w_gu.forward_ring(), w_gu.spread_pair()),
+        lambda: (begin(3),),
+        lambda: (gcot.forward_pair(), w_gu.forward_pair()),
+        lambda: (w_down.forward_ring(), w_down.spread_pair()),
+        lambda: (gcot.finish(), w_gu.finish()),
+        lambda: (from_sibling(1),),
+    ]
+    for n in range(3):
+        cols = pl.ds(n * 256, 256)
+        weight = qkv_s[:, :, :, cols].reshape(D, 256)
+        proj[:, cols] = (
+            jnp.dot(normed[...], weight, preferred_element_type=F32) + bias_in[:, cols]
+        )
+        between[n]()
+    attend(proj, tables, seg_col, seg_row, qkv_out, att_out, max_out, sum_out, between[3:])
+    put(out_s, out_s_out, 11)
+    put(tables, tab_out, 12)
+    rs = RowScatter(at, part, half_in, full_in, pair_in, pair_out, (rs_send, rs_recv))
+    weight = out_s[...].reshape(256, D)
+
+    def product(xt):
+        block = pl.ds(pl.multiple_of(xt * 128, 128), 128)
+        part[block, :] = jnp.dot(att_out[block, :], weight, preferred_element_type=F32).astype(BF)
+
+    product((x + 2) % 4)
+    rs.first()
+    product((x + 1) % 4)
+    product((x + 3) % 4)
+    rs.second(0)
+    rs.second(1)
+    product(x)
+    w_down.forward_pair()
+    rs.third()
+    hidden_in = rs.fourth() + x_v[own_rows(at), :].astype(F32)
+    hidden_out[...] = hidden_in
+    scaled, _ = norm(hidden_in)
+    rows[...] = (scaled * par[2:3, :] + par[3:4, :]).astype(BF)
+    normed2[own_rows(at), :] = rows[...]
+    gn = row_gather(at, normed2, act, 18)
+    gn.start(rows)
+    w_down.finish()
+    gn.forward_ring()
+    gn.spread_pair()
+    gn.forward_pair()
+    from_sibling(2)
+    from_sibling(3)
+    gn.finish()
+    put(normed2, normed2_out, 13)
     for k in range(4):
         for j in range(1, 4):
-            xt = (x + j) % 4
-            waits.append(push(source(k, xt), landing(k, x), step_a, k * 3 + j - 1, at.row(xt)))
-    own = []
-    for k in range(4):
-        own.append(pltpu.make_async_copy(source(k, x), landing(k, x), local.at[k]))
-    slot = pl.ds(at.g * 256, 256)
-    own.append(pltpu.make_async_copy(x_in, x_out.at[:, slot], local.at[4]))
-    own.append(pltpu.make_async_copy(cot_in, cot_out.at[:, slot], local.at[5]))
-    own.append(pltpu.make_async_copy(par_in, par_out.at[:, slot], local.at[6]))
-    for copy in own:
-        copy.start()
-    for j, device in enumerate(group_others(at)):
-        waits.append(push(par_in, par_out.at[:, slot], act, 14 + j, device))
-    for j, device in enumerate(group_others(at)):
-        waits.append(push(x_in, x_out.at[:, slot], act, j, device))
-    for j, device in enumerate(group_others(at)):
-        waits.append(push(cot_in, cot_out.at[:, slot], act, 7 + j, device))
-    for copy in own:
+            first[k, j].wait_send()
+        weights[k].drain()
+    for copy in core_copies + par_copies:
+        copy.wait_send()
+    for program in (gx, gcot, gn, rs):
+        program.drain()
+    for copy in outgoing:
         copy.wait()
-    second = []
-    for k in range(4):
-        for j in range(3):
-            waits[k * 3 + j].wait_recv()
-        for m, device in enumerate(chip_others(at)):
-            second.append(push(piece(k, dp), piece(k, dp), step_b, k * 7 + m, device))
-        third = push(piece(k, dp), piece(k, dp), step_c, k * 8, at.sibling())
-        waits.append(third)
-    for k in range(4):
-        for m in range(1, 8):
-            second[k * 7 + m - 1].wait_recv()
-            p = (q ^ m) * 2 + core
-            waits.append(push(piece(k, p), piece(k, p), step_c, k * 8 + m, at.sibling()))
-    for index, copy in enumerate(waits):
-        copy.wait_send()
-        if index >= 12:
-            copy.wait_recv()
-    for copy in second:
-        copy.wait_send()
-
-
-def gather_inputs(x_in, cot_in, par_in, qkv_w, out_w, gu_w, down_w):
+
+
+def front(x_in, cot_in, par_in, bias_in, seg_col, seg_row, qkv_w, out_w, gu_w, down_w):
     shape = jax.ShapeDtypeStruct
-    outs = pl.pallas_call(
-        gather_kernel,
+    vmem = pltpu.VMEM
+    return pl.pallas_call(
+        front_kernel,
         out_shape=(
             shape((TOK, D), BF),
+            shape((8, D), F32),
             shape((TOK, D), BF),
-            shape((8, D), F32),
+            shape((TOK, WIDE), BF),
+            shape((TOK, 256), BF),
+            shape((TOK, 128), F32),
+            shape((TOK, 128), F32),
+            shape((3, TOK, 384), F32),
+            shape((OWN, D), BF),
+            shape((OWN, D), F32),
+            shape((TOK, D), BF),
             shape((4, 16, 32, WIDE), BF),
             shape((16, 16, D), BF),
             shape((2, 4, 16, 32, WIDE), BF),
             shape((16, 48, D), BF),
         ),
-        in_specs=[IN_ANY] * 7,
-        out_specs=(IN_ANY,) * 7,
-        scratch_shapes=dma_sems(21)
+        in_specs=[IN_ANY] * 3 + [IN_VMEM] * 3 + [IN_ANY] * 4,
+        out_specs=(IN_ANY,) * 3 + (IN_VMEM,) * 4 + (IN_ANY,) * 2 + (IN_VMEM,) + (IN_ANY,) * 5,
+        scratch_shapes=[
+            vmem((TOK, D), BF),
+            vmem((TOK, D), BF),
+            vmem((8, D), F32),
+            vmem((TOK, WIDE), F32),
+            vmem((3, TOK, 384), F32),
+            vmem((4, 16, 32, WIDE), BF),
+            vmem((16, 16, D), BF),
+            vmem((TOK, D), BF),
+            vmem((OWN, D), BF),
+        ]
+        + scatter_scratch()
+        + dma_sems(7)
+        + dma_sems(27)
         + dma_sems(12)
-        + dma_sems(28)
+        + dma_sems(36)
         + dma_sems(32)
-        + [pltpu.SemaphoreType.DMA((7,))],
+        + [pltpu.SemaphoreType.DMA((14,))],
         compiler_params=params(1),
-        name="gather_inputs",
-    )(x_in, cot_in, par_in, qkv_w, out_w, gu_w, down_w)
-    x_full, cot_full, par_full, qkv_s, out_s, gu_s, down_s = outs
-    return (
-        x_full,
-        cot_full,
-        par_full,
-        qkv_s.reshape(D, WIDE),
-        out_s.reshape(256, D),
-        gu_s.reshape(2, D, WIDE),
-        down_s.reshape(WIDE, D),
-    )
-
-
-def settle(src, sems, index, device):
-    send, recv = sems
-    return pltpu.make_async_remote_copy(
-        src_ref=src,
-        dst_ref=src,
-        send_sem=send.at[index],
-        recv_sem=recv.at[index],
-        device_id=device,
-        device_id_type=MESH,
-    )
+        name="front",
+    )(x_in, cot_in, par_in, bias_in, seg_col, seg_row, qkv_w, out_w, gu_w, down_w)
 
 
 def scatter_sum(at, product, part, got, sems):
@@ -304,47 +619,6 @@
     mean = jnp.mean(inner, axis=1, keepdims=True)
     along = jnp.mean(inner * scaled, axis=1, keepdims=True)
     return inverse * (inner - mean - scaled * along)
-
-
-def attend_out_kernel(
-    attended, weight, x_full, par, hidden_out, normed_out,
-    part, got, rows, rs_send, rs_recv, ag_send, ag_recv, local,
-):
-    at = Place()
-    greet(group_others(at))
-    rs, ag = (rs_send, rs_recv), (ag_send, ag_recv)
-
-    def product(xt):
-        block = attended[pl.ds(pl.multiple_of(xt * 128, 128), 128), :]
-        return jnp.dot(block, weight[...], preferred_element_type=F32)
-
-    scatter_sum(at, product, part, got, rs)
-    hidden_in = summed(at, part, got, rs) + x_full[own_rows(at), :].astype(F32)
-    hidden_out[...] = hidden_in
-    scaled, _ = norm(hidden_in)
-    rows[...] = (scaled * par[2:3, :] + par[3:4, :]).astype(BF)
-    gather_rows(at, rows, normed_out, ag, local.at[0])
-    sent(at, got.at[0], rs)
-    settle_all(at, rows, ag)
-
-
-def attend_out(attended, weight, x_full, par):
-    return pl.pallas_call(
-        attend_out_kernel,
-        out_shape=(jax.ShapeDtypeStruct((OWN, D), F32), jax.ShapeDtypeStruct((TOK, D), BF)),
-        in_specs=[IN_VMEM] * 4,
-        out_specs=(IN_VMEM, IN_ANY),
-        scratch_shapes=[
-            pltpu.VMEM((TOK, D), BF),
-            pltpu.VMEM((7, OWN, D), BF),
-            pltpu.VMEM((OWN, D), BF),
-        ]
-        + dma_sems(7)
-        + dma_sems(7)
-        + [pltpu.SemaphoreType.DMA((1,))],
-        compiler_params=params(2),
-        name="attend_out",
-    )(attended, weight, x_full, par)
 
 
 def mlp_back_kernel(
@@ -419,7 +693,7 @@
 
 
 def input_back_kernel(
-    grad_proj, qkv_s, x_full, grad_in, par, out, sums_out,
+    grad_proj, qkv_s, x_own, grad_in, par, out, sums_out,
     part, got, rows, rs_send, rs_recv, tr_send, tr_recv, local,
 ):
     at = Place()
@@ -433,7 +707,7 @@
         )
 
     scatter_sum(at, product, part, got, rs)
-    scaled, inverse = norm(x_full[own_rows(at), :].astype(F32))
+    scaled, inverse = norm(x_own[...].astype(F32))
     grad = summed(at, part, got, rs)
     total = grad_in[...] + norm_back(grad, scaled, inverse, par[0:1, :])
     rows[...] = total.astype(BF)
@@ -445,7 +719,7 @@
     settle_all(at, rows.at[:, pl.ds(0, 256)], tr)
 
 
-def input_back(grad_proj, qkv_s, x_full, grad_in, par):
+def input_back(grad_proj, qkv_s, x_own, grad_in, par):
     shape = jax.ShapeDtypeStruct
     return pl.pallas_call(
         input_back_kernel,
@@ -461,7 +735,7 @@
         + [pltpu.SemaphoreType.DMA((1,))],
         compiler_params=params(4),
         name="input_back",
-    )(grad_proj, qkv_s, x_full, grad_in, par)
+    )(grad_proj, qkv_s, x_own, grad_in, par)
 
 
 def rotary(value, tables, sign):
@@ -473,6 +747,29 @@
     )
 
 
+def make_tables(seg_col, seg_row, tables):
+    half = ROT // 2
+    for block in range(4):
+        rows = pl.ds(block * 128, 128)
+        places = lax.broadcasted_iota(jnp.int32, (128, 128), 0) + block * 128
+        before = jnp.where(seg_row[0:1, :] < seg_col[rows, :], 1.0, 0.0)
+        starts = jnp.sum(before, axis=1, keepdims=True)
+        offsets = places.astype(F32) - starts
+        lane = lax.broadcasted_iota(jnp.int32, (128, 128), 1)
+        entry = lane % HD
+        power = (entry % half).astype(F32) * (-2.0 * math.log(10000.0) / ROT)
+        angles = offsets * jnp.exp(power)
+        cosine, sine = jnp.cos(angles), jnp.sin(angles)
+        keep = jnp.where(entry < ROT, cosine, 1.0)
+        fore = jnp.where(entry < half, -sine, 0.0)
+        back = jnp.where((entry >= half) & (entry < ROT), sine, 0.0)
+        for j, (table, rest) in enumerate(((keep, 1.0), (fore, 0.0), (back, 0.0))):
+            low = lane < HD
+            tables[j, rows, 0:128] = table
+            tables[j, rows, 128:256] = jnp.where(low, rest, table)
+            tables[j, rows, 256:384] = jnp.where(low, table, rest)
+
+
 def head_part(value, head, kind):
     start = head * 3 * HD + kind * HD
     return value[:, start : start + HD]
@@ -486,7 +783,7 @@
     return (cols <= rows) & same
 
 
-def attention_kernel(proj, tables, seg_col, seg_row, qkv_out, att_out, max_out, sum_out):
+def attend(proj, tables, seg_col, seg_row, qkv_out, att_out, max_out, sum_out, between):
     scale = 1.0 / math.sqrt(HD)
     for half in range(2):
         cols = pl.ds(half * 384, 384)
@@ -514,23 +811,8 @@
         for head in range(HEADS):
             max_out[rows, head : head + 1] = maxima[head]
             sum_out[rows, head : head + 1] = totals[head]
-
-
-def attention(proj, tables, seg_col, seg_row):
-    shape = jax.ShapeDtypeStruct
-    return pl.pallas_call(
-        attention_kernel,
-        out_shape=(
-            shape((TOK, WIDE), BF),
-            shape((TOK, 256), BF),
-            shape((TOK, 128), F32),
-            shape((TOK, 128), F32),
-        ),
-        in_specs=[IN_VMEM] * 4,
-        out_specs=(IN_VMEM,) * 4,
-        compiler_params=pltpu.CompilerParams(vmem_limit_bytes=VMEM_LIMIT),
-        name="attention",
-    )(proj, tables, seg_col, seg_row)
+        if block < len(between):
+            between[block]()
 
 
 def attention_back_kernel(
@@ -584,24 +866,6 @@
         compiler_params=pltpu.CompilerParams(vmem_limit_bytes=VMEM_LIMIT),
         name="attention_back",
     )(qkv, grad_att, tables, seg_col, seg_row, maxima, totals)
-
-
-def rotary_tables(segment):
-    places = jnp.arange(TOK, dtype=jnp.int32)
-    starts_flag = jnp.concatenate([jnp.array([True]), segment[1:] != segment[:-1]])
-    starts = lax.cummax(jnp.where(starts_flag, places, 0), axis=0)
-    offsets = (places - starts).astype(F32)
-    half = ROT // 2
-    frequencies = jnp.exp(jnp.arange(half, dtype=F32) * (-2.0 * math.log(10000.0) / ROT))
-    angles = offsets[:, None] * frequencies[None, :]
-    cosine, sine = jnp.cos(angles), jnp.sin(angles)
-    one, zero = jnp.ones((TOK, HD), F32), jnp.zeros((TOK, HD), F32)
-    rest = HD - ROT
-    keep = jnp.concatenate([cosine, cosine, one[:, :rest]], axis=1)
-    fore = jnp.concatenate([-sine, zero[:, : HD - half]], axis=1)
-    back = jnp.concatenate([zero[:, :half], sine, zero[:, :rest]], axis=1)
-    wide = [jnp.concatenate([t, t, e], axis=1) for t, e in ((keep, one), (fore, zero), (back, zero))]
-    return jnp.stack([jnp.concatenate([t, t], axis=1) for t in wide])
 
 
 def sum_grads_kernel(
@@ -831,17 +1095,17 @@
     zero = jnp.zeros((256,), F32)
     par = jnp.stack([ln1_gain, ln1_bias, ln2_gain, ln2_bias, zero, zero, zero, zero])
     gate_up = jnp.transpose(gate_up_weight, (1, 0, 2))
-    x_full, cot_full, par, qkv_s, out_s, gu_s, down_s = gather_inputs(
-        block_in, cotangent, par, qkv_weight, out_weight, gate_up, down_weight
-    )
-    tables = rotary_tables(segments)
     seg_col = segments[:, None]
     seg_row = segments[None, :]
-    scaled, _ = norm(x_full.astype(F32))
-    normed = (scaled * par[0:1] + par[1:2]).astype(BF)
-    proj = matmul(normed, qkv_s) + qkv_bias[None, :]
-    qkv, attended, maxima, totals = attention(proj, tables, seg_col, seg_row)
-    hidden_in, normed_two = attend_out(attended, out_s, x_full, par)
+    (
+        cot_full, par, normed, qkv, attended, maxima, totals, tables, x_own,
+        hidden_in, normed_two, qkv_s, out_s, gu_s, down_s,
+    ) = front(
+        block_in, cotangent, par, qkv_bias[None, :], seg_col, seg_row,
+        qkv_weight, out_weight, gate_up, down_weight,
+    )
+    qkv_s, out_s = qkv_s.reshape(D, WIDE), out_s.reshape(256, D)
+    gu_s, down_s = gu_s.reshape(2, D, WIDE), down_s.reshape(WIDE, D)
     gate = matmul(normed_two, gu_s[0])
     up = matmul(normed_two, gu_s[1])
     sig = jax.nn.sigmoid(gate)
@@ -859,7 +1123,7 @@
     grad_proj, bias_sums = attention_back(
         qkv, grad_att, tables, seg_col, seg_row, maxima, totals
     )
-    input_grad, sums_one = input_back(grad_proj, qkv_s, x_full, grad_in, par)
+    input_grad, sums_one = input_back(grad_proj, qkv_s, x_own, grad_in, par)
     gu_p = jnp.stack([outer(normed_two, grad_gate), outer(normed_two, grad_up)])
     qkv_p = outer(normed, grad_proj)
     down_p = outer(hidden, cot_full)

time: 674 us -> 533 us (0.79)
  Pallas kernels: 570 us -> 450 us
  local copies, waits for them, and re-layouts: 36 us -> 27.9 us
    pallas_call x3 -> x1, Pallas kernels: 213 us -> 115 us  [front(): pl.pallas_call(front_kernel, out_shape=(shape((TOK, D), BF), shape((8, D)...]
    pallas_call x1, Pallas kernels: 113 us -> 86.4 us  [mlp_back(): pl.pallas_call(mlp_back_kernel, out_shape=(shape((OWN, D), F32), shape((T...]
    concatenate x3 -> x0, local copies, waits for them, and re-layouts: 8.27 us -> none  [rotary_tables(): return jnp.stack([jnp.concatenate([t, t], axis=1) for t in wide])]
    pallas_call x1, Pallas kernels: 192 us -> 199 us  [sum_grads(): pl.pallas_call(sum_grads_kernel, out_shape=(shape((4, 2, 16, 32, WIDE), B...]
    dot_general x3 -> x2, matrix products: 14.8 us -> 9.19 us  [matmul(): return jnp.dot(a, b, preferred_element_type=F32)]
where the time goes in v2:
time: 533 us; the launch traced here: 530 us
  Pallas kernels  450 us (84%)
  matrix products  28.1 us (5%)
  local copies, waits for them, and re-layouts  27.9 us (5%)
  other arithmetic  22.3 us (4%)
    pallas_call x1, Pallas kernels, sum_grads(): pl.pallas_call(sum_grads_kernel, out_shape=(shape((4, 2, 16, 32, WIDE), B...  199 us
    pallas_call x1, Pallas kernels, front(): pl.pallas_call(front_kernel, out_shape=(shape((TOK, D), BF), shape((8, D)...  115 us
    pallas_call x1, Pallas kernels, mlp_back(): pl.pallas_call(mlp_back_kernel, out_shape=(shape((OWN, D), F32), shape((T...  86.4 us
    pallas_call x1, Pallas kernels, input_back(): pl.pallas_call(input_back_kernel, out_shape=(shape((TOK, 256), BF), shape...  38.1 us
    dot_general x5, matrix products, outer(): lax.dot_general(a, b, OVER_ROWS, preferred_element_type=F32).astype(BF)  12.5 us
    pallas_call x1, Pallas kernels, attention_back(): pl.pallas_call(attention_back_kernel, out_shape=(shape((TOK, WIDE), BF),...  11.4 us

profile of v2, /device:TPU:1, one launch (start us, length us, event | category | flops | bytes accessed | tf_op | source)
XLA Modules:
  0.0 529.7 jit_solution(9682797149600482052)
XLA Ops:
  3.5 5.9 %copy.40 = bf16[512,2,2816]{2,0,1:T(8,128)(2,1)} copy(bf16[512,2,2816]{2,1,0:T(2,128)(2,1)} %param.21) | data formatting | bytes 11534336 | tf_op args[9]
  10.0 115.1 %front.1 = (bf16[512,2048]{1,0:T(8,128)(2,1)}, f32[8,2048]{1,0:T(8,128)}, bf16[512,2048]{1,0:T(8,128)(2,1)}, bf16[512,768]{1,0:T(8,128)(2,1)}, bf16[512,256]{1,0...) custom-call(bf16[512,256]{1,0:T(8,128)(2,1)} %x_in.1, ...), custom_call_target="tpu_custom_call" | custom-call | tf_op jit(solution)/shard_map/front/pallas_call | solution.py:499
  125.1 3.6 fusion.4
  128.8 2.9 fusion.8
  131.7 3.4 fusion.7
  135.1 6.3 %select_convert_fusion = (bf16[512,768]{1,0:T(8,128)(2,1)}, bf16[512,768]{1,0:T(8,128)(2,1)}, bf16[512,768]{1,0:T(8,128)(2,1)}) fusion(pred[768]{0:T(1024)(128)(4,1)S(1)} %fusion.1, f32[512,768]{1,0:T(8,128)} %fusion.8, f32[512,768]{1,0:T(8,128)} %fusion.7, bf16[512,2048]{1,0:T(8,128)(2,1)} %get-tuple-element.41, bf16[2048,768]{1,0:T(8,128)(2,1)S(1)} %bitcast.79), kind=kOutput, calls=%fused_computation.10 | convolution fusion | flops 1617297408 | bytes 10748672 | tf_op jit(solution)/shard_map/dot_general | solution.py:1080
  141.4 86.4 %mlp_back.1 = (f32[64,2048]{1,0:T(8,128)}, bf16[512,2048]{1,0:T(8,128)(2,1)}, bf16[512,256]{1,0:T(8,128)(2,1)}, f32[8,2048]{1,0:T(8,128)}) custom-call(bf16[512,768]{1,0:T(8,128)(2,1)} %get-tuple-element.74.grad_gate, bf16[512,768]{1,0:T(8,128)(2,1)} %get-tuple-element.75.grad_up, bf16[2,2048,768]{2,1,0:T(8,128)(2,1)} %bitcast.65, ...), custom_call_target="tpu_custom_call" | custom-call | tf_op jit(solution)/shard_map/mlp_back/pallas_call | solution.py:672
  227.7 3.0 convolution_convert_fusion.5.grad_att
  230.8 11.4 %attention_back.1 = (bf16[512,768]{1,0:T(8,128)(2,1)}, f32[8,768]{1,0:T(8,128)}) custom-call(bf16[512,768]{1,0:T(8,128)(2,1)} %get-tuple-element.46.qkv, bf16[512,256]{1,0:T(8,128)(2,1)} %convolution_convert_fusion.5.grad_att, f32[3,512,384]{2,1,0:T(8,128)} %get-tuple-element.49.tables, s32[512,1]{1,0:T(8,128)} %copy.29.seg_col, s32[1,512]{1,0:T(1,128)} %bitcast.87, ...), custom_call_target="tpu_custom_call" | custom-call | tf_op jit(solution)/shard_map/attention_back/pallas_call | solution.py:860
  242.2 38.1 %input_back.1 = (bf16[512,256]{1,0:T(8,128)(2,1)}, f32[8,2048]{1,0:T(8,128)}) custom-call(bf16[512,768]{1,0:T(8,128)(2,1)} %get-tuple-element.52.grad_proj, bf16[2048,768]{1,0:T(8,128)(2,1)} %bitcast.75, bf16[64,2048]{1,0:T(8,128)(2,1)} %get-tuple-element.54.x_own, f32[64,2048]{1,0:T(8,128)} %get-tuple-element.55.grad_in, f32[8,2048]{1,0:T(8,128)} %get-tuple-element.44.par), custom_call_target="tpu_custom_call" | custom-call | tf_op jit(solution)/shard_map/input_back/pallas_call | solution.py:724
  283.0 1.7 convolution_convert_fusion.4
  284.8 3.5 convolution_convert_fusion.1
  288.3 1.9 convolution_convert_fusion.3
  290.2 1.9 convolution_convert_fusion.2
  292.1 3.2 pad_maximum_fusion.gu_p
  296.8 3.5 convolution_convert_fusion
  300.3 199.3 %sum_grads.1 = (bf16[4,2,16,32,768]{4,3,2,1,0:T(8,128)(2,1)}, bf16[16,32,3072]{2,1,0:T(8,128)(2,1)}, bf16[4,16,48,512]{3,2,1,0:T(8,128)(2,1)}, bf16[4,16,16,512]{3,2,1,0:T(8,128)(2,1)}, f32[8,256]{1,0:T(8,128)}) custom-call(bf16[2,4,2,8,32,768]{5,4,3,2,1,0:T(8,128)(2,1)} %pad_maximum_fusion.gu_p, bf16[4,2,8,32,768]{4,3,2,1,0:T(8,128)(2,1)} %bitcast.78, ...), custom_call_target="tpu_custom_call" | custom-call | tf_op jit(solution)/shard_map/sum_grads/pallas_call | solution.py:1035
  499.6 1.6 fusion.5
  502.7 2.7 maximum_convert_fusion
  505.7 2.7 copy_bitcast_fusion.1
  508.7 1.6 copy.33
  512.0 9.5 %convert_bitcast_fusion = f32[512,2,2816]{2,1,0:T(2,128)} fusion(bf16[2,512,640]{2,0,1:T(2,128)(2,1)S(1)} %get-tuple-element.84, bf16[2,512,640]{2,0,1:T(2,128)(2,1)S(1)} %get-tuple-element.85, bf16[2,512,768]{2,0,1:T(2,128)(2,1)S(1)} %copy.34, bf16[2,512,768]{2,0,1:T(2,128)(2,1)S(1)} %copy.33), kind=kLoop, calls=%fused_computation | loop fusion | flops 23068672 | bytes 17301504 | tf_op jit(solution)/shard_map/convert_element_type | solution.py:1145
  521.5 3.7 bitcast_convert_fusion
  525.2 1.7 bitcast_convert_fusion.1
  (66 shorter events, 13.9 us)
Async XLA Ops:
  3.5 5.9 %copy-start.14 = (f32[768]{0:T(1024)S(1)}, f32[768]{0:T(1024)}, u32[]{:S(2)}) copy-start(f32[768]{0:T(1024)} %param.17) | copy-start | bytes 9220
  125.1 3.6 copy-start.15
  128.7 3.0 copy-start
  128.7 2.9 copy-start.2
  141.4 86.4 %copy-start.18 = (bf16[16,16,2048]{2,1,0:T(8,128)(2,1)S(1)}, bf16[16,16,2048]{2,1,0:T(8,128)(2,1)}, u32[]{:S(2)}) copy-start(bf16[16,16,2048]{2,1,0:T(8,128)(2,1)} %get-tuple-element.48) | copy-start | bytes 3145732
  242.2 40.8 %copy-start.4 = (bf16[512,2048]{1,0:T(8,128)(2,1)S(1)}, bf16[512,2048]{1,0:T(8,128)(2,1)}, u32[]{:S(2)}) copy-start(bf16[512,2048]{1,0:T(8,128)(2,1)} %get-tuple-element.47) | copy-start | bytes 6291460
  242.2 40.8 %copy-start.12 = (bf16[512,256]{1,0:T(8,128)(2,1)S(1)}, bf16[512,256]{1,0:T(8,128)(2,1)}, u32[]{:S(2)}) copy-start(bf16[512,256]{1,0:T(8,128)(2,1)} %get-tuple-element.58) | copy-start | bytes 786436
  280.4 4.4 copy-start.9
  280.4 4.3 copy-start.17
  284.7 3.5 copy-start.8
  284.7 3.5 copy-start.16
  288.3 1.9 copy-start.7
  292.0 4.8 copy-start.3
  292.0 4.8 copy-start.6
  499.6 5.9 %slice-start = ((s8[6291456]{0:T(1024)(128)(4,1)}), s8[4194304]{0:T(1024)(128)(4,1)S(1)}, s32[]{:S(2)}) async-start(s8[6291456]{0:T(1024)(128)(4,1)} %bitcast.69), calls=%async_computation | async-start | bytes 8388608
  502.7 2.8 slice-start.1
  512.0 9.5 %copy-start.1 = (bf16[16,32,3072]{2,1,0:T(8,128)(2,1)S(1)}, bf16[16,32,3072]{2,1,0:T(8,128)(2,1)}, u32[]{:S(2)}) copy-start(bf16[16,32,3072]{2,1,0:T(8,128)(2,1)} %get-tuple-element.63) | copy-start | bytes 9437188
  521.5 3.7 copy-start.5
  525.2 1.7 copy-start.13
  525.2 2.9 copy-start.10
  525.2 3.6 copy-start.11

commit v3 on v2

--- a/solution.py
+++ b/solution.py
@@ -18,7 +18,7 @@
 BF = jnp.bfloat16
 F32 = jnp.float32
 MESH = pl.DeviceIdType.MESH
-VMEM_LIMIT = 60 * 2**20
+VMEM_LIMIT = 59 * 2**20
 ROWS_BY_COLS = (((1,), (1,)), ((), ()))
 OVER_ROWS = (((0,), (0,)), ((), ()))
 
@@ -128,11 +128,9 @@
         self.whole, self.half, self.sems, self.base = whole, half, sems, base
         self.right, self.left, self.far = (pos + 1) % 4, (pos + 3) % 4, (pos + 2) % 4
         self.on_piece = on_piece or (lambda r, p, k: None)
-        self.copies = {}
 
     def push(self, index, ref, device, src=None):
-        copy = push(ref if src is None else src, ref, self.sems, self.base + index, device)
-        self.copies[index] = copy
+        push(ref if src is None else src, ref, self.sems, self.base + index, device)
 
     def arrived(self, index, ref):
         settle(ref, self.sems, self.base + index, self.device(self.pos, self.pair)).wait_recv()
@@ -172,8 +170,11 @@
             self.on_piece(self.far, pair, slot)
 
     def drain(self):
-        for copy in self.copies.values():
-            copy.wait_send()
+        for index in range(9):
+            ref = self.whole(self.pos, self.pair)
+            if index in (3, 4, 7, 8):
+                ref = self.half(self.pos, self.pair, 0)
+            settle(ref, self.sems, self.base + index, self.device(self.pos, self.pair)).wait_send()
 
 
 class RowScatter:
@@ -182,7 +183,6 @@
         self.pair_in, self.pair_out, self.sems, self.base = pair_in, pair_out, sems, base
         self.right, self.left = (at.x + 1) % 4, (at.x + 3) % 4
         self.planes = (1 - at.zh, at.zh)
-        self.copies = []
 
     def rows(self, x, plane, half=None):
         start = (x * 2 + plane) * OWN
@@ -191,7 +191,7 @@
         return pl.ds(pl.multiple_of(start + half * (OWN // 2), OWN // 2), OWN // 2)
 
     def push(self, index, src, dst, device):
-        self.copies.append(push(src, dst, self.sems, self.base + index, device))
+        push(src, dst, self.sems, self.base + index, device)
 
     def arrived(self, index, ref):
         settle(ref, self.sems, self.base + index, self.at.row(self.at.x)).wait_recv()
@@ -237,8 +237,11 @@
         return total + self.pair_in[...].astype(F32)
 
     def drain(self):
-        for copy in self.copies:
-            copy.wait_send()
+        for index in range(9):
+            box = self.full_in.at[0, 0] if index % 4 > 1 else self.half_in.at[0, 0]
+            if index == 8:
+                box = self.pair_in
+            settle(box, self.sems, self.base + index, self.at.row(self.at.x)).wait_send()
 
 
 def scatter_scratch():
@@ -251,6 +254,90 @@
     ] + dma_sems(9)
 
 
+class PieceScatter:
+    def __init__(self, at, acc, boxes, sems, base):
+        self.at, self.acc, self.sems, self.base = at, acc, sems, base
+        self.half_in, self.full_in, self.pair_in, self.pair_out, self.pack = boxes
+        self.right, self.left = (at.y + 1) % 4, (at.y + 3) % 4
+        self.planes = (1 - at.zl, at.zl)
+
+    def push(self, index, src, dst, y, zl):
+        device = ((y * 2 + zl) * 2 + self.at.core, self.at.x, self.at.zh)
+        push(src, dst, self.sems, self.base + index, device)
+
+    def arrived(self, index, ref):
+        settle(ref, self.sems, self.base + index, self.at.row(self.at.x)).wait_recv()
+
+    def first(self):
+        far = (self.at.y + 2) % 4
+        for role, plane in enumerate(self.planes):
+            for side, y in enumerate((self.right, self.left)):
+                self.push(
+                    role * 4 + side,
+                    self.acc.at[side, :, far * 2 + plane],
+                    self.half_in.at[role, side],
+                    y,
+                    self.at.zl,
+                )
+
+    def second(self, role):
+        plane = self.planes[role]
+        for side, y in enumerate((self.right, self.left)):
+            self.arrived(role * 4 + side, self.half_in.at[role, side])
+            q = y * 2 + plane
+            for b in range(self.acc.shape[1]):
+                self.acc[side, b, q] = (
+                    self.acc[side, b, q].astype(F32) + self.half_in[role, side, b].astype(F32)
+                ).astype(BF)
+            self.push(
+                role * 4 + 2 + side,
+                self.acc.at[:, :, q],
+                self.full_in.at[role, side],
+                y,
+                self.at.zl,
+            )
+
+    def total(self, role, out, extra=None):
+        for side in range(2):
+            self.arrived(role * 4 + 2 + side, self.full_in.at[role, side])
+        q = self.at.y * 2 + self.planes[role]
+        for a in range(2):
+            for b in range(self.acc.shape[1]):
+                value = self.acc[a, b, q].astype(F32)
+                value += self.full_in[role, 0, a, b].astype(F32)
+                value += self.full_in[role, 1, a, b].astype(F32)
+                if extra is not None:
+                    value += extra[a, b].astype(F32)
+                out[a, b] = value.astype(BF)
+
+    def third(self):
+        self.total(0, self.pair_out)
+        self.push(8, self.pair_out, self.pair_in, self.at.y, 1 - self.at.zl)
+
+    def fourth(self):
+        self.arrived(8, self.pair_in)
+        self.total(1, self.pack, self.pair_in)
+
+    def drain(self):
+        for index in range(9):
+            box = self.full_in.at[0, 0] if index % 4 > 1 else self.half_in.at[0, 0]
+            if index == 8:
+                box = self.pair_in
+            settle(box, self.sems, self.base + index, self.at.row(self.at.x)).wait_send()
+
+
+def piece_scratch(blocks, rows, width):
+    vmem = pltpu.VMEM
+    return [
+        vmem((2, blocks, 8, rows, width), BF),
+        vmem((2, 2, blocks, rows, width), BF),
+        vmem((2, 2, 2, blocks, rows, width), BF),
+        vmem((2, blocks, rows, width), BF),
+        vmem((2, blocks, rows, width), BF),
+        vmem((2, blocks, rows, width), BF),
+    ]
+
+
 def row_gather(at, ref, sems, base=0):
     def whole(x, plane):
         return ref.at[pl.ds(pl.multiple_of((x * 2 + plane) * OWN, OWN), OWN)]
@@ -278,11 +365,11 @@
 def front_kernel(
     x_in, cot_in, par_in, bias_in, seg_col, seg_row, qkv_w, out_w, gu_w, down_w,
     cot_out, par_out, normed_out, qkv_out, att_out, max_out, sum_out, tab_out, own_out,
-    hidden_out, normed2_out, qkv_s_out, out_s_out, gu_s, down_s,
+    hidden_out, normed2_out, qkv_s_out, out_s_out, gu_s, down_s, norm_sib, cot_sib, att_sib,
     x_v, normed, par, proj, tables, qkv_s, out_s, normed2, rows,
     part, half_in, full_in, pair_in, pair_out, rs_send, rs_recv,
     par_send, par_recv, act_send, act_recv, a_send, a_recv, dp_send, dp_recv, core_send, core_recv,
-    local,
+    sib_send, sib_recv, local,
 ):
     at = Place()
     greet(group_others(at) + at.near_replicas())
@@ -428,6 +515,11 @@
         outgoing.append(copy)
 
     put(normed, normed_out, 7)
+    sib = (sib_send, sib_recv)
+    sib_copies = []
+    for xt in range(4):
+        cols = pl.ds(xt * 512 + pl.multiple_of((1 - core) * 256, 256), 256)
+        sib_copies.append(push(normed.at[:, cols], norm_sib.at[xt], sib, xt, at.sibling()))
     put(qkv_s, qkv_s_out, 8)
     put(x_v.at[own_rows(at)], own_out, 9)
     put(par, par_out, 10)
@@ -449,11 +541,14 @@
         between[n]()
     attend(proj, tables, seg_col, seg_row, qkv_out, att_out, max_out, sum_out, between[3:])
     put(out_s, out_s_out, 11)
+    sib_copies.append(push(cot_out, cot_sib, sib, 4, at.sibling()))
+    cols = pl.ds(pl.multiple_of((1 - core) * 128, 128), 128)
+    sib_copies.append(push(att_out.at[:, cols], att_sib, sib, 5, at.sibling()))
     put(tables, tab_out, 12)
     rs = RowScatter(at, part, half_in, full_in, pair_in, pair_out, (rs_send, rs_recv))
-    weight = out_s[...].reshape(256, D)
 
     def product(xt):
+        weight = out_s[...].reshape(256, D)
         block = pl.ds(pl.multiple_of(xt * 128, 128), 128)
         part[block, :] = jnp.dot(att_out[block, :], weight, preferred_element_type=F32).astype(BF)
 
@@ -487,6 +582,8 @@
         weights[k].drain()
     for copy in core_copies + par_copies:
         copy.wait_send()
+    for copy in sib_copies:
+        copy.wait()
     for program in (gx, gcot, gn, rs):
         program.drain()
     for copy in outgoing:
@@ -514,9 +611,12 @@
             shape((16, 16, D), BF),
             shape((2, 4, 16, 32, WIDE), BF),
             shape((16, 48, D), BF),
+            shape((4, TOK, 256), BF),
+            shape((TOK, D), BF),
+            shape((TOK, 128), BF),
         ),
         in_specs=[IN_ANY] * 3 + [IN_VMEM] * 3 + [IN_ANY] * 4,
-        out_specs=(IN_ANY,) * 3 + (IN_VMEM,) * 4 + (IN_ANY,) * 2 + (IN_VMEM,) + (IN_ANY,) * 5,
+        out_specs=(IN_ANY,) * 3 + (IN_VMEM,) * 4 + (IN_ANY,) * 2 + (IN_VMEM,) + (IN_ANY,) * 8,
         scratch_shapes=[
             vmem((TOK, D), BF),
             vmem((TOK, D), BF),
@@ -534,58 +634,15 @@
         + dma_sems(12)
         + dma_sems(36)
         + dma_sems(32)
+        + dma_sems(6)
         + [pltpu.SemaphoreType.DMA((14,))],
         compiler_params=params(1),
         name="front",
     )(x_in, cot_in, par_in, bias_in, seg_col, seg_row, qkv_w, out_w, gu_w, down_w)
 
 
-def scatter_sum(at, product, part, got, sems):
-    def step(i, carry):
-        xt = (at.x + i + 1) % 4
-        part[pl.ds(pl.multiple_of(xt * 128, 128), 128), :] = product(xt).astype(BF)
-        for half in range(2):
-            g = xt * 2 + half
-            index = (g - at.g + 15) % 8
-
-            @pl.when(index < 7)
-            def _():
-                push(
-                    part.at[pl.ds(pl.multiple_of(g * OWN, OWN), OWN)],
-                    got.at[index],
-                    sems,
-                    index,
-                    at.group(g),
-                )
-
-        return carry
-
-    lax.fori_loop(0, 4, step, 0)
-
-
 def own_rows(at):
     return pl.ds(pl.multiple_of(at.g * OWN, OWN), OWN)
-
-
-def summed(at, part, got, sems):
-    total = part[own_rows(at), :].astype(F32)
-    for k in range(7):
-        settle(got.at[k], sems, k, at.group(at.g)).wait_recv()
-        total += got[k].astype(F32)
-    return total
-
-
-def sent(at, buffer, sems, amount=7):
-    for k in range(amount):
-        settle(buffer, sems, k, at.group(at.g)).wait_send()
-
-
-def gather_rows(at, rows, full, sems, local):
-    copy = pltpu.make_async_copy(rows, full.at[own_rows(at)], local)
-    copy.start()
-    for k in range(1, 8):
-        push(rows, full.at[own_rows(at)], sems, k - 1, at.group((at.g + k) % 8))
-    copy.wait()
 
 
 def gather_columns(at, rows, full, sems, local):
@@ -619,123 +676,6 @@
     mean = jnp.mean(inner, axis=1, keepdims=True)
     along = jnp.mean(inner * scaled, axis=1, keepdims=True)
     return inverse * (inner - mean - scaled * along)
-
-
-def mlp_back_kernel(
-    grad_gate, grad_up, gu_s, hidden, down_s, hidden_in, cot_full, par,
-    grad_in_out, branch_out, act_out, sums_out,
-    part, got, rows, part2, got2, rows2,
-    rs_send, rs_recv, ag_send, ag_recv, rt_send, rt_recv, tr_send, tr_recv, local,
-):
-    at = Place()
-    greet(group_others(at))
-    rs, ag = (rs_send, rs_recv), (ag_send, ag_recv)
-    rt, tr = (rt_send, rt_recv), (tr_send, tr_recv)
-
-    def product(xt):
-        block = pl.ds(pl.multiple_of(xt * 128, 128), 128)
-        first = lax.dot_general(
-            grad_gate[block, :], gu_s[0], ROWS_BY_COLS, preferred_element_type=F32
-        )
-        return first + lax.dot_general(
-            grad_up[block, :], gu_s[1], ROWS_BY_COLS, preferred_element_type=F32
-        )
-
-    def product_two(xt):
-        block = pl.ds(pl.multiple_of(xt * 128, 128), 128)
-        return jnp.dot(hidden[block, :], down_s[...], preferred_element_type=F32)
-
-    scatter_sum(at, product, part, got, rs)
-    scaled, inverse = norm(hidden_in[...])
-    grad = summed(at, part, got, rs)
-    grad_in = cot_full[own_rows(at), :].astype(F32) + norm_back(
-        grad, scaled, inverse, par[2:3, :]
-    )
-    grad_in_out[...] = grad_in
-    rows[...] = grad_in.astype(BF)
-    gather_rows(at, rows, branch_out, ag, local.at[0])
-    sums_out[...] = jnp.zeros_like(sums_out)
-    sums_out[0:1, :] = jnp.sum(grad * scaled, axis=0, keepdims=True)
-    sums_out[1:2, :] = jnp.sum(grad, axis=0, keepdims=True)
-    scatter_sum(at, product_two, part2, got2, rt)
-    total = summed(at, part2, got2, rt) + hidden_in[...]
-    rows2[...] = total.astype(BF)
-    gather_columns(at, rows2, act_out, tr, local.at[1])
-    sent(at, got.at[0], rs)
-    sent(at, got.at[0], rt)
-    settle_all(at, rows, ag)
-    settle_all(at, rows2.at[:, pl.ds(0, 256)], tr)
-
-
-def mlp_back(grad_gate, grad_up, gu_s, hidden, down_s, hidden_in, cot_full, par):
-    shape = jax.ShapeDtypeStruct
-    return pl.pallas_call(
-        mlp_back_kernel,
-        out_shape=(
-            shape((OWN, D), F32),
-            shape((TOK, D), BF),
-            shape((TOK, 256), BF),
-            shape((8, D), F32),
-        ),
-        in_specs=[IN_VMEM] * 8,
-        out_specs=(IN_VMEM, IN_ANY, IN_ANY, IN_VMEM),
-        scratch_shapes=[
-            pltpu.VMEM((TOK, D), BF),
-            pltpu.VMEM((7, OWN, D), BF),
-            pltpu.VMEM((OWN, D), BF),
-        ]
-        * 2
-        + dma_sems(7) * 4
-        + [pltpu.SemaphoreType.DMA((2,))],
-        compiler_params=params(3),
-        name="mlp_back",
-    )(grad_gate, grad_up, gu_s, hidden, down_s, hidden_in, cot_full, par)
-
-
-def input_back_kernel(
-    grad_proj, qkv_s, x_own, grad_in, par, out, sums_out,
-    part, got, rows, rs_send, rs_recv, tr_send, tr_recv, local,
-):
-    at = Place()
-    greet(group_others(at))
-    rs, tr = (rs_send, rs_recv), (tr_send, tr_recv)
-
-    def product(xt):
-        block = pl.ds(pl.multiple_of(xt * 128, 128), 128)
-        return lax.dot_general(
-            grad_proj[block, :], qkv_s[...], ROWS_BY_COLS, preferred_element_type=F32
-        )
-
-    scatter_sum(at, product, part, got, rs)
-    scaled, inverse = norm(x_own[...].astype(F32))
-    grad = summed(at, part, got, rs)
-    total = grad_in[...] + norm_back(grad, scaled, inverse, par[0:1, :])
-    rows[...] = total.astype(BF)
-    gather_columns(at, rows, out, tr, local.at[0])
-    sums_out[...] = jnp.zeros_like(sums_out)
-    sums_out[0:1, :] = jnp.sum(grad * scaled, axis=0, keepdims=True)
-    sums_out[1:2, :] = jnp.sum(grad, axis=0, keepdims=True)
-    sent(at, got.at[0], rs)
-    settle_all(at, rows.at[:, pl.ds(0, 256)], tr)
-
-
-def input_back(grad_proj, qkv_s, x_own, grad_in, par):
-    shape = jax.ShapeDtypeStruct
-    return pl.pallas_call(
-        input_back_kernel,
-        out_shape=(shape((TOK, 256), BF), shape((8, D), F32)),
-        in_specs=[IN_VMEM] * 5,
-        out_specs=(IN_ANY, IN_VMEM),
-        scratch_shapes=[
-            pltpu.VMEM((TOK, D), BF),
-            pltpu.VMEM((7, OWN, D), BF),
-            pltpu.VMEM((OWN, D), BF),
-        ]
-        + dma_sems(7) * 2
-        + [pltpu.SemaphoreType.DMA((1,))],
-        compiler_params=params(4),
-        name="input_back",
-    )(grad_proj, qkv_s, x_own, grad_in, par)
 
 
 def rotary(value, tables, sign):
@@ -815,8 +755,8 @@
             between[block]()
 
 
-def attention_back_kernel(
-    qkv, grad_att, tables, seg_col, seg_row, maxima, totals, grad_out, bias_out, pieces
+def attend_back(
+    qkv, grad_att, tables, seg_col, seg_row, maxima, totals, grad_out, pieces, between
 ):
     scale = 1.0 / math.sqrt(HD)
     pieces[...] = jnp.zeros_like(pieces)
@@ -845,247 +785,491 @@
             pieces[head, 2, upto, :] += lax.dot_general(
                 probs.astype(BF), grad, OVER_ROWS, preferred_element_type=F32
             )
+        between[block]()
     tab = (tables[0], tables[1], tables[2])
-    bias_out[...] = jnp.zeros_like(bias_out)
+    sums = []
     for half in range(2):
         parts = [pieces[half * 2 + j // 3, j % 3] for j in range(6)]
         cols = pl.ds(half * 384, 384)
         low = rotary(jnp.concatenate(parts, axis=1), tab, -1.0).astype(BF)
         grad_out[:, cols] = low
-        bias_out[0:1, cols] = jnp.sum(low.astype(F32), axis=0, keepdims=True)
-
-
-def attention_back(qkv, grad_att, tables, seg_col, seg_row, maxima, totals):
-    shape = jax.ShapeDtypeStruct
-    return pl.pallas_call(
-        attention_back_kernel,
-        out_shape=(shape((TOK, WIDE), BF), shape((8, WIDE), F32)),
-        in_specs=[IN_VMEM] * 7,
-        out_specs=(IN_VMEM,) * 2,
-        scratch_shapes=[pltpu.VMEM((HEADS, 3, TOK, HD), F32)],
-        compiler_params=pltpu.CompilerParams(vmem_limit_bytes=VMEM_LIMIT),
-        name="attention_back",
-    )(qkv, grad_att, tables, seg_col, seg_row, maxima, totals)
-
-
-def sum_grads_kernel(
-    gu_p, qkv_p, down_p, out_p, ln_p, bias_p,
-    gu_f, qkv_f, down_f, out_f, small_f,
-    gu_a, gu_r, gu_t, gu_c, qkv_a, qkv_r, qkv_t, qkv_c,
-    down_a, down_r, down_t, down_c, out_a, out_r, out_t, out_c,
-    ln_t, small_t,
-    a_send, a_recv, b_send, b_recv, c_send, c_recv, d_send, d_recv, e_send, e_recv,
-    g_send, g_recv, h_send, h_recv, local,
+        sums.append(jnp.sum(low.astype(F32), axis=0, keepdims=True))
+    return jnp.concatenate(sums, axis=1)
+
+
+def back_kernel(
+    n2_h, gu_h, down_h, out_h, qkvs_h, cot_h, normed_h, tab_h, norm_sib_h, cot_sib_h, att_sib_h,
+    hidden_in, par, att, qkv, seg_col, seg_row, maxima, totals, x_own,
+    act_out, input_out, gu_f, qkv_f, down_f, out_f, small_f,
+    n2, n2_sib, cot, cot_sib, gb, gb_sib, att_sib,
+    hidden, hidden_sib, gg, gg_sib, gate_up_sib, grad_up, gp_sib, grad_att, grad_in,
+    out_s, rows, sums, ln_t, small_t,
+    part, part2,
+    *rest,
 ):
     at = Place()
     others = [at.replica((at.dp + k) % 16) for k in range(1, 16)]
     greet(group_others(at) + others)
-    step_a, step_b, step_c = (a_send, a_recv), (b_send, b_recv), (c_send, c_recv)
-    step_d, step_e = (d_send, d_recv), (e_send, e_recv)
-    step_g, step_h = (g_send, g_recv), (h_send, h_recv)
     core, q, x = at.core, at.q, at.x
     cq = core * 8 + q
-
-    partial = (gu_p, qkv_p, down_p, out_p)
-    accs = (gu_a, qkv_a, down_a, out_a)
-    recvs = (gu_r, qkv_r, down_r, out_r)
-    slots = (gu_t, qkv_t, down_t, out_t)
-    packs = (gu_c, qkv_c, down_c, out_c)
-    order = (0, 2, 3, 1)
-
-    def half(k, c):
-        if k == 0:
-            return gu_p.at[:, :, c]
-        if k == 1:
-            return qkv_p.at[:, c]
-        return partial[k].at[c]
-
-    def chunk(k, p):
-        if k == 0:
-            return gu_a.at[:, :, p]
-        if k == 1:
-            return qkv_a.at[:, p]
-        return accs[k].at[p]
-
-    def blocks(k):
-        if k == 0:
-            return [(a, b) for a in range(2) for b in range(4)]
-        if k == 1:
-            return [(b,) for b in range(4)]
-        return [()]
-
-    def full(lead, p):
-        return lead + (p,)
+    rest = list(rest)
+
+    def take(amount):
+        head, rest[:] = rest[:amount], rest[amount:]
+        return head
+
+    boxes = [take(4) for _ in range(2)]
+    boxes.append(boxes[0])
+    arrays = [take(6) for _ in range(4)]
+    (gu_a, qkv_a, down_a, out_a) = [a[0] for a in arrays]
+    packs = [a[5] for a in arrays]
+    rs_sems, act_sems, sib_sems = take(2), take(2), take(2)
+    dps_sems, row_sems, dpg_sems, core_sems = take(2), take(2), take(2), take(2)
+    ln_sems, small_sems = take(2), take(2)
+    (local,) = take(1)
+    finals = (gu_f, qkv_f, down_f, out_f)
+
+    loads = {}
+
+    def load(name, src, dst, index):
+        loads[name] = lambda: pltpu.make_async_copy(src, dst, local.at[index])
+        loads[name]().start()
+
+    def columns(c, xt):
+        return pl.ds(pl.multiple_of(xt * 512 + c * 256, 256), 256)
+
+    exchange = {}
+
+    def to_sibling(name, src, dst, index):
+        exchange[name] = (dst, index)
+        push(src, inbox(name), sib_sems, index, at.sibling())
+
+    def inbox(name):
+        ref = exchange[name][0]
+        return ref.at[name[1]] if isinstance(name, tuple) else ref
+
+    def exchanged(name):
+        settle(inbox(name), sib_sems, exchange[name][1], at.sibling()).wait_recv()
+
+    load("n2", n2_h, n2, 0)
+    load("cot", cot_h, cot, 1)
+    load("out_s", out_h, out_s, 2)
 
     def pack_for(k, xt):
         if k == 0:
-            return gu_c.at[:, xt]
+            return packs[0].at[:, xt]
         if k == 1:
-            return qkv_c.at[xt]
-        return packs[k].at[:, pl.ds(pl.multiple_of(xt * 512, 512), 512)]
+            return packs[1].at[xt // 2, xt % 2]
+        return packs[k].at[xt // 2, 0, :, pl.ds(pl.multiple_of((xt % 2) * 512, 512), 512)]
 
     def landing(k, xs, p):
         if k == 0:
             return gu_f.at[xs, :, p]
         if k == 1:
             return qkv_f.at[p, :, pl.ds(pl.multiple_of(xs * WIDE, WIDE), WIDE)]
-        return (gu_f, qkv_f, down_f, out_f)[k].at[xs, p]
-
-    def piece(k, p):
-        if k == 0:
-            return gu_f.at[:, :, p]
-        if k == 1:
-            return qkv_f.at[p]
-        return (gu_f, qkv_f, down_f, out_f)[k].at[:, p]
-
-    mine = pl.ds(pl.multiple_of(at.g * 256, 256), 256)
+        return finals[k].at[xs, p]
+
+    def slot(y, zl):
+        return core * 8 + y * 2 + zl
+
+    def whole(k):
+        def of(y, zl):
+            p = slot(y, zl)
+            if k == 0:
+                return gu_f.at[:, :, p]
+            if k == 1:
+                return qkv_f.at[p]
+            return finals[k].at[:, p]
+
+        return of
+
+    def half(k):
+        def of(y, zl, side):
+            p = slot(y, zl)
+            if k == 0:
+                return gu_f.at[pl.ds(side * 2, 2), :, p]
+            if k == 1:
+                return qkv_f.at[p, :, pl.ds(side * 2 * WIDE, 2 * WIDE)]
+            return finals[k].at[pl.ds(side * 2, 2), p]
+
+        return of
+
+    def share(k):
+        def on_piece(y, zl, index):
+            ref = whole(k)(y, zl)
+            push(ref, ref, core_sems, k * 8 + index, at.sibling())
+
+        return on_piece
+
+    scatters = [
+        PieceScatter(at, arrays[k][0], arrays[k][1:], dps_sems, k * 9) for k in range(4)
+    ]
+    s_gu, s_qkv, s_down, s_out = scatters
+    gathers = [
+        Gather(
+            at.y, at.zl, lambda y, zl: ((y * 2 + zl) * 2 + core, x, at.zh), whole(k), half(k),
+            dpg_sems, k * 9, share(k),
+        )
+        for k in range(4)
+    ]
+    g_gu, g_qkv, g_down, g_out = gathers
+    def send_rows(k):
+        scatters[k].fourth()
+        for j in (2, 1, 3):
+            xt = (x + j) % 4
+            push(pack_for(k, xt), landing(k, x, cq), row_sems, k * 3 + j - 1, at.row(xt))
+        pltpu.make_async_copy(pack_for(k, x), landing(k, x, cq), local.at[12 + k]).start()
+
+    def begin(k):
+        pltpu.make_async_copy(pack_for(k, x), landing(k, x, cq), local.at[12 + k]).wait()
+        for j in range(3):
+            settle(pack_for(k, x), row_sems, k * 3 + j, at.row(x)).wait_recv()
+        gathers[k].start()
+
+    rs1, rs2, rs3 = [
+        RowScatter(at, p, *boxes[j], rs_sems, j * 9) for j, p in enumerate((part, part2, part))
+    ]
+    block_of = lambda xt: pl.ds(pl.multiple_of(xt * 128, 128), 128)
+    far, right, left = (x + 2) % 4, (x + 1) % 4, (x + 3) % 4
+    g_branch = row_gather(at, gb, act_sems, 0)
+
+    def feed_forward(gu_s, down_s):
+        load("gate", gu_h.at[0], gu_s.at[0], 7)
+        load("up", gu_h.at[1], gu_s.at[1], 8)
+        load("down", down_h, down_s, 9)
+        for xt in range(4):
+            to_sibling(("n2", xt), n2_h.at[:, columns(1 - core, xt)], n2_sib, xt)
+        for name in ("n2", "gate", "up", "cot", "down"):
+            loads[name]().wait()
+        lane = lax.broadcasted_iota(jnp.int32, (1, 256), 1)
+
+        def chunk(n, carry):
+            cols = pl.ds(pl.multiple_of(n * 256, 256), 256)
+            gate = jnp.dot(n2[...], gu_s[0, :, cols], preferred_element_type=F32)
+            up = jnp.dot(n2[...], gu_s[1, :, cols], preferred_element_type=F32)
+            grad = lax.dot_general(
+                cot[...], down_s[cols, :], ROWS_BY_COLS, preferred_element_type=F32
+            )
+            kept = (lane >= 128) | (x < 2) | (n > 0)
+            sig = jax.nn.sigmoid(gate)
+            act = gate * sig
+            grad = jnp.where(kept, grad, 0.0)
+            hidden[:, cols] = jnp.where(kept, act * up, 0.0).astype(BF)
+            gg[:, cols] = (grad * up * (sig * (1.0 + gate * (1.0 - sig)))).astype(BF)
+            grad_up[:, cols] = (grad * act).astype(BF)
+            return carry
+
+        lax.fori_loop(0, 3, chunk, 0)
+        to_sibling(
+            "hidden",
+            hidden.at[:, pl.ds(pl.multiple_of((1 - core) * 384, 128), 384)],
+            hidden_sib,
+            5,
+        )
+        to_sibling("gg", gg, gg_sib, 6)
+        to_sibling("up", grad_up, gate_up_sib, 7)
+
+        def product(xt):
+            block = block_of(xt)
+            value = lax.dot_general(
+                gg[block, :], gu_s[0], ROWS_BY_COLS, preferred_element_type=F32
+            ) + lax.dot_general(
+                grad_up[block, :], gu_s[1], ROWS_BY_COLS, preferred_element_type=F32
+            )
+            part[block, :] = value.astype(BF)
+
+        product(far)
+        rs1.first()
+        product(right)
+        product(left)
+        product(x)
+
+        def product_two(i, carry):
+            block = block_of(i)
+            part2[block, :] = jnp.dot(
+                hidden[block, :], down_s[...], preferred_element_type=F32
+            ).astype(BF)
+            return carry
+
+        lax.fori_loop(0, 4, product_two, 0)
+
+    pl.run_scoped(
+        feed_forward, pltpu.VMEM((2, D, WIDE), BF), pltpu.VMEM((WIDE, D), BF)
+    )
+
+    def outer_sum(a, b, a_sib, b_sib):
+        return lax.dot_general(
+            a, b, OVER_ROWS, preferred_element_type=F32
+        ) + lax.dot_general(a_sib, b_sib, OVER_ROWS, preferred_element_type=F32)
+
+    load(("cot_sib", 0), cot_sib_h.at[:, pl.ds(0, 256)], cot_sib.at[0], 3)
+    exchanged("hidden")
+    mine = hidden[:, pl.ds(pl.multiple_of(core * 384, 128), 384)]
+    for a in range(8):
+        cols = pl.ds(a * 256, 256)
+        loads["cot_sib", a]().wait()
+        if a < 7:
+            load(("cot_sib", a + 1), cot_sib_h.at[:, pl.ds((a + 1) * 256, 256)], cot_sib.at[(a + 1) % 2], 3 if a % 2 else 18)
+        down_a[a // 4, 0, :, :, pl.ds((a % 4) * 256, 256)] = (
+            outer_sum(mine, cot[:, cols], hidden_sib[...], cot_sib[a % 2])
+            .astype(BF)
+            .reshape(8, 48, 256)
+        )
+    s_down.first()
+    rs1.second(0)
+    rs1.second(1)
+    exchanged("gg")
+    exchanged("up")
+    for xt in range(4):
+        exchanged(("n2", xt))
+
+    def gate_up_grad(xt, carry):
+        own, sib = n2[:, columns(core, xt)], n2_sib[xt]
+        gu_a[0, xt] = outer_sum(own, gg[...], sib, gg_sib[...]).astype(BF).reshape(8, 32, WIDE)
+        gu_a[1, xt] = (
+            outer_sum(own, grad_up[...], sib, gate_up_sib[...]).astype(BF).reshape(8, 32, WIDE)
+        )
+        return carry
+
+    lax.fori_loop(0, 4, gate_up_grad, 0)
+    load("nh", normed_h, n2, 4)
+    load("nh_sib", norm_sib_h, n2_sib, 5)
+    load("att_sib", att_sib_h, att_sib, 6)
+    s_gu.first()
+    s_down.second(0)
+    s_down.second(1)
+    rs1.third()
+    scaled, inverse = norm(hidden_in[...])
+    grad = rs1.fourth()
+    value = cot[own_rows(at), :].astype(F32) + norm_back(grad, scaled, inverse, par[2:3, :])
+    grad_in[...] = value
+    rows[0] = value.astype(BF)
+    gb[own_rows(at), :] = value.astype(BF)
+    g_branch.start(rows.at[0])
+    sums[...] = jnp.zeros_like(sums)
+    sums[2:3, :] = jnp.sum(grad * scaled, axis=0, keepdims=True)
+    sums[3:4, :] = jnp.sum(grad, axis=0, keepdims=True)
+    g_branch.forward_ring()
+    s_gu.second(0)
+    g_branch.spread_pair()
+    s_gu.second(1)
+    s_down.third()
+    g_branch.forward_pair()
+    send_rows(2)
+    g_branch.finish()
+    to_sibling("gb", gb, gb_sib, 13)
+
+    settle(inbox("gg"), sib_sems, exchange["gg"][1], at.sibling()).wait_send()
+    gp = gg
+
+    def attention(tables, pieces, qkv_s):
+        load("tab", tab_h, tables, 10)
+        load("qkv_s", qkvs_h, qkv_s, 11)
+        loads["out_s"]().wait()
+        grad_att[...] = lax.dot_general(
+            gb[...], out_s[...].reshape(256, D), ROWS_BY_COLS, preferred_element_type=F32
+        ).astype(BF)
+        rs2.first()
+        loads["tab"]().wait()
+
+        def after_two():
+            total = rs2.fourth() + hidden_in[...]
+            rows[1] = total.astype(BF)
+            gather_columns(at, rows.at[1], act_out, (act_sems[0].at[pl.ds(9, 7)], act_sems[1].at[pl.ds(9, 7)]), local.at[16])
+
+        between = [
+            lambda: (rs2.second(0), rs2.second(1), s_gu.third()),
+            lambda: (rs2.third(), begin(2)),
+            lambda: (send_rows(0), g_down.forward_ring(), g_down.spread_pair()),
+            lambda: (after_two(), begin(0)),
+        ]
+        bias_sums = attend_back(
+            qkv, grad_att, tables, seg_col, seg_row, maxima, totals, gp, pieces, between
+        )
+        to_sibling("gp", gp, gp_sib, 14)
+        loads["qkv_s"]().wait()
+        rs1.drain()
+
+        def product(xt):
+            block = block_of(xt)
+            weight = qkv_s[...].reshape(D, WIDE)
+            part[block, :] = lax.dot_general(
+                gp[block, :], weight, ROWS_BY_COLS, preferred_element_type=F32
+            ).astype(BF)
+
+        product(far)
+        rs3.first()
+        product(right)
+        product(left)
+        product(x)
+        sums[4:7, 0:256] = jnp.concatenate([bias_sums[:, j * 256 : (j + 1) * 256] for j in range(3)])
+
+    pl.run_scoped(
+        attention,
+        pltpu.VMEM((3, TOK, 384), F32),
+        pltpu.VMEM((HEADS, 3, TOK, HD), F32),
+        pltpu.VMEM((4, 16, 32, WIDE), BF),
+    )
+    exchanged("gb")
+    loads["att_sib"]().wait()
+    mine = att[:, pl.ds(pl.multiple_of(core * 128, 128), 128)]
+    for a in range(2):
+        cols = pl.ds(a * 1024, 1024)
+        out_a[a, 0] = (
+            outer_sum(mine, gb[:, cols], att_sib[...], gb_sib[:, cols])
+            .astype(BF)
+            .reshape(8, 16, 1024)
+        )
+    rs3.second(0)
+    rs3.second(1)
+    s_out.first()
+    exchanged("gp")
+    loads["nh"]().wait()
+    loads["nh_sib"]().wait()
+
+    def qkv_grad(xt, carry):
+        qkv_a[xt // 2, xt % 2] = (
+            outer_sum(n2[:, columns(core, xt)], gp[...], n2_sib[xt], gp_sib[...]).astype(BF).reshape(8, 32, WIDE)
+        )
+        return carry
+
+    lax.fori_loop(0, 4, qkv_grad, 0)
+    s_qkv.first()
+    rs3.third()
+    g_down.forward_pair()
+    g_gu.forward_ring()
+    s_out.second(0)
+    s_out.second(1)
+    scaled, inverse = norm(x_own[...].astype(F32))
+    grad = rs3.fourth()
+    value = grad_in[...] + norm_back(grad, scaled, inverse, par[0:1, :])
+    rows[2] = value.astype(BF)
+    gather_columns(at, rows.at[2], input_out, (act_sems[0].at[pl.ds(16, 7)], act_sems[1].at[pl.ds(16, 7)]), local.at[17])
+    sums[0:1, :] = jnp.sum(grad * scaled, axis=0, keepdims=True)
+    sums[1:2, :] = jnp.sum(grad, axis=0, keepdims=True)
+    own_columns = pl.ds(pl.multiple_of(at.g * 256, 256), 256)
+    ln_copies = []
     for j in range(1, 8):
         g = (at.g + j) % 8
-        push(
-            ln_p.at[:, pl.ds(pl.multiple_of(g * 256, 256), 256)],
-            ln_t.at[j - 1],
-            step_g,
-            j - 1,
-            at.group(g),
+        ln_copies.append(
+            push(
+                sums.at[pl.ds(0, 4), pl.ds(pl.multiple_of(g * 256, 256), 256)],
+                ln_t.at[j - 1],
+                ln_sems,
+                j - 1,
+                at.group(g),
+            )
         )
-    first = {}
-    for k in order:
-        first[k] = push(half(k, 1 - core), recvs[k], step_a, k, at.sibling())
-        copy = pltpu.make_async_copy(half(k, core), accs[k], local.at[k])
-        copy.start()
-        first[k + 4] = copy
-    total = ln_p[:, mine] + bias_p[...]
+    s_qkv.second(0)
+    s_qkv.second(1)
+    g_gu.spread_pair()
+    s_out.third()
+    s_qkv.third()
+    send_rows(3)
+    send_rows(1)
+    total = sums[0:4, own_columns]
     for j in range(7):
-        settle(ln_t.at[j], step_g, j, at.group(at.g)).wait_recv()
+        ln_copies[j].wait_recv()
         total += ln_t[j]
-    small_t[pl.ds(at.dp, 1)] = total[None]
-    for j, device in enumerate(others):
-        push(small_t.at[at.dp], small_t.at[at.dp], step_h, j, device)
-    second = {}
-    for k in order:
-        first[k].wait_recv()
-        first[k + 4].wait()
-        for lead in blocks(k):
-
-            def add(p, carry):
-                index = full(lead, p)
-                accs[k][index] = (accs[k][index].astype(F32) + recvs[k][index].astype(F32)).astype(
-                    BF
-                )
-                return carry
-
-            lax.fori_loop(0, 8, add, 0)
-        for m, device in enumerate(chip_others(at)):
-            second[k, m] = push(chunk(k, q ^ (m + 1)), slots[k].at[m], step_b, k * 7 + m, device)
-    third = {}
-    for k in order:
-        for m in range(7):
-            second[k, m].wait_recv()
-        for lead in blocks(k):
-            value = accs[k][full(lead, q)].astype(F32)
-            for m in range(7):
-                value += slots[k][(m,) + lead].astype(F32)
-            packs[k][lead + (Ellipsis,)] = value.astype(BF)
-        for j in range(1, 4):
-            xt = (x + j) % 4
-            third[k, j] = push(
-                pack_for(k, xt), landing(k, x, cq), step_c, k * 3 + j - 1, at.row(xt)
-            )
-        copy = pltpu.make_async_copy(pack_for(k, x), landing(k, x, cq), local.at[4 + k])
-        copy.start()
-        third[k, 0] = copy
-    fourth, fifth = {}, {}
-    for k in order:
-        third[k, 0].wait()
-        for j in range(1, 4):
-            third[k, j].wait_recv()
-        for m, device in enumerate(chip_others(at)):
-            fourth[k, m] = push(piece(k, cq), piece(k, cq), step_d, k * 7 + m, device)
-        fifth[k, 7] = push(piece(k, cq), piece(k, cq), step_e, k * 8 + 7, at.sibling())
-    for k in order:
-        for m in range(7):
-            fourth[k, m].wait_recv()
-            p = core * 8 + (q ^ (m + 1))
-            fifth[k, m] = push(piece(k, p), piece(k, p), step_e, k * 8 + m, at.sibling())
-    for j in range(15):
-        settle(small_t.at[0], step_h, j, at.group(at.g)).wait_recv()
+    small_t[pl.ds(at.dp, 1), 0:4] = total[None]
+    small_t[pl.ds(at.dp, 1), 4:8] = sums[4:8, 0:256][None]
+    small_copies = [
+        push(small_t.at[at.dp], small_t.at[at.dp], small_sems, j, device)
+        for j, device in enumerate(others)
+    ]
+    begin(3)
+    begin(1)
+    g_down.finish()
+    g_gu.forward_pair()
+    g_out.forward_ring()
+    g_out.spread_pair()
+    g_qkv.forward_ring()
+    g_qkv.spread_pair()
+    g_gu.finish()
+    g_out.forward_pair()
+    g_qkv.forward_pair()
+    for copy in small_copies:
+        copy.wait_recv()
     result = small_t[0]
     for j in range(1, 16):
         result += small_t[j]
     small_f[...] = result
-    for k in order:
-        first[k].wait_send()
-        for m in range(7):
-            second[k, m].wait_send()
-            fourth[k, m].wait_send()
-        for j in range(1, 4):
-            third[k, j].wait_send()
-        for m in range(8):
-            fifth[k, m].wait_send()
-            fifth[k, m].wait_recv()
-    for j in range(7):
-        settle(ln_t.at[j], step_g, j, at.group(at.g)).wait_send()
-    for j in range(15):
-        settle(small_t.at[0], step_h, j, at.group(at.g)).wait_send()
-
-
-def sum_grads(gu_p, qkv_p, down_p, out_p, ln_p, bias_p):
+    g_out.finish()
+    g_qkv.finish()
+    for k in range(4):
+        ref = whole(k)(at.y, at.zl)
+        for index in range(8):
+            settle(ref, core_sems, k * 8 + index, at.sibling()).wait_recv()
+            settle(ref, core_sems, k * 8 + index, at.sibling()).wait_send()
+        scatters[k].drain()
+        gathers[k].drain()
+        for j in range(3):
+            settle(pack_for(k, x), row_sems, k * 3 + j, at.row(x)).wait_send()
+    for copy in ln_copies + small_copies:
+        copy.wait_send()
+    for name in exchange:
+        if name == "gg":
+            continue
+        settle(inbox(name), sib_sems, exchange[name][1], at.sibling()).wait_send()
+    g_branch.drain()
+    rs2.drain()
+    rs3.drain()
+    for j in (9, 16):
+        settle_all(at, rows.at[1, :, pl.ds(0, 256)], (act_sems[0].at[pl.ds(j, 7)], act_sems[1].at[pl.ds(j, 7)]))
+
+
+def back(
+    n2, gu_s, down_s, out_s, qkv_s, cot, normed, tables, norm_sib, cot_sib, att_sib,
+    hidden_in, par, att, qkv, seg_col, seg_row, maxima, totals, x_own,
+):
     shape = jax.ShapeDtypeStruct
     vmem = pltpu.VMEM
+    wide = vmem((TOK, D), BF)
+    inner = vmem((TOK, WIDE), BF)
+    quarters = vmem((4, TOK, 256), BF)
+    box = scatter_scratch()[1:5]
     return pl.pallas_call(
-        sum_grads_kernel,
+        back_kernel,
         out_shape=(
+            shape((TOK, 256), BF),
+            shape((TOK, 256), BF),
             shape((4, 2, 16, 32, WIDE), BF),
             shape((16, 32, 4 * WIDE), BF),
             shape((4, 16, 48, 512), BF),
             shape((4, 16, 16, 512), BF),
             shape((8, 256), F32),
         ),
-        in_specs=[IN_ANY] * 4 + [IN_VMEM] * 2,
-        out_specs=(IN_ANY,) * 4 + (IN_VMEM,),
+        in_specs=[IN_ANY] * 11 + [IN_VMEM] * 9,
+        out_specs=(IN_ANY,) * 6 + (IN_VMEM,),
         scratch_shapes=[
-            vmem((2, 4, 8, 32, WIDE), BF),
-            vmem((2, 4, 8, 32, WIDE), BF),
-            vmem((7, 2, 4, 32, WIDE), BF),
-            vmem((2, 4, 32, WIDE), BF),
-            vmem((4, 8, 32, WIDE), BF),
-            vmem((4, 8, 32, WIDE), BF),
-            vmem((7, 4, 32, WIDE), BF),
-            vmem((4, 32, WIDE), BF),
-            vmem((8, 48, D), BF),
-            vmem((8, 48, D), BF),
-            vmem((7, 48, D), BF),
-            vmem((48, D), BF),
-            vmem((8, 16, D), BF),
-            vmem((8, 16, D), BF),
-            vmem((7, 16, D), BF),
-            vmem((16, D), BF),
-            vmem((7, 8, 256), F32),
-            vmem((16, 8, 256), F32),
+            wide, quarters, wide, vmem((2, TOK, 256), BF), wide, wide, vmem((TOK, 128), BF),
+            inner, vmem((TOK, 384), BF), inner, inner, inner, inner, inner,
+            vmem((TOK, 256), BF), vmem((OWN, D), F32),
+            vmem((16, 16, D), BF), vmem((3, OWN, D), BF), vmem((8, D), F32),
+            vmem((7, 4, 256), F32), vmem((16, 8, 256), F32),
+            wide, wide,
         ]
-        + dma_sems(4)
-        + dma_sems(28)
+        + box * 2
+        + piece_scratch(4, 32, WIDE)
+        + piece_scratch(2, 32, WIDE)
+        + piece_scratch(1, 48, 1024)
+        + piece_scratch(1, 16, 1024)
+        + dma_sems(27)
+        + dma_sems(23)
+        + dma_sems(15)
+        + dma_sems(36)
         + dma_sems(12)
-        + dma_sems(28)
+        + dma_sems(36)
         + dma_sems(32)
         + dma_sems(7)
         + dma_sems(15)
-        + [pltpu.SemaphoreType.DMA((8,))],
-        compiler_params=params(5),
-        name="sum_grads",
-    )(gu_p, qkv_p, down_p, out_p, ln_p, bias_p)
-
-
-def matmul(a, b):
-    return jnp.dot(a, b, preferred_element_type=F32)
-
-
-def matmul_t(a, b):
-    return lax.dot_general(a, b, ROWS_BY_COLS, preferred_element_type=F32)
-
-
-def outer(a, b):
-    return lax.dot_general(a, b, OVER_ROWS, preferred_element_type=F32).astype(BF)
+        + [pltpu.SemaphoreType.DMA((19,))],
+        compiler_params=params(2),
+        name="back",
+    )(
+        n2, gu_s, down_s, out_s, qkv_s, cot, normed, tables, norm_sib, cot_sib, att_sib,
+        hidden_in, par, att, qkv, seg_col, seg_row, maxima, totals, x_own,
+    )
 
 
 def on_device(
@@ -1099,46 +1283,14 @@
     seg_row = segments[None, :]
     (
         cot_full, par, normed, qkv, attended, maxima, totals, tables, x_own,
-        hidden_in, normed_two, qkv_s, out_s, gu_s, down_s,
+        hidden_in, normed_two, qkv_s, out_s, gu_s, down_s, norm_sib, cot_sib, att_sib,
     ) = front(
         block_in, cotangent, par, qkv_bias[None, :], seg_col, seg_row,
         qkv_weight, out_weight, gate_up, down_weight,
     )
-    qkv_s, out_s = qkv_s.reshape(D, WIDE), out_s.reshape(256, D)
-    gu_s, down_s = gu_s.reshape(2, D, WIDE), down_s.reshape(WIDE, D)
-    gate = matmul(normed_two, gu_s[0])
-    up = matmul(normed_two, gu_s[1])
-    sig = jax.nn.sigmoid(gate)
-    lane = lax.broadcasted_iota(jnp.int32, (1, WIDE), 1)
-    kept = (lane >= 128) | (lax.axis_index("row") < 2)
-    act = gate * sig
-    hidden = jnp.where(kept, act * up, 0.0).astype(BF)
-    grad_hidden = jnp.where(kept, matmul_t(cot_full, down_s), 0.0)
-    grad_gate = (grad_hidden * up * (sig * (1.0 + gate * (1.0 - sig)))).astype(BF)
-    grad_up = (grad_hidden * act).astype(BF)
-    grad_in, branch, activations, sums_two = mlp_back(
-        grad_gate, grad_up, gu_s, hidden, down_s, hidden_in, cot_full, par
-    )
-    grad_att = matmul_t(branch, out_s).astype(BF)
-    grad_proj, bias_sums = attention_back(
-        qkv, grad_att, tables, seg_col, seg_row, maxima, totals
-    )
-    input_grad, sums_one = input_back(grad_proj, qkv_s, x_own, grad_in, par)
-    gu_p = jnp.stack([outer(normed_two, grad_gate), outer(normed_two, grad_up)])
-    qkv_p = outer(normed, grad_proj)
-    down_p = outer(hidden, cot_full)
-    out_p = outer(attended, branch)
-    ln_p = jnp.concatenate([sums_one[0:2], sums_two[0:2], jnp.zeros((4, D), F32)])
-    bias_p = jnp.concatenate(
-        [jnp.zeros((4, 256), F32), bias_sums[0].reshape(3, 256), jnp.zeros((1, 256), F32)]
-    )
-    gu_f, qkv_f, down_f, out_f, small = sum_grads(
-        gu_p.reshape(2, 4, 2, 8, 32, WIDE),
-        qkv_p.reshape(4, 2, 8, 32, WIDE),
-        down_p.reshape(2, 8, 48, D),
-        out_p.reshape(2, 8, 16, D),
-        ln_p,
-        bias_p,
+    activations, input_grad, gu_f, qkv_f, down_f, out_f, small = back(
+        normed_two, gu_s.reshape(2, D, WIDE), down_s.reshape(WIDE, D), out_s, qkv_s, cot_full,
+        normed, tables, norm_sib, cot_sib, att_sib, hidden_in, par, attended, qkv, seg_col, seg_row, maxima, totals, x_own,
     )
     gu_f = gu_f.reshape(4, 2, 512, WIDE)
     gu_f = jnp.concatenate([gu_f[0], gu_f[1], gu_f[2, :, :, 128:], gu_f[3, :, :, 128:]], axis=2)

time: 533 us -> 347 us (0.65)
  Pallas kernels: 450 us -> 301 us
  matrix products: 28.1 us -> 0 us
    pallas_call x4 -> x1, Pallas kernels: 335 us -> 186 us  [back(): pl.pallas_call(back_kernel, out_shape=(shape((TOK, 256), BF), shape((TOK,...]
    dot_general x9 -> x0, matrix products: 28.1 us -> none  [the longest x5 12.5 us: outer(): lax.dot_general(a, b, OVER_ROWS, preferred_element_type=F32).astype(BF)]
    slice x4 -> x0, local copies, waits for them, and re-layouts: 6.21 us -> none  [the longest x1 3.62 us: on_device(): up = matmul(normed_two, gu_s[1])]
where the time goes in v3:
time: 347 us; the launch traced here: 344 us
  Pallas kernels  301 us (87%)
  local copies, waits for them, and re-layouts  24.3 us (7%)
  other arithmetic  17.6 us (5%)
    pallas_call x1, Pallas kernels, back(): pl.pallas_call(back_kernel, out_shape=(shape((TOK, 256), BF), shape((TOK,...  186 us
    pallas_call x1, Pallas kernels, front(): pl.pallas_call(front_kernel, out_shape=(shape((TOK, D), BF), shape((8, D)...  115 us
    convert_element_type x1, other arithmetic, on_device(): gu_grad = jnp.transpose(gu_f, (1, 0, 2)).astype(F32)  9.52 us
    unnamed x13, local copies, waits for them, and re-layouts  7.85 us

profile of v3, /device:TPU:1, one launch (start us, length us, event | category | flops | bytes accessed | tf_op | source)
XLA Modules:
  0.0 343.9 jit_solution(10256357440989386010)
XLA Ops:
  0.6 1.3 broadcast_in_dim.9.bias_in
  1.9 1.3 stack.23.par_in
  3.3 1.5 copy.29.seg_col
  4.8 5.9 %copy.40 = bf16[512,2,2816]{2,0,1:T(8,128)(2,1)} copy(bf16[512,2,2816]{2,1,0:T(2,128)(2,1)} %param.21) | data formatting | bytes 11534336 | tf_op args[9]
  10.6 115.2 %front.1 = (bf16[512,2048]{1,0:T(8,128)(2,1)}, f32[8,2048]{1,0:T(8,128)}, bf16[512,2048]{1,0:T(8,128)(2,1)}, bf16[512,768]{1,0:T(8,128)(2,1)}, bf16[512,256]{1,0...) custom-call(bf16[512,256]{1,0:T(8,128)(2,1)} %x_in.1, ...), custom_call_target="tpu_custom_call" | custom-call | tf_op jit(solution)/shard_map/front/pallas_call | solution.py:596
  125.8 185.9 %back.1 = (bf16[512,256]{1,0:T(8,128)(2,1)}, bf16[512,256]{1,0:T(8,128)(2,1)}, bf16[4,2,16,32,768]{4,3,2,1,0:T(8,128)(2,1)}, bf16[16,32,3072]{2,1,0:T(8,128)(2,1...) custom-call(bf16[512,2048]{1,0:T(8,128)(2,1)} %get-tuple-element.36.n2_h, ...), custom_call_target="tpu_custom_call" | custom-call | tf_op jit(solution)/shard_map/back/pallas_call | solution.py:1231
  311.8 0.8 slice.45
  312.6 1.4 fusion.3
  314.0 0.6 reshape.53
  314.6 1.4 slice_bitcast_fusion.1
  316.0 0.0 copy-start
  316.0 1.6 fusion.2
  317.6 1.7 bitcast_convert_fusion.1
  319.3 0.6 copy-done
  319.9 0.2 fusion.1
  320.1 2.7 copy_bitcast_fusion.1
  322.8 2.7 maximum_convert_fusion
  325.5 0.3 fusion
  325.8 1.6 copy.33
  327.5 1.6 copy.34
  329.1 9.5 %convert_bitcast_fusion = f32[512,2,2816]{2,1,0:T(2,128)} fusion(bf16[2,512,640]{2,0,1:T(2,128)(2,1)S(1)} %get-tuple-element.73, bf16[2,512,640]{2,0,1:T(2,128)(2,1)S(1)} %get-tuple-element.74, bf16[2,512,768]{2,0,1:T(2,128)(2,1)S(1)} %copy.34, bf16[2,512,768]{2,0,1:T(2,128)(2,1)S(1)} %copy.33), kind=kLoop, calls=%fused_computation | loop fusion | flops 23068672 | bytes 17301504 | tf_op jit(solution)/shard_map/convert_element_type | solution.py:1297
  338.6 3.7 %bitcast_convert_fusion = f32[512,3072]{1,0:T(8,128)} fusion(bf16[16,32,3072]{2,1,0:T(8,128)(2,1)S(1)} %copy-done.1), kind=kLoop, calls=%fused_computation.2 | loop fusion | flops 1572864 | bytes 9437184 | tf_op jit(solution)/shard_map/convert_element_type | solution.py:1307
  342.3 0.7 copy.43
  343.0 0.7 copy.44
  (9 shorter events, 0.0 us)
Async XLA Ops:
  311.8 5.8 %copy-start.2 = (bf16[4,16,16,512]{3,2,1,0:T(8,128)(2,1)S(1)}, bf16[4,16,16,512]{3,2,1,0:T(8,128)(2,1)}, u32[]{:S(2)}) copy-start(bf16[4,16,16,512]{3,2,1,0:T(8,128)(2,1)} %get-tuple-element.58) | copy-start | bytes 3145732
  316.0 3.9 %copy-start = (bf16[4,2,16,32,768]{4,3,2,1,0:T(8,128)(2,1)S(1)}, bf16[4,2,16,32,768]{4,3,2,1,0:T(8,128)(2,1)}, u32[]{:S(2)}) copy-start(bf16[4,2,16,32,768]{4,3,2,1,0:T(8,128)(2,1)} %get-tuple-element.59) | copy-start | bytes 18874372
  329.1 9.5 %copy-start.1 = (bf16[16,32,3072]{2,1,0:T(8,128)(2,1)S(1)}, bf16[16,32,3072]{2,1,0:T(8,128)(2,1)}, u32[]{:S(2)}) copy-start(bf16[16,32,3072]{2,1,0:T(8,128)(2,1)} %get-tuple-element.57) | copy-start | bytes 9437188
  338.6 3.7 %copy-start.4 = (bf16[512,256]{1,0:T(8,128)(2,1)S(1)}, bf16[512,256]{1,0:T(8,128)(2,1)}, u32[]{:S(2)}) copy-start(bf16[512,256]{1,0:T(8,128)(2,1)} %get-tuple-element.86) | copy-start | bytes 786436
  338.6 4.4 %copy-start.3 = (bf16[512,256]{1,0:T(8,128)(2,1)S(1)}, bf16[512,256]{1,0:T(8,128)(2,1)}, u32[]{:S(2)}) copy-start(bf16[512,256]{1,0:T(8,128)(2,1)} %get-tuple-element.87) | copy-start | bytes 786436

commit v4 on v3

--- a/solution.py
+++ b/solution.py
@@ -177,12 +177,70 @@
             settle(ref, self.sems, self.base + index, self.device(self.pos, self.pair)).wait_send()
 
 
+class RingGather(Gather):
+    def start(self, own=None):
+        ref = self.whole(self.pos, self.pair)
+        self.push(1, ref, self.device(self.right, self.pair), own)
+        self.push(2, ref, self.device(self.left, self.pair), own)
+        self.push(0, ref, self.device(self.pos, 1 - self.pair), own)
+        self.on_piece(self.pos, self.pair, 0)
+
+    def forward_ring(self):
+        mate = self.device(self.pos, 1 - self.pair)
+        self.arrived(1, self.whole(self.left, self.pair))
+        self.push(3, self.half(self.left, self.pair, 0), self.device(self.right, self.pair))
+        self.push(5, self.whole(self.left, self.pair), mate)
+        self.on_piece(self.left, self.pair, 1)
+        self.arrived(2, self.whole(self.right, self.pair))
+        self.push(4, self.half(self.right, self.pair, 1), self.device(self.left, self.pair))
+        self.push(6, self.whole(self.right, self.pair), mate)
+        self.on_piece(self.right, self.pair, 2)
+
+    def spread_far(self):
+        self.arrived(3, self.half(self.far, self.pair, 0))
+        self.arrived(4, self.half(self.far, self.pair, 1))
+        ref = self.whole(self.far, self.pair)
+        self.push(7, ref, self.device(self.pos, 1 - self.pair))
+        self.on_piece(self.far, self.pair, 3)
+
+    def finish(self):
+        pieces = ((0, self.pos), (5, self.left), (6, self.right), (7, self.far))
+        for slot, (index, r) in enumerate(pieces):
+            self.arrived(index, self.whole(r, 1 - self.pair))
+            self.on_piece(r, 1 - self.pair, 4 + slot)
+
+    def drain(self):
+        for index in range(8):
+            ref = self.whole(self.pos, self.pair)
+            if index in (3, 4):
+                ref = self.half(self.pos, self.pair, 0)
+            settle(ref, self.sems, self.base + index, self.device(self.pos, self.pair)).wait_send()
+
+
+class MixedGather(RingGather):
+    def forward_ring(self):
+        self.arrived(1, self.whole(self.left, self.pair))
+        self.push(3, self.half(self.left, self.pair, 0), self.device(self.right, self.pair))
+        self.arrived(2, self.whole(self.right, self.pair))
+        self.push(4, self.half(self.right, self.pair, 1), self.device(self.left, self.pair))
+
+    def spread_pair(self):
+        ref = self.whole(self.pos, 1 - self.pair)
+        self.arrived(0, ref)
+        self.push(5, ref, self.device(self.right, self.pair))
+        self.push(6, ref, self.device(self.left, self.pair))
+
+    def finish(self):
+        for index, r in ((5, self.left), (6, self.right), (7, self.far)):
+            self.arrived(index, self.whole(r, 1 - self.pair))
+
+
 class RowScatter:
-    def __init__(self, at, part, half_in, full_in, pair_in, pair_out, sems, base=0):
-        self.at, self.part, self.half_in, self.full_in = at, part, half_in, full_in
-        self.pair_in, self.pair_out, self.sems, self.base = pair_in, pair_out, sems, base
-        self.right, self.left = (at.x + 1) % 4, (at.x + 3) % 4
-        self.planes = (1 - at.zh, at.zh)
+    def __init__(self, at, part, far_in, other_in, half_in, full_in, pair_in, pair_out, sems, base=0):
+        self.at, self.part, self.sems, self.base = at, part, sems, base
+        self.far_in, self.other_in, self.half_in, self.full_in = far_in, other_in, half_in, full_in
+        self.pair_in, self.pair_out = pair_in, pair_out
+        self.right, self.left, self.far = (at.x + 1) % 4, (at.x + 3) % 4, (at.x + 2) % 4
 
     def rows(self, x, plane, half=None):
         start = (x * 2 + plane) * OWN
@@ -196,61 +254,67 @@
     def arrived(self, index, ref):
         settle(ref, self.sems, self.base + index, self.at.row(self.at.x)).wait_recv()
 
+    def add(self, rows, box):
+        self.part[rows, :] = (self.part[rows, :].astype(F32) + box[...].astype(F32)).astype(BF)
+
+    def zero(self):
+        other = 1 - self.at.zh
+        self.push(0, self.part.at[self.rows(self.far, other)], self.far_in, self.at.mate())
+
+    def sides(self):
+        other = 1 - self.at.zh
+        for side, x in enumerate((self.right, self.left)):
+            src = self.part.at[self.rows(x, other)]
+            self.push(1 + side, src, self.other_in.at[side], self.at.row(x))
+
     def first(self):
-        far = (self.at.x + 2) % 4
-        for role, plane in enumerate(self.planes):
-            for side, x in enumerate((self.right, self.left)):
-                self.push(
-                    role * 4 + side,
-                    self.part.at[self.rows(far, plane, side)],
-                    self.half_in.at[role, side],
-                    self.at.row(x),
-                )
-
-    def second(self, role):
-        plane = self.planes[role]
+        plane = self.at.zh
+        self.arrived(0, self.far_in)
+        self.add(self.rows(self.far, plane), self.far_in)
         for side, x in enumerate((self.right, self.left)):
-            box = self.half_in.at[role, side]
-            self.arrived(role * 4 + side, box)
-            rows = self.rows(x, plane, side)
-            self.part[rows, :] = (self.part[rows, :].astype(F32) + box[...].astype(F32)).astype(BF)
-            self.push(
-                role * 4 + 2 + side,
-                self.part.at[self.rows(x, plane)],
-                self.full_in.at[role, side],
-                self.at.row(x),
-            )
-
-    def own(self, role):
+            src = self.part.at[self.rows(self.far, plane, side)]
+            self.push(3 + side, src, self.half_in.at[side], self.at.row(x))
+
+    def second(self):
+        plane = self.at.zh
+        for side, x in enumerate((self.right, self.left)):
+            box = self.half_in.at[side]
+            self.arrived(3 + side, box)
+            self.add(self.rows(x, plane, side), box)
+            src = self.part.at[self.rows(x, plane)]
+            self.push(5 + side, src, self.full_in.at[side], self.at.row(x))
+
+    def own(self, plane, boxes, index):
         for side in range(2):
-            self.arrived(role * 4 + 2 + side, self.full_in.at[role, side])
-        total = self.part[self.rows(self.at.x, self.planes[role]), :].astype(F32)
-        return total + self.full_in[role, 0].astype(F32) + self.full_in[role, 1].astype(F32)
+            self.arrived(index + side, boxes.at[side])
+        total = self.part[self.rows(self.at.x, plane), :].astype(F32)
+        return total + boxes[0].astype(F32) + boxes[1].astype(F32)
 
     def third(self):
-        self.pair_out[...] = self.own(0).astype(BF)
-        self.push(8, self.pair_out, self.pair_in, self.at.mate())
+        self.pair_out[...] = self.own(1 - self.at.zh, self.other_in, 1).astype(BF)
+        self.push(7, self.pair_out, self.pair_in, self.at.mate())
 
     def fourth(self):
-        total = self.own(1)
-        self.arrived(8, self.pair_in)
+        total = self.own(self.at.zh, self.full_in, 5)
+        self.arrived(7, self.pair_in)
         return total + self.pair_in[...].astype(F32)
 
     def drain(self):
-        for index in range(9):
-            box = self.full_in.at[0, 0] if index % 4 > 1 else self.half_in.at[0, 0]
-            if index == 8:
-                box = self.pair_in
+        for index in range(8):
+            box = self.half_in.at[0] if index in (3, 4) else self.pair_in
             settle(box, self.sems, self.base + index, self.at.row(self.at.x)).wait_send()
 
 
 def scatter_scratch():
+    vmem = pltpu.VMEM
     return [
-        pltpu.VMEM((TOK, D), BF),
-        pltpu.VMEM((2, 2, OWN // 2, D), BF),
-        pltpu.VMEM((2, 2, OWN, D), BF),
-        pltpu.VMEM((OWN, D), BF),
-        pltpu.VMEM((OWN, D), BF),
+        vmem((TOK, D), BF),
+        vmem((OWN, D), BF),
+        vmem((2, OWN, D), BF),
+        vmem((2, OWN // 2, D), BF),
+        vmem((2, OWN, D), BF),
+        vmem((OWN, D), BF),
+        vmem((OWN, D), BF),
     ] + dma_sems(9)
 
 
@@ -338,7 +402,7 @@
     ]
 
 
-def row_gather(at, ref, sems, base=0):
+def row_gather(at, ref, sems, base=0, kind=MixedGather):
     def whole(x, plane):
         return ref.at[pl.ds(pl.multiple_of((x * 2 + plane) * OWN, OWN), OWN)]
 
@@ -346,10 +410,10 @@
         start = (x * 2 + plane) * OWN + side * (OWN // 2)
         return ref.at[pl.ds(pl.multiple_of(start, OWN // 2), OWN // 2)]
 
-    return Gather(at.x, at.zh, lambda x, plane: (at.dp, x, plane), whole, half, sems, base)
-
-
-def column_gather(at, ref, sems, base=0):
+    return kind(at.x, at.zh, lambda x, plane: (at.dp, x, plane), whole, half, sems, base)
+
+
+def column_gather(at, ref, sems, base=0, kind=MixedGather):
     def columns(x, plane):
         return pl.ds(pl.multiple_of((x * 2 + plane) * 256, 256), 256)
 
@@ -359,21 +423,27 @@
     def half(x, plane, side):
         return ref.at[pl.ds(side * 256, 256), columns(x, plane)]
 
-    return Gather(at.x, at.zh, lambda x, plane: (at.dp, x, plane), whole, half, sems, base)
+    return kind(at.x, at.zh, lambda x, plane: (at.dp, x, plane), whole, half, sems, base)
 
 
 def front_kernel(
-    x_in, cot_in, par_in, bias_in, seg_col, seg_row, qkv_w, out_w, gu_w, down_w,
+    x_in, cot_in, gain1, shift1, gain2, shift2, bias, seg, qkv_w, out_w, gu_w, down_w,
     cot_out, par_out, normed_out, qkv_out, att_out, max_out, sum_out, tab_out, own_out,
-    hidden_out, normed2_out, qkv_s_out, out_s_out, gu_s, down_s, norm_sib, cot_sib, att_sib,
-    x_v, normed, par, proj, tables, qkv_s, out_s, normed2, rows,
-    part, half_in, full_in, pair_in, pair_out, rs_send, rs_recv,
+    seg_col, seg_row, grad_hidden,
+    hidden_out, normed2_out, qkv_s_out, out_s_out, gu_s, down_s_out, norm_sib, cot_sib, att_sib,
+    x_v, normed, par, par_in, proj, tables, qkv_s, out_s, down_s, cot, normed2, rows, raw, split,
+    part, far_in, other_in, half_in, full_in, pair_in, pair_out, rs_send, rs_recv,
     par_send, par_recv, act_send, act_recv, a_send, a_recv, dp_send, dp_recv, core_send, core_recv,
     sib_send, sib_recv, local,
 ):
     at = Place()
+    dp, x, core = at.dp, at.x, at.core
+    raw_copy = pltpu.make_async_copy(gu_w.at[pl.ds(dp * 32, 32)], raw, local.at[13])
+    raw_copy.start()
+    par_in[...] = jnp.zeros_like(par_in)
+    for j, vector in enumerate((gain1, shift1, gain2, shift2)):
+        par_in[j : j + 1, :] = vector[...].reshape(1, 256)
     greet(group_others(at) + at.near_replicas())
-    dp, x, core = at.dp, at.x, at.core
     act, step_a, step_dp = (act_send, act_recv), (a_send, a_recv), (dp_send, dp_recv)
     step_core, step_par = (core_send, core_recv), (par_send, par_recv)
     slabs = (qkv_s, out_s, gu_s, down_s)
@@ -385,7 +455,7 @@
             return out_w.at[pl.ds(xt * 256 + dp * 16, 16), :]
         start = pl.multiple_of(tile_start(xt) * 128, 128)
         if k == 2:
-            return gu_w.at[:, pl.ds(dp * 32, 32), pl.ds(start, WIDE)]
+            return split.at[:, :, pl.ds(start, WIDE)]
         return down_w.at[pl.ds(start + dp * 48, 48), :]
 
     def landing(k, xs, p):
@@ -470,28 +540,32 @@
     own = [
         pltpu.make_async_copy(x_in, x_v.at[:, slot], local.at[4]),
         pltpu.make_async_copy(par_in, par.at[:, slot], local.at[5]),
-        pltpu.make_async_copy(cot_in, cot_out.at[:, slot], local.at[6]),
+        pltpu.make_async_copy(cot_in, cot.at[:, slot], local.at[6]),
     ]
     for copy in own:
         copy.start()
-    send_rows(1)
-    send_rows(2)
-    send_rows(3)
+    line = seg[...].reshape(1, TOK).astype(F32)
+    seg_row[...] = jnp.broadcast_to(line, (8, TOK))
+    seg_col[...] = jnp.transpose(jnp.broadcast_to(line, (128, TOK)))
     begin(0)
     make_tables(seg_col, seg_row, tables)
+    raw_copy.wait()
+    both = raw[...]
+    split[0] = both[:, 0, :]
+    split[1] = both[:, 1, :]
     gx.forward_ring()
     gx.spread_pair()
     w_qkv.forward_ring()
     w_qkv.spread_pair()
+    send_rows(1)
+    gx.spread_far()
+    w_qkv.forward_pair()
     begin(1)
-    gx.forward_pair()
-    w_qkv.forward_pair()
-    w_out.forward_ring()
-    w_out.spread_pair()
     gx.finish()
-    gcot = column_gather(at, cot_out, act, 9)
+    gcot = column_gather(at, cot, act, 9)
     gcot.start(cot_in)
-    begin(2)
+    send_rows(3)
+    send_rows(2)
     for copy in own:
         copy.wait()
     for copy in par_copies:
@@ -505,7 +579,8 @@
 
     lax.fori_loop(0, TOK // 32, norm_rows, 0)
     w_qkv.finish()
-    w_out.forward_pair()
+    w_out.forward_ring()
+    w_out.spread_pair()
     from_sibling(0)
     outgoing = []
 
@@ -514,38 +589,34 @@
         copy.start()
         outgoing.append(copy)
 
+    for n in range(3):
+        cols = pl.ds(n * 256, 256)
+        weight = qkv_s[:, :, :, cols].reshape(D, 256)
+        proj[:, cols] = jnp.dot(normed[...], weight, preferred_element_type=F32) + bias[
+            cols
+        ].reshape(1, 256)
     put(normed, normed_out, 7)
+    put(qkv_s, qkv_s_out, 8)
+    put(x_v.at[own_rows(at)], own_out, 9)
+    put(par, par_out, 10)
     sib = (sib_send, sib_recv)
     sib_copies = []
     for xt in range(4):
         cols = pl.ds(xt * 512 + pl.multiple_of((1 - core) * 256, 256), 256)
         sib_copies.append(push(normed.at[:, cols], norm_sib.at[xt], sib, xt, at.sibling()))
-    put(qkv_s, qkv_s_out, 8)
-    put(x_v.at[own_rows(at)], own_out, 9)
-    put(par, par_out, 10)
     between = [
-        lambda: (gcot.forward_ring(), w_out.finish()),
-        lambda: (gcot.spread_pair(), w_gu.forward_ring(), w_gu.spread_pair()),
+        lambda: (w_out.forward_pair(), gcot.forward_ring(), gcot.spread_pair()),
         lambda: (begin(3),),
-        lambda: (gcot.forward_pair(), w_gu.forward_pair()),
-        lambda: (w_down.forward_ring(), w_down.spread_pair()),
-        lambda: (gcot.finish(), w_gu.finish()),
-        lambda: (from_sibling(1),),
+        lambda: (w_out.finish(),),
+        lambda: (gcot.spread_far(),),
     ]
-    for n in range(3):
-        cols = pl.ds(n * 256, 256)
-        weight = qkv_s[:, :, :, cols].reshape(D, 256)
-        proj[:, cols] = (
-            jnp.dot(normed[...], weight, preferred_element_type=F32) + bias_in[:, cols]
-        )
-        between[n]()
-    attend(proj, tables, seg_col, seg_row, qkv_out, att_out, max_out, sum_out, between[3:])
+    attend(proj, tables, seg_col, seg_row, qkv_out, att_out, max_out, sum_out, between)
+    from_sibling(1)
     put(out_s, out_s_out, 11)
-    sib_copies.append(push(cot_out, cot_sib, sib, 4, at.sibling()))
-    cols = pl.ds(pl.multiple_of((1 - core) * 128, 128), 128)
-    sib_copies.append(push(att_out.at[:, cols], att_sib, sib, 5, at.sibling()))
     put(tables, tab_out, 12)
-    rs = RowScatter(at, part, half_in, full_in, pair_in, pair_out, (rs_send, rs_recv))
+    rs = RowScatter(
+        at, part, far_in, other_in, half_in, full_in, pair_in, pair_out, (rs_send, rs_recv)
+    )
 
     def product(xt):
         weight = out_s[...].reshape(256, D)
@@ -553,14 +624,24 @@
         part[block, :] = jnp.dot(att_out[block, :], weight, preferred_element_type=F32).astype(BF)
 
     product((x + 2) % 4)
-    rs.first()
+    rs.zero()
     product((x + 1) % 4)
     product((x + 3) % 4)
-    rs.second(0)
-    rs.second(1)
+    rs.sides()
     product(x)
-    w_down.forward_pair()
+    begin(2)
+    w_down.forward_ring()
+    rs.first()
+    w_down.spread_pair()
     rs.third()
+    rs.second()
+    w_gu.forward_ring()
+    w_gu.spread_pair()
+    gcot.finish()
+    put(cot, cot_out, 14)
+    sib_copies.append(push(cot, cot_sib, sib, 4, at.sibling()))
+    cols = pl.ds(pl.multiple_of((1 - core) * 128, 128), 128)
+    sib_copies.append(push(att_out.at[:, cols], att_sib, sib, 5, at.sibling()))
     hidden_in = rs.fourth() + x_v[own_rows(at), :].astype(F32)
     hidden_out[...] = hidden_in
     scaled, _ = norm(hidden_in)
@@ -568,14 +649,23 @@
     normed2[own_rows(at), :] = rows[...]
     gn = row_gather(at, normed2, act, 18)
     gn.start(rows)
-    w_down.finish()
+    w_down.forward_pair()
     gn.forward_ring()
     gn.spread_pair()
-    gn.forward_pair()
+    w_gu.forward_pair()
+    w_down.finish()
+    from_sibling(3)
+    put(down_s, down_s_out, 15)
+    for n in range(3):
+        weight = down_s[...].reshape(WIDE, D)[n * 256 : (n + 1) * 256]
+        grad_hidden[:, pl.ds(n * 256, 256)] = lax.dot_general(
+            cot[...], weight, ROWS_BY_COLS, preferred_element_type=F32
+        ).astype(BF)
+    gn.spread_far()
+    w_gu.finish()
     from_sibling(2)
-    from_sibling(3)
     gn.finish()
-    put(normed2, normed2_out, 13)
+    put(normed2, normed2_out, 16)
     for k in range(4):
         for j in range(1, 4):
             first[k, j].wait_send()
@@ -590,7 +680,7 @@
         copy.wait()
 
 
-def front(x_in, cot_in, par_in, bias_in, seg_col, seg_row, qkv_w, out_w, gu_w, down_w):
+def front(*operands):
     shape = jax.ShapeDtypeStruct
     vmem = pltpu.VMEM
     return pl.pallas_call(
@@ -605,6 +695,9 @@
             shape((TOK, 128), F32),
             shape((3, TOK, 384), F32),
             shape((OWN, D), BF),
+            shape((TOK, 128), F32),
+            shape((8, TOK), F32),
+            shape((TOK, WIDE), BF),
             shape((OWN, D), F32),
             shape((TOK, D), BF),
             shape((4, 16, 32, WIDE), BF),
@@ -615,18 +708,27 @@
             shape((TOK, D), BF),
             shape((TOK, 128), BF),
         ),
-        in_specs=[IN_ANY] * 3 + [IN_VMEM] * 3 + [IN_ANY] * 4,
-        out_specs=(IN_ANY,) * 3 + (IN_VMEM,) * 4 + (IN_ANY,) * 2 + (IN_VMEM,) + (IN_ANY,) * 8,
+        in_specs=[IN_ANY] * 2 + [IN_VMEM] * 6 + [IN_ANY] * 4,
+        out_specs=(IN_ANY,) * 3
+        + (IN_VMEM,) * 4
+        + (IN_ANY,) * 2
+        + (IN_VMEM,) * 4
+        + (IN_ANY,) * 8,
         scratch_shapes=[
             vmem((TOK, D), BF),
             vmem((TOK, D), BF),
             vmem((8, D), F32),
+            vmem((8, 256), F32),
             vmem((TOK, WIDE), F32),
             vmem((3, TOK, 384), F32),
             vmem((4, 16, 32, WIDE), BF),
             vmem((16, 16, D), BF),
+            vmem((16, 48, D), BF),
+            vmem((TOK, D), BF),
             vmem((TOK, D), BF),
             vmem((OWN, D), BF),
+            vmem((32, 2, 2816), BF),
+            vmem((2, 32, 2816), BF),
         ]
         + scatter_scratch()
         + dma_sems(7)
@@ -635,31 +737,31 @@
         + dma_sems(36)
         + dma_sems(32)
         + dma_sems(6)
-        + [pltpu.SemaphoreType.DMA((14,))],
+        + [pltpu.SemaphoreType.DMA((17,))],
         compiler_params=params(1),
         name="front",
-    )(x_in, cot_in, par_in, bias_in, seg_col, seg_row, qkv_w, out_w, gu_w, down_w)
+    )(*operands)
 
 
 def own_rows(at):
     return pl.ds(pl.multiple_of(at.g * OWN, OWN), OWN)
 
 
-def gather_columns(at, rows, full, sems, local):
-    def columns(g):
-        return rows.at[:, pl.ds(pl.multiple_of(g * 256, 256), 256)]
-
-    copy = pltpu.make_async_copy(columns(at.g), full.at[own_rows(at)], local)
-    copy.start()
+def columns_of(rows, g):
+    return rows.at[:, pl.ds(pl.multiple_of(g * 256, 256), 256)]
+
+
+def start_columns(at, rows, full, sems, base, local):
+    pltpu.make_async_copy(columns_of(rows, at.g), full.at[own_rows(at)], local).start()
     for k in range(1, 8):
         g = (at.g + k) % 8
-        push(columns(g), full.at[own_rows(at)], sems, k - 1, at.group(g))
-    copy.wait()
-
-
-def settle_all(at, piece, sems, amount=7):
-    for k in range(amount):
-        copy = settle(piece, sems, k, at.group(at.g))
+        push(columns_of(rows, g), full.at[own_rows(at)], sems, base + k - 1, at.group(g))
+
+
+def finish_columns(at, rows, full, sems, base, local):
+    pltpu.make_async_copy(columns_of(rows, at.g), full.at[own_rows(at)], local).wait()
+    for k in range(7):
+        copy = settle(columns_of(rows, at.g), sems, base + k, at.group(at.g))
         copy.wait_send()
         copy.wait_recv()
 
@@ -692,7 +794,7 @@
     for block in range(4):
         rows = pl.ds(block * 128, 128)
         places = lax.broadcasted_iota(jnp.int32, (128, 128), 0) + block * 128
-        before = jnp.where(seg_row[0:1, :] < seg_col[rows, :], 1.0, 0.0)
+        before = jnp.where(seg_row[0:1, :] < seg_col[rows, 0:1], 1.0, 0.0)
         starts = jnp.sum(before, axis=1, keepdims=True)
         offsets = places.astype(F32) - starts
         lane = lax.broadcasted_iota(jnp.int32, (128, 128), 1)
@@ -719,7 +821,7 @@
     start = block * 128
     rows = lax.broadcasted_iota(jnp.int32, (128, keys), 0) + start
     cols = lax.broadcasted_iota(jnp.int32, (128, keys), 1)
-    same = seg_col[start : start + 128, :] == seg_row[0:1, :keys]
+    same = seg_col[start : start + 128, 0:1] == seg_row[0:1, :keys]
     return (cols <= rows) & same
 
 
@@ -799,7 +901,7 @@
 
 def back_kernel(
     n2_h, gu_h, down_h, out_h, qkvs_h, cot_h, normed_h, tab_h, norm_sib_h, cot_sib_h, att_sib_h,
-    hidden_in, par, att, qkv, seg_col, seg_row, maxima, totals, x_own,
+    hidden_in, par, att, qkv, seg_col, seg_row, maxima, totals, x_own, grad_hidden,
     act_out, input_out, gu_f, qkv_f, down_f, out_f, small_f,
     n2, n2_sib, cot, cot_sib, gb, gb_sib, att_sib,
     hidden, hidden_sib, gg, gg_sib, gate_up_sib, grad_up, gp_sib, grad_att, grad_in,
@@ -809,7 +911,6 @@
 ):
     at = Place()
     others = [at.replica((at.dp + k) % 16) for k in range(1, 16)]
-    greet(group_others(at) + others)
     core, q, x = at.core, at.q, at.x
     cq = core * 8 + q
     rest = list(rest)
@@ -818,11 +919,11 @@
         head, rest[:] = rest[:amount], rest[amount:]
         return head
 
-    boxes = [take(4) for _ in range(2)]
+    boxes = [take(6) for _ in range(2)]
     boxes.append(boxes[0])
     arrays = [take(6) for _ in range(4)]
     (gu_a, qkv_a, down_a, out_a) = [a[0] for a in arrays]
-    packs = [a[5] for a in arrays]
+    packs = [a[-1] for a in arrays]
     rs_sems, act_sems, sib_sems = take(2), take(2), take(2)
     dps_sems, row_sems, dpg_sems, core_sems = take(2), take(2), take(2), take(2)
     ln_sems, small_sems = take(2), take(2)
@@ -851,10 +952,11 @@
     def exchanged(name):
         settle(inbox(name), sib_sems, exchange[name][1], at.sibling()).wait_recv()
 
+    def load_cot_sib(a):
+        cols = pl.ds(a * 512, 512)
+        load(("cot_sib", a), cot_sib_h.at[:, cols], cot_sib.at[a % 2], 3 if a % 2 else 18)
+
     load("n2", n2_h, n2, 0)
-    load("cot", cot_h, cot, 1)
-    load("out_s", out_h, out_s, 2)
-
     def pack_for(k, xt):
         if k == 0:
             return packs[0].at[:, xt]
@@ -906,7 +1008,7 @@
     ]
     s_gu, s_qkv, s_down, s_out = scatters
     gathers = [
-        Gather(
+        (RingGather if k == 2 else Gather)(
             at.y, at.zl, lambda y, zl: ((y * 2 + zl) * 2 + core, x, at.zh), whole(k), half(k),
             dpg_sems, k * 9, share(k),
         )
@@ -933,33 +1035,56 @@
     far, right, left = (x + 2) % 4, (x + 1) % 4, (x + 3) % 4
     g_branch = row_gather(at, gb, act_sems, 0)
 
-    def feed_forward(gu_s, down_s):
+    def outer_sum(a, b, a_sib, b_sib):
+        return lax.dot_general(
+            a, b, OVER_ROWS, preferred_element_type=F32
+        ) + lax.dot_general(a_sib, b_sib, OVER_ROWS, preferred_element_type=F32)
+
+    def down_grad(a):
+        cols = pl.ds(a * 512, 512)
+        mine = hidden[:, pl.ds(pl.multiple_of(core * 384, 128), 384)]
+        loads["cot_sib", a]().wait()
+        down_a[a // 2, 0, :, :, pl.ds((a % 2) * 512, 512)] = (
+            outer_sum(mine, cot[:, cols], hidden_sib[...], cot_sib[a % 2])
+            .astype(BF)
+            .reshape(8, 48, 512)
+        )
+        if a < 2:
+            load_cot_sib(a + 2)
+
+    def feed_forward(gu_s, gate_v, up_v):
         load("gate", gu_h.at[0], gu_s.at[0], 7)
         load("up", gu_h.at[1], gu_s.at[1], 8)
-        load("down", down_h, down_s, 9)
+        load("cot", cot_h, cot, 1)
+        load("out_s", out_h, out_s, 2)
+        greet(group_others(at) + others)
         for xt in range(4):
             to_sibling(("n2", xt), n2_h.at[:, columns(1 - core, xt)], n2_sib, xt)
-        for name in ("n2", "gate", "up", "cot", "down"):
+        for name in ("n2", "gate", "up"):
             loads[name]().wait()
         lane = lax.broadcasted_iota(jnp.int32, (1, 256), 1)
 
-        def chunk(n, carry):
-            cols = pl.ds(pl.multiple_of(n * 256, 256), 256)
-            gate = jnp.dot(n2[...], gu_s[0, :, cols], preferred_element_type=F32)
-            up = jnp.dot(n2[...], gu_s[1, :, cols], preferred_element_type=F32)
-            grad = lax.dot_general(
-                cot[...], down_s[cols, :], ROWS_BY_COLS, preferred_element_type=F32
-            )
-            kept = (lane >= 128) | (x < 2) | (n > 0)
-            sig = jax.nn.sigmoid(gate)
-            act = gate * sig
-            grad = jnp.where(kept, grad, 0.0)
-            hidden[:, cols] = jnp.where(kept, act * up, 0.0).astype(BF)
-            gg[:, cols] = (grad * up * (sig * (1.0 + gate * (1.0 - sig)))).astype(BF)
-            grad_up[:, cols] = (grad * act).astype(BF)
-            return carry
-
-        lax.fori_loop(0, 3, chunk, 0)
+        def chunk(n):
+            cols = pl.ds(n * 256, 256)
+            gate_v[...] = jnp.dot(n2[...], gu_s[0, :, cols], preferred_element_type=F32)
+            up_v[...] = jnp.dot(n2[...], gu_s[1, :, cols], preferred_element_type=F32)
+            kept = (lane >= (128 if n == 0 else 0)) | (x < 2)
+
+            def gated(i, carry):
+                block = pl.ds(pl.multiple_of(i * 64, 64), 64)
+                gate, up = gate_v[block, :], up_v[block, :]
+                sig = jax.nn.sigmoid(gate)
+                act = gate * sig
+                grad = jnp.where(kept, grad_hidden[block, cols].astype(F32), 0.0)
+                hidden[block, cols] = jnp.where(kept, act * up, 0.0).astype(BF)
+                gg[block, cols] = (grad * up * (sig * (1.0 + gate * (1.0 - sig)))).astype(BF)
+                grad_up[block, cols] = (grad * act).astype(BF)
+                return carry
+
+            lax.fori_loop(0, 8, gated, 0)
+
+        for n in range(3):
+            chunk(n)
         to_sibling(
             "hidden",
             hidden.at[:, pl.ds(pl.multiple_of((1 - core) * 384, 128), 384)],
@@ -979,10 +1104,16 @@
             part[block, :] = value.astype(BF)
 
         product(far)
-        rs1.first()
+        rs1.zero()
         product(right)
         product(left)
+        rs1.sides()
+        rs1.first()
         product(x)
+
+    def down_product(down_s):
+        load("down", down_h, down_s, 9)
+        loads["down"]().wait()
 
         def product_two(i, carry):
             block = block_of(i)
@@ -993,31 +1124,14 @@
 
         lax.fori_loop(0, 4, product_two, 0)
 
+    load_cot_sib(0)
+    load_cot_sib(1)
     pl.run_scoped(
-        feed_forward, pltpu.VMEM((2, D, WIDE), BF), pltpu.VMEM((WIDE, D), BF)
+        feed_forward,
+        pltpu.VMEM((2, D, WIDE), BF),
+        pltpu.VMEM((TOK, 256), F32),
+        pltpu.VMEM((TOK, 256), F32),
     )
-
-    def outer_sum(a, b, a_sib, b_sib):
-        return lax.dot_general(
-            a, b, OVER_ROWS, preferred_element_type=F32
-        ) + lax.dot_general(a_sib, b_sib, OVER_ROWS, preferred_element_type=F32)
-
-    load(("cot_sib", 0), cot_sib_h.at[:, pl.ds(0, 256)], cot_sib.at[0], 3)
-    exchanged("hidden")
-    mine = hidden[:, pl.ds(pl.multiple_of(core * 384, 128), 384)]
-    for a in range(8):
-        cols = pl.ds(a * 256, 256)
-        loads["cot_sib", a]().wait()
-        if a < 7:
-            load(("cot_sib", a + 1), cot_sib_h.at[:, pl.ds((a + 1) * 256, 256)], cot_sib.at[(a + 1) % 2], 3 if a % 2 else 18)
-        down_a[a // 4, 0, :, :, pl.ds((a % 4) * 256, 256)] = (
-            outer_sum(mine, cot[:, cols], hidden_sib[...], cot_sib[a % 2])
-            .astype(BF)
-            .reshape(8, 48, 256)
-        )
-    s_down.first()
-    rs1.second(0)
-    rs1.second(1)
     exchanged("gg")
     exchanged("up")
     for xt in range(4):
@@ -1032,35 +1146,61 @@
         return carry
 
     lax.fori_loop(0, 4, gate_up_grad, 0)
+    s_gu.first()
+    rs1.third()
+    rs1.second()
+    pl.run_scoped(down_product, pltpu.VMEM((WIDE, D), BF))
     load("nh", normed_h, n2, 4)
     load("nh_sib", norm_sib_h, n2_sib, 5)
     load("att_sib", att_sib_h, att_sib, 6)
-    s_gu.first()
-    s_down.second(0)
-    s_down.second(1)
-    rs1.third()
+    loads["cot"]().wait()
+    exchanged("hidden")
+    down_grad(0)
     scaled, inverse = norm(hidden_in[...])
     grad = rs1.fourth()
     value = cot[own_rows(at), :].astype(F32) + norm_back(grad, scaled, inverse, par[2:3, :])
-    grad_in[...] = value
     rows[0] = value.astype(BF)
     gb[own_rows(at), :] = value.astype(BF)
     g_branch.start(rows.at[0])
+    grad_in[...] = value
     sums[...] = jnp.zeros_like(sums)
     sums[2:3, :] = jnp.sum(grad * scaled, axis=0, keepdims=True)
     sums[3:4, :] = jnp.sum(grad, axis=0, keepdims=True)
+    s_gu.second(0)
+    s_gu.second(1)
+    down_grad(1)
+    down_grad(2)
+    down_grad(3)
+    s_down.first()
     g_branch.forward_ring()
-    s_gu.second(0)
     g_branch.spread_pair()
-    s_gu.second(1)
-    s_down.third()
-    g_branch.forward_pair()
-    send_rows(2)
+    g_branch.spread_far()
+    s_gu.third()
     g_branch.finish()
     to_sibling("gb", gb, gb_sib, 13)
-
     settle(inbox("gg"), sib_sems, exchange["gg"][1], at.sibling()).wait_send()
     gp = gg
+
+    def qkv_grad(xt, carry):
+        qkv_a[xt // 2, xt % 2] = (
+            outer_sum(n2[:, columns(core, xt)], gp[...], n2_sib[xt], gp_sib[...])
+            .astype(BF)
+            .reshape(8, 32, WIDE)
+        )
+        return carry
+
+    def out_grad():
+        exchanged("gb")
+        loads["att_sib"]().wait()
+        mine = att[:, pl.ds(pl.multiple_of(core * 128, 128), 128)]
+        for a in range(2):
+            cols = pl.ds(a * 1024, 1024)
+            out_a[a, 0] = (
+                outer_sum(mine, gb[:, cols], att_sib[...], gb_sib[:, cols])
+                .astype(BF)
+                .reshape(8, 16, 1024)
+            )
+        s_out.first()
 
     def attention(tables, pieces, qkv_s):
         load("tab", tab_h, tables, 10)
@@ -1069,19 +1209,17 @@
         grad_att[...] = lax.dot_general(
             gb[...], out_s[...].reshape(256, D), ROWS_BY_COLS, preferred_element_type=F32
         ).astype(BF)
-        rs2.first()
+        rs2.zero()
+        rs2.sides()
+        s_down.second(0)
+        s_down.second(1)
         loads["tab"]().wait()
 
-        def after_two():
-            total = rs2.fourth() + hidden_in[...]
-            rows[1] = total.astype(BF)
-            gather_columns(at, rows.at[1], act_out, (act_sems[0].at[pl.ds(9, 7)], act_sems[1].at[pl.ds(9, 7)]), local.at[16])
-
         between = [
-            lambda: (rs2.second(0), rs2.second(1), s_gu.third()),
-            lambda: (rs2.third(), begin(2)),
-            lambda: (send_rows(0), g_down.forward_ring(), g_down.spread_pair()),
-            lambda: (after_two(), begin(0)),
+            lambda: (send_rows(0),),
+            lambda: (out_grad(), rs2.first(), rs2.third()),
+            lambda: (begin(0),),
+            lambda: (s_down.third(),),
         ]
         bias_sums = attend_back(
             qkv, grad_att, tables, seg_col, seg_row, maxima, totals, gp, pieces, between
@@ -1098,9 +1236,15 @@
             ).astype(BF)
 
         product(far)
-        rs3.first()
+        rs3.zero()
         product(right)
         product(left)
+        rs3.sides()
+        exchanged("gp")
+        loads["nh"]().wait()
+        loads["nh_sib"]().wait()
+        lax.fori_loop(0, 4, qkv_grad, 0)
+        s_qkv.first()
         product(x)
         sums[4:7, 0:256] = jnp.concatenate([bias_sums[:, j * 256 : (j + 1) * 256] for j in range(3)])
 
@@ -1110,41 +1254,22 @@
         pltpu.VMEM((HEADS, 3, TOK, HD), F32),
         pltpu.VMEM((4, 16, 32, WIDE), BF),
     )
-    exchanged("gb")
-    loads["att_sib"]().wait()
-    mine = att[:, pl.ds(pl.multiple_of(core * 128, 128), 128)]
-    for a in range(2):
-        cols = pl.ds(a * 1024, 1024)
-        out_a[a, 0] = (
-            outer_sum(mine, gb[:, cols], att_sib[...], gb_sib[:, cols])
-            .astype(BF)
-            .reshape(8, 16, 1024)
-        )
-    rs3.second(0)
-    rs3.second(1)
-    s_out.first()
-    exchanged("gp")
-    loads["nh"]().wait()
-    loads["nh_sib"]().wait()
-
-    def qkv_grad(xt, carry):
-        qkv_a[xt // 2, xt % 2] = (
-            outer_sum(n2[:, columns(core, xt)], gp[...], n2_sib[xt], gp_sib[...]).astype(BF).reshape(8, 32, WIDE)
-        )
-        return carry
-
-    lax.fori_loop(0, 4, qkv_grad, 0)
-    s_qkv.first()
+    rs3.first()
+    g_gu.forward_ring()
+    g_gu.spread_pair()
     rs3.third()
-    g_down.forward_pair()
-    g_gu.forward_ring()
     s_out.second(0)
     s_out.second(1)
+    rs3.second()
+    rs2.second()
+    s_qkv.second(0)
+    s_qkv.second(1)
+    send_rows(2)
     scaled, inverse = norm(x_own[...].astype(F32))
     grad = rs3.fourth()
     value = grad_in[...] + norm_back(grad, scaled, inverse, par[0:1, :])
     rows[2] = value.astype(BF)
-    gather_columns(at, rows.at[2], input_out, (act_sems[0].at[pl.ds(16, 7)], act_sems[1].at[pl.ds(16, 7)]), local.at[17])
+    start_columns(at, rows.at[2], input_out, act_sems, 16, local.at[17])
     sums[0:1, :] = jnp.sum(grad * scaled, axis=0, keepdims=True)
     sums[1:2, :] = jnp.sum(grad, axis=0, keepdims=True)
     own_columns = pl.ds(pl.multiple_of(at.g * 256, 256), 256)
@@ -1160,13 +1285,13 @@
                 at.group(g),
             )
         )
-    s_qkv.second(0)
-    s_qkv.second(1)
-    g_gu.spread_pair()
+    s_qkv.third()
     s_out.third()
-    s_qkv.third()
-    send_rows(3)
-    send_rows(1)
+    begin(2)
+    g_gu.forward_pair()
+    total = rs2.fourth() + hidden_in[...]
+    rows[1] = total.astype(BF)
+    start_columns(at, rows.at[1], act_out, act_sems, 9, local.at[16])
     total = sums[0:4, own_columns]
     for j in range(7):
         ln_copies[j].wait_recv()
@@ -1177,17 +1302,20 @@
         push(small_t.at[at.dp], small_t.at[at.dp], small_sems, j, device)
         for j, device in enumerate(others)
     ]
+    send_rows(1)
+    send_rows(3)
+    g_down.forward_ring()
+    begin(1)
     begin(3)
-    begin(1)
-    g_down.finish()
-    g_gu.forward_pair()
+    g_gu.finish()
+    g_down.spread_far()
+    g_qkv.forward_ring()
+    g_qkv.spread_pair()
     g_out.forward_ring()
     g_out.spread_pair()
-    g_qkv.forward_ring()
-    g_qkv.spread_pair()
-    g_gu.finish()
+    g_qkv.forward_pair()
     g_out.forward_pair()
-    g_qkv.forward_pair()
+    g_down.finish()
     for copy in small_copies:
         copy.wait_recv()
     result = small_t[0]
@@ -1214,20 +1342,20 @@
     g_branch.drain()
     rs2.drain()
     rs3.drain()
-    for j in (9, 16):
-        settle_all(at, rows.at[1, :, pl.ds(0, 256)], (act_sems[0].at[pl.ds(j, 7)], act_sems[1].at[pl.ds(j, 7)]))
+    finish_columns(at, rows.at[1], act_out, act_sems, 9, local.at[16])
+    finish_columns(at, rows.at[2], input_out, act_sems, 16, local.at[17])
 
 
 def back(
     n2, gu_s, down_s, out_s, qkv_s, cot, normed, tables, norm_sib, cot_sib, att_sib,
-    hidden_in, par, att, qkv, seg_col, seg_row, maxima, totals, x_own,
+    hidden_in, par, att, qkv, seg_col, seg_row, maxima, totals, x_own, grad_hidden,
 ):
     shape = jax.ShapeDtypeStruct
     vmem = pltpu.VMEM
     wide = vmem((TOK, D), BF)
     inner = vmem((TOK, WIDE), BF)
     quarters = vmem((4, TOK, 256), BF)
-    box = scatter_scratch()[1:5]
+    box = scatter_scratch()[1:7]
     return pl.pallas_call(
         back_kernel,
         out_shape=(
@@ -1239,10 +1367,10 @@
             shape((4, 16, 16, 512), BF),
             shape((8, 256), F32),
         ),
-        in_specs=[IN_ANY] * 11 + [IN_VMEM] * 9,
+        in_specs=[IN_ANY] * 11 + [IN_VMEM] * 10,
         out_specs=(IN_ANY,) * 6 + (IN_VMEM,),
         scratch_shapes=[
-            wide, quarters, wide, vmem((2, TOK, 256), BF), wide, wide, vmem((TOK, 128), BF),
+            wide, quarters, wide, vmem((2, TOK, 512), BF), wide, wide, vmem((TOK, 128), BF),
             inner, vmem((TOK, 384), BF), inner, inner, inner, inner, inner,
             vmem((TOK, 256), BF), vmem((OWN, D), F32),
             vmem((16, 16, D), BF), vmem((3, OWN, D), BF), vmem((8, D), F32),
@@ -1268,33 +1396,48 @@
         name="back",
     )(
         n2, gu_s, down_s, out_s, qkv_s, cot, normed, tables, norm_sib, cot_sib, att_sib,
-        hidden_in, par, att, qkv, seg_col, seg_row, maxima, totals, x_own,
+        hidden_in, par, att, qkv, seg_col, seg_row, maxima, totals, x_own, grad_hidden,
     )
+
+
+def widen_gate_up_kernel(low, out):
+    for j in range(2):
+        shares = [low[x, j] for x in range(4)]
+        out[:, j, 0:768] = shares[0].astype(F32)
+        out[:, j, 768:1536] = shares[1].astype(F32)
+        out[:, j, 1536:2176] = shares[2][:, 128:].astype(F32)
+        out[:, j, 2176:2816] = shares[3][:, 128:].astype(F32)
+
+
+def widen_gate_up(low):
+    return pl.pallas_call(
+        widen_gate_up_kernel,
+        out_shape=jax.ShapeDtypeStruct((512, 2, 2816), F32),
+        grid=(8,),
+        in_specs=[pl.BlockSpec((4, 2, 64, WIDE), lambda i: (0, 0, i, 0))],
+        out_specs=pl.BlockSpec((64, 2, 2816), lambda i: (i, 0, 0)),
+        compiler_params=pltpu.CompilerParams(vmem_limit_bytes=VMEM_LIMIT),
+        name="widen_gate_up",
+    )(low)
 
 
 def on_device(
     block_in, segments, ln1_gain, ln1_bias, qkv_weight, qkv_bias, out_weight,
     ln2_gain, ln2_bias, gate_up_weight, down_weight, cotangent,
 ):
-    zero = jnp.zeros((256,), F32)
-    par = jnp.stack([ln1_gain, ln1_bias, ln2_gain, ln2_bias, zero, zero, zero, zero])
-    gate_up = jnp.transpose(gate_up_weight, (1, 0, 2))
-    seg_col = segments[:, None]
-    seg_row = segments[None, :]
     (
         cot_full, par, normed, qkv, attended, maxima, totals, tables, x_own,
+        seg_col, seg_row, grad_hidden,
         hidden_in, normed_two, qkv_s, out_s, gu_s, down_s, norm_sib, cot_sib, att_sib,
     ) = front(
-        block_in, cotangent, par, qkv_bias[None, :], seg_col, seg_row,
-        qkv_weight, out_weight, gate_up, down_weight,
+        block_in, cotangent, ln1_gain, ln1_bias, ln2_gain, ln2_bias, qkv_bias, segments,
+        qkv_weight, out_weight, gate_up_weight, down_weight,
     )
     activations, input_grad, gu_f, qkv_f, down_f, out_f, small = back(
         normed_two, gu_s.reshape(2, D, WIDE), down_s.reshape(WIDE, D), out_s, qkv_s, cot_full,
-        normed, tables, norm_sib, cot_sib, att_sib, hidden_in, par, attended, qkv, seg_col, seg_row, maxima, totals, x_own,
+        normed, tables, norm_sib, cot_sib, att_sib, hidden_in, par, attended, qkv, seg_col, seg_row, maxima, totals, x_own, grad_hidden,
     )
-    gu_f = gu_f.reshape(4, 2, 512, WIDE)
-    gu_f = jnp.concatenate([gu_f[0], gu_f[1], gu_f[2, :, :, 128:], gu_f[3, :, :, 128:]], axis=2)
-    gu_grad = jnp.transpose(gu_f, (1, 0, 2)).astype(F32)
+    gu_grad = widen_gate_up(gu_f.reshape(4, 2, 512, WIDE))
     down_f = down_f.reshape(4, WIDE, 512)
     down_grad = jnp.concatenate(
         [down_f[0], down_f[1], down_f[2, 128:], down_f[3, 128:]], axis=0

time: 347 us -> 283 us (0.82)
  Pallas kernels: 301 us -> 263 us
  local copies, waits for them, and re-layouts: 24.3 us -> 7.8 us
  other arithmetic: 17.6 us -> 8.39 us
    pallas_call x1, Pallas kernels: 186 us -> 152 us  [back(): pl.pallas_call(back_kernel, out_shape=(shape((TOK, 256), BF), shape((TOK,...]
    pallas_call x1, Pallas kernels: 115 us -> 101 us  [front(): pl.pallas_call(front_kernel, out_shape=(shape((TOK, D), BF), shape((8, D)...]
    pallas_call x0 -> x1, Pallas kernels: none -> 9.77 us  [widen_gate_up(): pl.pallas_call(widen_gate_up_kernel, out_shape=jax.ShapeDtypeStruct((512,...]
    convert_element_type x1 -> x0, other arithmetic: 9.52 us -> none  [on_device(): gu_grad = jnp.transpose(gu_f, (1, 0, 2)).astype(F32)]
    squeeze x3 -> x0, local copies, waits for them, and re-layouts: 5.94 us -> none  [the longest x1 2.7 us: on_device(): gu_f[3, :, :, 128:]]
    unnamed x13 -> x10, local copies, waits for them, and re-layouts: 7.85 us -> 2.14 us
where the time goes in v4:
time: 283 us; the launch traced here: 280 us
  Pallas kernels  263 us (93%)
  other arithmetic  8.39 us (3%)
  local copies, waits for them, and re-layouts  7.8 us (3%)
    pallas_call x1, Pallas kernels, back(): pl.pallas_call(back_kernel, out_shape=(shape((TOK, 256), BF), shape((TOK,...  152 us
    pallas_call x1, Pallas kernels, front(): pl.pallas_call(front_kernel, out_shape=(shape((TOK, D), BF), shape((8, D)...  101 us
    pallas_call x1, Pallas kernels, widen_gate_up(): pl.pallas_call(widen_gate_up_kernel, out_shape=jax.ShapeDtypeStruct((512,...  9.77 us

profile of v4, /device:TPU:1, one launch (start us, length us, event | category | flops | bytes accessed | tf_op | source)
XLA Modules:
  0.0 280.0 jit_solution(14569460872654555998)
XLA Ops:
  0.6 100.6 %front.1 = (bf16[512,2048]{1,0:T(8,128)(2,1)}, f32[8,2048]{1,0:T(8,128)}, bf16[512,2048]{1,0:T(8,128)(2,1)}, bf16[512,768]{1,0:T(8,128)(2,1)}, bf16[512,256]{1,0...) custom-call(bf16[512,256]{1,0:T(8,128)(2,1)} %x_in.1, ...), custom_call_target="tpu_custom_call" | custom-call | tf_op jit(solution)/shard_map/front/pallas_call | solution.py:686
  101.3 152.4 %back.1 = (bf16[512,256]{1,0:T(8,128)(2,1)}, bf16[512,256]{1,0:T(8,128)(2,1)}, bf16[4,2,16,32,768]{4,3,2,1,0:T(8,128)(2,1)}, bf16[16,32,3072]{2,1,0:T(8,128)(2,1...) custom-call(bf16[512,2048]{1,0:T(8,128)(2,1)} %get-tuple-element.39.n2_h, ...), custom_call_target="tpu_custom_call" | custom-call | tf_op jit(solution)/shard_map/back/pallas_call | solution.py:1359
  253.7 0.0 copy-start.1
  253.7 0.8 slice.31
  254.5 1.4 fusion.1
  255.9 0.6 reshape.49
  256.5 1.4 slice_bitcast_fusion.1
  257.9 1.5 fusion
  259.4 0.0 copy-done.1
  259.4 1.7 bitcast_convert_fusion.1
  261.1 0.0 copy-start
  261.1 3.0 %maximum_convert_fusion = f32[2816,512]{1,0:T(8,128)} fusion(bf16[640,512]{1,0:T(8,128)(2,1)S(1)} %get-tuple-element.70, bf16[640,512]{1,0:T(8,128)(2,1)S(1)} %get-tuple-element.69, bf16[768,512]{1,0:T(8,128)(2,1)S(1)} %bitcast.24, bf16[768,512]{1,0:T(8,128)(2,1)S(1)} %bitcast.23), kind=kLoop, calls=%fused_computation.1 | loop fusion | flops 11534336 | bytes 8650752 | tf_op jit(solution)/shard_map/convert_element_type | solution.py:1444
  264.1 0.7 copy-done
  264.8 3.7 %bitcast_convert_fusion = f32[512,3072]{1,0:T(8,128)} fusion(bf16[16,32,3072]{2,1,0:T(8,128)(2,1)S(1)} %copy-done), kind=kLoop, calls=%fused_computation | loop fusion | flops 1572864 | bytes 9437184 | tf_op jit(solution)/shard_map/convert_element_type | solution.py:1450
  268.5 0.0 copy-start.3
  268.5 0.0 copy-start.2
  268.5 9.8 %widen_gate_up.1 = f32[512,2,2816]{2,1,0:T(2,128)} custom-call(bf16[4,2,512,768]{3,2,1,0:T(8,128)(2,1)} %bitcast.20), custom_call_target="tpu_custom_call" | custom-call | tf_op jit(solution)/shard_map/widen_gate_up/pallas_call | solution.py:1413
  278.3 0.0 copy-done.3
  278.3 0.7 copy.25
  279.0 0.0 copy-done.2
  279.0 0.7 copy.26
Async XLA Ops:
  253.7 5.7 %copy-start.1 = (bf16[4,16,16,512]{3,2,1,0:T(8,128)(2,1)S(1)}, bf16[4,16,16,512]{3,2,1,0:T(8,128)(2,1)}, u32[]{:S(2)}) copy-start(bf16[4,16,16,512]{3,2,1,0:T(8,128)(2,1)} %get-tuple-element.64) | copy-start | bytes 3145732
  261.1 3.7 %copy-start = (bf16[16,32,3072]{2,1,0:T(8,128)(2,1)S(1)}, bf16[16,32,3072]{2,1,0:T(8,128)(2,1)}, u32[]{:S(2)}) copy-start(bf16[16,32,3072]{2,1,0:T(8,128)(2,1)} %get-tuple-element.63) | copy-start | bytes 9437188
  268.5 9.8 %copy-start.3 = (bf16[512,256]{1,0:T(8,128)(2,1)S(1)}, bf16[512,256]{1,0:T(8,128)(2,1)}, u32[]{:S(2)}) copy-start(bf16[512,256]{1,0:T(8,128)(2,1)} %get-tuple-element.86) | copy-start | bytes 786436
  268.5 10.5 %copy-start.2 = (bf16[512,256]{1,0:T(8,128)(2,1)S(1)}, bf16[512,256]{1,0:T(8,128)(2,1)}, u32[]{:S(2)}) copy-start(bf16[512,256]{1,0:T(8,128)(2,1)} %get-tuple-element.87) | copy-start | bytes 786436

commit v5 on v4

--- a/solution.py
+++ b/solution.py
@@ -136,11 +136,18 @@
         settle(ref, self.sems, self.base + index, self.device(self.pos, self.pair)).wait_recv()
 
     def start(self, own=None):
+        self.start_ring(own)
+        self.start_pair(own)
+
+    def start_ring(self, own=None):
         ref = self.whole(self.pos, self.pair)
         self.push(1, ref, self.device(self.right, self.pair), own)
         self.push(2, ref, self.device(self.left, self.pair), own)
+        self.on_piece(self.pos, self.pair, 0)
+
+    def start_pair(self, own=None):
+        ref = self.whole(self.pos, self.pair)
         self.push(0, ref, self.device(self.pos, 1 - self.pair), own)
-        self.on_piece(self.pos, self.pair, 0)
 
     def forward(self, first, pair, slot):
         self.arrived(first, self.whole(self.left, pair))
@@ -608,7 +615,7 @@
         lambda: (w_out.forward_pair(), gcot.forward_ring(), gcot.spread_pair()),
         lambda: (begin(3),),
         lambda: (w_out.finish(),),
-        lambda: (gcot.spread_far(),),
+        lambda: None,
     ]
     attend(proj, tables, seg_col, seg_row, qkv_out, att_out, max_out, sum_out, between)
     from_sibling(1)
@@ -634,14 +641,10 @@
     rs.first()
     w_down.spread_pair()
     rs.third()
+    gcot.spread_far()
     rs.second()
     w_gu.forward_ring()
     w_gu.spread_pair()
-    gcot.finish()
-    put(cot, cot_out, 14)
-    sib_copies.append(push(cot, cot_sib, sib, 4, at.sibling()))
-    cols = pl.ds(pl.multiple_of((1 - core) * 128, 128), 128)
-    sib_copies.append(push(att_out.at[:, cols], att_sib, sib, 5, at.sibling()))
     hidden_in = rs.fourth() + x_v[own_rows(at), :].astype(F32)
     hidden_out[...] = hidden_in
     scaled, _ = norm(hidden_in)
@@ -649,6 +652,11 @@
     normed2[own_rows(at), :] = rows[...]
     gn = row_gather(at, normed2, act, 18)
     gn.start(rows)
+    gcot.finish()
+    put(cot, cot_out, 14)
+    sib_copies.append(push(cot, cot_sib, sib, 4, at.sibling()))
+    cols = pl.ds(pl.multiple_of((1 - core) * 128, 128), 128)
+    sib_copies.append(push(att_out.at[:, cols], att_sib, sib, 5, at.sibling()))
     w_down.forward_pair()
     gn.forward_ring()
     gn.spread_pair()
@@ -1008,7 +1016,7 @@
     ]
     s_gu, s_qkv, s_down, s_out = scatters
     gathers = [
-        (RingGather if k == 2 else Gather)(
+        Gather(
             at.y, at.zl, lambda y, zl: ((y * 2 + zl) * 2 + core, x, at.zh), whole(k), half(k),
             dpg_sems, k * 9, share(k),
         )
@@ -1022,11 +1030,14 @@
             push(pack_for(k, xt), landing(k, x, cq), row_sems, k * 3 + j - 1, at.row(xt))
         pltpu.make_async_copy(pack_for(k, x), landing(k, x, cq), local.at[12 + k]).start()
 
-    def begin(k):
+    def begin(k, pair=True):
         pltpu.make_async_copy(pack_for(k, x), landing(k, x, cq), local.at[12 + k]).wait()
         for j in range(3):
             settle(pack_for(k, x), row_sems, k * 3 + j, at.row(x)).wait_recv()
-        gathers[k].start()
+        if pair:
+            gathers[k].start()
+        else:
+            gathers[k].start_ring()
 
     rs1, rs2, rs3 = [
         RowScatter(at, p, *boxes[j], rs_sems, j * 9) for j, p in enumerate((part, part2, part))
@@ -1052,6 +1063,14 @@
         if a < 2:
             load_cot_sib(a + 2)
 
+    def gate_up_grad(xt, carry):
+        own, sib = n2[:, columns(core, xt)], n2_sib[xt]
+        gu_a[0, xt] = outer_sum(own, gg[...], sib, gg_sib[...]).astype(BF).reshape(8, 32, WIDE)
+        gu_a[1, xt] = (
+            outer_sum(own, grad_up[...], sib, gate_up_sib[...]).astype(BF).reshape(8, 32, WIDE)
+        )
+        return carry
+
     def feed_forward(gu_s, gate_v, up_v):
         load("gate", gu_h.at[0], gu_s.at[0], 7)
         load("up", gu_h.at[1], gu_s.at[1], 8)
@@ -1105,6 +1124,12 @@
 
         product(far)
         rs1.zero()
+        exchanged("gg")
+        exchanged("up")
+        for xt in range(4):
+            exchanged(("n2", xt))
+        lax.fori_loop(0, 4, gate_up_grad, 0)
+        s_gu.first()
         product(right)
         product(left)
         rs1.sides()
@@ -1132,30 +1157,20 @@
         pltpu.VMEM((TOK, 256), F32),
         pltpu.VMEM((TOK, 256), F32),
     )
-    exchanged("gg")
-    exchanged("up")
-    for xt in range(4):
-        exchanged(("n2", xt))
-
-    def gate_up_grad(xt, carry):
-        own, sib = n2[:, columns(core, xt)], n2_sib[xt]
-        gu_a[0, xt] = outer_sum(own, gg[...], sib, gg_sib[...]).astype(BF).reshape(8, 32, WIDE)
-        gu_a[1, xt] = (
-            outer_sum(own, grad_up[...], sib, gate_up_sib[...]).astype(BF).reshape(8, 32, WIDE)
-        )
-        return carry
-
-    lax.fori_loop(0, 4, gate_up_grad, 0)
-    s_gu.first()
+    s_gu.second(0)
+    s_gu.second(1)
     rs1.third()
     rs1.second()
-    pl.run_scoped(down_product, pltpu.VMEM((WIDE, D), BF))
     load("nh", normed_h, n2, 4)
     load("nh_sib", norm_sib_h, n2_sib, 5)
     load("att_sib", att_sib_h, att_sib, 6)
     loads["cot"]().wait()
     exchanged("hidden")
     down_grad(0)
+    down_grad(1)
+    down_grad(2)
+    down_grad(3)
+    s_down.first()
     scaled, inverse = norm(hidden_in[...])
     grad = rs1.fourth()
     value = cot[own_rows(at), :].astype(F32) + norm_back(grad, scaled, inverse, par[2:3, :])
@@ -1166,16 +1181,14 @@
     sums[...] = jnp.zeros_like(sums)
     sums[2:3, :] = jnp.sum(grad * scaled, axis=0, keepdims=True)
     sums[3:4, :] = jnp.sum(grad, axis=0, keepdims=True)
-    s_gu.second(0)
-    s_gu.second(1)
-    down_grad(1)
-    down_grad(2)
-    down_grad(3)
-    s_down.first()
+    s_gu.third()
+    pl.run_scoped(down_product, pltpu.VMEM((WIDE, D), BF))
     g_branch.forward_ring()
     g_branch.spread_pair()
+    s_down.second(0)
+    s_down.second(1)
     g_branch.spread_far()
-    s_gu.third()
+    send_rows(0)
     g_branch.finish()
     to_sibling("gb", gb, gb_sib, 13)
     settle(inbox("gg"), sib_sems, exchange["gg"][1], at.sibling()).wait_send()
@@ -1211,15 +1224,13 @@
         ).astype(BF)
         rs2.zero()
         rs2.sides()
-        s_down.second(0)
-        s_down.second(1)
         loads["tab"]().wait()
 
         between = [
-            lambda: (send_rows(0),),
-            lambda: (out_grad(), rs2.first(), rs2.third()),
             lambda: (begin(0),),
-            lambda: (s_down.third(),),
+            lambda: (out_grad(),),
+            lambda: (rs2.first(), s_down.third()),
+            lambda: (g_gu.forward_ring(),),
         ]
         bias_sums = attend_back(
             qkv, grad_att, tables, seg_col, seg_row, maxima, totals, gp, pieces, between
@@ -1240,12 +1251,15 @@
         product(right)
         product(left)
         rs3.sides()
+        s_out.second(0)
+        s_out.second(1)
         exchanged("gp")
         loads["nh"]().wait()
         loads["nh_sib"]().wait()
         lax.fori_loop(0, 4, qkv_grad, 0)
         s_qkv.first()
         product(x)
+        g_gu.spread_pair()
         sums[4:7, 0:256] = jnp.concatenate([bias_sums[:, j * 256 : (j + 1) * 256] for j in range(3)])
 
     pl.run_scoped(
@@ -1255,16 +1269,13 @@
         pltpu.VMEM((4, 16, 32, WIDE), BF),
     )
     rs3.first()
-    g_gu.forward_ring()
-    g_gu.spread_pair()
     rs3.third()
-    s_out.second(0)
-    s_out.second(1)
-    rs3.second()
-    rs2.second()
     s_qkv.second(0)
     s_qkv.second(1)
+    rs3.second()
     send_rows(2)
+    rs2.third()
+    rs2.second()
     scaled, inverse = norm(x_own[...].astype(F32))
     grad = rs3.fourth()
     value = grad_in[...] + norm_back(grad, scaled, inverse, par[0:1, :])
@@ -1285,13 +1296,10 @@
                 at.group(g),
             )
         )
+    begin(2)
     s_qkv.third()
     s_out.third()
-    begin(2)
     g_gu.forward_pair()
-    total = rs2.fourth() + hidden_in[...]
-    rows[1] = total.astype(BF)
-    start_columns(at, rows.at[1], act_out, act_sems, 9, local.at[16])
     total = sums[0:4, own_columns]
     for j in range(7):
         ln_copies[j].wait_recv()
@@ -1305,14 +1313,18 @@
     send_rows(1)
     send_rows(3)
     g_down.forward_ring()
+    g_down.spread_pair()
     begin(1)
     begin(3)
-    g_gu.finish()
-    g_down.spread_far()
+    total = rs2.fourth() + hidden_in[...]
+    rows[1] = total.astype(BF)
+    start_columns(at, rows.at[1], act_out, act_sems, 9, local.at[16])
     g_qkv.forward_ring()
     g_qkv.spread_pair()
     g_out.forward_ring()
     g_out.spread_pair()
+    g_gu.finish()
+    g_down.forward_pair()
     g_qkv.forward_pair()
     g_out.forward_pair()
     g_down.finish()

time: 283 us -> 279 us (0.986)
  Pallas kernels: 263 us -> 259 us
    pallas_call x1, Pallas kernels: 101 us -> 97.1 us  [front(): pl.pallas_call(front_kernel, out_shape=(shape((TOK, D), BF), shape((8, D)...]
where the time goes in v5:
time: 279 us; the launch traced here: 276 us
  Pallas kernels  259 us (93%)
  other arithmetic  8.39 us (3%)
  local copies, waits for them, and re-layouts  7.8 us (3%)
    pallas_call x1, Pallas kernels, back(): pl.pallas_call(back_kernel, out_shape=(shape((TOK, 256), BF), shape((TOK,...  152 us
    pallas_call x1, Pallas kernels, front(): pl.pallas_call(front_kernel, out_shape=(shape((TOK, D), BF), shape((8, D)...  97.1 us
    pallas_call x1, Pallas kernels, widen_gate_up(): pl.pallas_call(widen_gate_up_kernel, out_shape=jax.ShapeDtypeStruct((512,...  9.77 us

profile of v5, /device:TPU:1, one launch (start us, length us, event | category | flops | bytes accessed | tf_op | source)
XLA Modules:
  0.0 275.7 jit_solution(8147789185259786363)
XLA Ops:
  0.6 97.1 %front.1 = (bf16[512,2048]{1,0:T(8,128)(2,1)}, f32[8,2048]{1,0:T(8,128)}, bf16[512,2048]{1,0:T(8,128)(2,1)}, bf16[512,768]{1,0:T(8,128)(2,1)}, bf16[512,256]{1,0...) custom-call(bf16[512,256]{1,0:T(8,128)(2,1)} %x_in.1, ...), custom_call_target="tpu_custom_call" | custom-call | tf_op jit(solution)/shard_map/front/pallas_call | solution.py:694
  97.8 151.7 %back.1 = (bf16[512,256]{1,0:T(8,128)(2,1)}, bf16[512,256]{1,0:T(8,128)(2,1)}, bf16[4,2,16,32,768]{4,3,2,1,0:T(8,128)(2,1)}, bf16[16,32,3072]{2,1,0:T(8,128)(2,1...) custom-call(bf16[512,2048]{1,0:T(8,128)(2,1)} %get-tuple-element.39.n2_h, ...), custom_call_target="tpu_custom_call" | custom-call | tf_op jit(solution)/shard_map/back/pallas_call | solution.py:1371
  249.5 0.0 copy-start.1
  249.5 0.8 slice.31
  250.3 1.4 fusion.1
  251.7 0.6 reshape.49
  252.3 1.4 slice_bitcast_fusion.1
  253.7 1.5 fusion
  255.1 0.0 copy-done.1
  255.1 1.7 bitcast_convert_fusion.1
  256.8 0.0 copy-start
  256.8 3.0 %maximum_convert_fusion = f32[2816,512]{1,0:T(8,128)} fusion(bf16[640,512]{1,0:T(8,128)(2,1)S(1)} %get-tuple-element.70, bf16[640,512]{1,0:T(8,128)(2,1)S(1)} %get-tuple-element.69, bf16[768,512]{1,0:T(8,128)(2,1)S(1)} %bitcast.24, bf16[768,512]{1,0:T(8,128)(2,1)S(1)} %bitcast.23), kind=kLoop, calls=%fused_computation.1 | loop fusion | flops 11534336 | bytes 8650752 | tf_op jit(solution)/shard_map/convert_element_type | solution.py:1456
  259.8 0.7 copy-done
  260.6 3.7 %bitcast_convert_fusion = f32[512,3072]{1,0:T(8,128)} fusion(bf16[16,32,3072]{2,1,0:T(8,128)(2,1)S(1)} %copy-done), kind=kLoop, calls=%fused_computation | loop fusion | flops 1572864 | bytes 9437184 | tf_op jit(solution)/shard_map/convert_element_type | solution.py:1462
  264.3 0.0 copy-start.3
  264.3 0.0 copy-start.2
  264.3 9.8 %widen_gate_up.1 = f32[512,2,2816]{2,1,0:T(2,128)} custom-call(bf16[4,2,512,768]{3,2,1,0:T(8,128)(2,1)} %bitcast.20), custom_call_target="tpu_custom_call" | custom-call | tf_op jit(solution)/shard_map/widen_gate_up/pallas_call | solution.py:1425
  274.0 0.0 copy-done.3
  274.1 0.7 copy.25
  274.8 0.0 copy-done.2
  274.8 0.7 copy.26
Async XLA Ops:
  249.5 5.7 %copy-start.1 = (bf16[4,16,16,512]{3,2,1,0:T(8,128)(2,1)S(1)}, bf16[4,16,16,512]{3,2,1,0:T(8,128)(2,1)}, u32[]{:S(2)}) copy-start(bf16[4,16,16,512]{3,2,1,0:T(8,128)(2,1)} %get-tuple-element.64) | copy-start | bytes 3145732
  256.8 3.7 %copy-start = (bf16[16,32,3072]{2,1,0:T(8,128)(2,1)S(1)}, bf16[16,32,3072]{2,1,0:T(8,128)(2,1)}, u32[]{:S(2)}) copy-start(bf16[16,32,3072]{2,1,0:T(8,128)(2,1)} %get-tuple-element.63) | copy-start | bytes 9437188
  264.3 9.8 %copy-start.3 = (bf16[512,256]{1,0:T(8,128)(2,1)S(1)}, bf16[512,256]{1,0:T(8,128)(2,1)}, u32[]{:S(2)}) copy-start(bf16[512,256]{1,0:T(8,128)(2,1)} %get-tuple-element.86) | copy-start | bytes 786436
  264.3 10.5 %copy-start.2 = (bf16[512,256]{1,0:T(8,128)(2,1)S(1)}, bf16[512,256]{1,0:T(8,128)(2,1)}, u32[]{:S(2)}) copy-start(bf16[512,256]{1,0:T(8,128)(2,1)} %get-tuple-element.87) | copy-start | bytes 786436

commit v6 on v5

--- a/solution.py
+++ b/solution.py
@@ -1270,10 +1270,12 @@
     )
     rs3.first()
     rs3.third()
+    send_rows(2)
     s_qkv.second(0)
     s_qkv.second(1)
     rs3.second()
-    send_rows(2)
+    g_gu.forward_pair()
+    begin(2)
     rs2.third()
     rs2.second()
     scaled, inverse = norm(x_own[...].astype(F32))
@@ -1296,10 +1298,10 @@
                 at.group(g),
             )
         )
-    begin(2)
     s_qkv.third()
     s_out.third()
-    g_gu.forward_pair()
+    g_down.forward_ring()
+    g_down.spread_pair()
     total = sums[0:4, own_columns]
     for j in range(7):
         ln_copies[j].wait_recv()
@@ -1312,8 +1314,6 @@
     ]
     send_rows(1)
     send_rows(3)
-    g_down.forward_ring()
-    g_down.spread_pair()
     begin(1)
     begin(3)
     total = rs2.fourth() + hidden_in[...]
@@ -1425,9 +1425,9 @@
     return pl.pallas_call(
         widen_gate_up_kernel,
         out_shape=jax.ShapeDtypeStruct((512, 2, 2816), F32),
-        grid=(8,),
-        in_specs=[pl.BlockSpec((4, 2, 64, WIDE), lambda i: (0, 0, i, 0))],
-        out_specs=pl.BlockSpec((64, 2, 2816), lambda i: (i, 0, 0)),
+        grid=(4,),
+        in_specs=[pl.BlockSpec((4, 2, 128, WIDE), lambda i: (0, 0, i, 0))],
+        out_specs=pl.BlockSpec((128, 2, 2816), lambda i: (i, 0, 0)),
         compiler_params=pltpu.CompilerParams(vmem_limit_bytes=VMEM_LIMIT),
         name="widen_gate_up",
     )(low)

time: 279 us -> 279 us (level)
  no operation moved by 1% of the time
where the time goes in v6:
time: 279 us; the launch traced here: 276 us
  Pallas kernels  259 us (93%)
  other arithmetic  8.39 us (3%)
  local copies, waits for them, and re-layouts  7.8 us (3%)
    pallas_call x1, Pallas kernels, back(): pl.pallas_call(back_kernel, out_shape=(shape((TOK, 256), BF), shape((TOK,...  153 us
    pallas_call x1, Pallas kernels, front(): pl.pallas_call(front_kernel, out_shape=(shape((TOK, D), BF), shape((8, D)...  97.1 us
    pallas_call x1, Pallas kernels, widen_gate_up(): pl.pallas_call(widen_gate_up_kernel, out_shape=jax.ShapeDtypeStruct((512,...  8.56 us

profile of v6, /device:TPU:1, one launch (start us, length us, event | category | flops | bytes accessed | tf_op | source)
XLA Modules:
  0.0 275.8 jit_solution(17764243000753082466)
XLA Ops:
  0.6 97.1 %front.1 = (bf16[512,2048]{1,0:T(8,128)(2,1)}, f32[8,2048]{1,0:T(8,128)}, bf16[512,2048]{1,0:T(8,128)(2,1)}, bf16[512,768]{1,0:T(8,128)(2,1)}, bf16[512,256]{1,0...) custom-call(bf16[512,256]{1,0:T(8,128)(2,1)} %x_in.1, ...), custom_call_target="tpu_custom_call" | custom-call | tf_op jit(solution)/shard_map/front/pallas_call | solution.py:694
  97.8 153.0 %back.1 = (bf16[512,256]{1,0:T(8,128)(2,1)}, bf16[512,256]{1,0:T(8,128)(2,1)}, bf16[4,2,16,32,768]{4,3,2,1,0:T(8,128)(2,1)}, bf16[16,32,3072]{2,1,0:T(8,128)(2,1...) custom-call(bf16[512,2048]{1,0:T(8,128)(2,1)} %get-tuple-element.39.n2_h, ...), custom_call_target="tpu_custom_call" | custom-call | tf_op jit(solution)/shard_map/back/pallas_call | solution.py:1371
  250.7 0.0 copy-start.1
  250.8 0.8 slice.31
  251.5 1.4 fusion.1
  253.0 0.6 reshape.49
  253.6 1.4 slice_bitcast_fusion.1
  254.9 1.5 fusion
  256.4 0.0 copy-done.1
  256.4 1.7 bitcast_convert_fusion.1
  258.1 0.0 copy-start
  258.1 3.0 %maximum_convert_fusion = f32[2816,512]{1,0:T(8,128)} fusion(bf16[640,512]{1,0:T(8,128)(2,1)S(1)} %get-tuple-element.70, bf16[640,512]{1,0:T(8,128)(2,1)S(1)} %get-tuple-element.69, bf16[768,512]{1,0:T(8,128)(2,1)S(1)} %bitcast.24, bf16[768,512]{1,0:T(8,128)(2,1)S(1)} %bitcast.23), kind=kLoop, calls=%fused_computation.1 | loop fusion | flops 11534336 | bytes 8650752 | tf_op jit(solution)/shard_map/convert_element_type | solution.py:1456
  261.1 0.7 copy-done
  261.8 3.7 %bitcast_convert_fusion = f32[512,3072]{1,0:T(8,128)} fusion(bf16[16,32,3072]{2,1,0:T(8,128)(2,1)S(1)} %copy-done), kind=kLoop, calls=%fused_computation | loop fusion | flops 1572864 | bytes 9437184 | tf_op jit(solution)/shard_map/convert_element_type | solution.py:1462
  265.5 0.0 copy-start.3
  265.5 0.0 copy-start.2
  265.6 8.6 %widen_gate_up.1 = f32[512,2,2816]{2,1,0:T(2,128)} custom-call(bf16[4,2,512,768]{3,2,1,0:T(8,128)(2,1)} %bitcast.20), custom_call_target="tpu_custom_call" | custom-call | tf_op jit(solution)/shard_map/widen_gate_up/pallas_call | solution.py:1425
  274.1 0.0 copy-done.3
  274.1 0.7 copy.25
  274.8 0.0 copy-done.2
  274.8 0.7 copy.26
Async XLA Ops:
  250.7 5.7 %copy-start.1 = (bf16[4,16,16,512]{3,2,1,0:T(8,128)(2,1)S(1)}, bf16[4,16,16,512]{3,2,1,0:T(8,128)(2,1)}, u32[]{:S(2)}) copy-start(bf16[4,16,16,512]{3,2,1,0:T(8,128)(2,1)} %get-tuple-element.64) | copy-start | bytes 3145732
  258.1 3.7 %copy-start = (bf16[16,32,3072]{2,1,0:T(8,128)(2,1)S(1)}, bf16[16,32,3072]{2,1,0:T(8,128)(2,1)}, u32[]{:S(2)}) copy-start(bf16[16,32,3072]{2,1,0:T(8,128)(2,1)} %get-tuple-element.63) | copy-start | bytes 9437188
  265.5 8.6 %copy-start.3 = (bf16[512,256]{1,0:T(8,128)(2,1)S(1)}, bf16[512,256]{1,0:T(8,128)(2,1)}, u32[]{:S(2)}) copy-start(bf16[512,256]{1,0:T(8,128)(2,1)} %get-tuple-element.86) | copy-start | bytes 786436
  265.5 9.3 %copy-start.2 = (bf16[512,256]{1,0:T(8,128)(2,1)S(1)}, bf16[512,256]{1,0:T(8,128)(2,1)}, u32[]{:S(2)}) copy-start(bf16[512,256]{1,0:T(8,128)(2,1)} %get-tuple-element.87) | copy-start | bytes 786436
